TPU v7x, 32 devices: a whole 2x2x4 slice. The times are simulated.
32 devices in a mesh: groups: 2 (over y), expert: 16 (over z, x, core).
Axes of the slice: x: 2, y: 2, z: 4, core: 2. Of those that a mesh axis runs over, the one named last changes fastest.
Arguments:
- tokens: bfloat16 [4096, 3584], P(('groups', 'expert')), parts along dimension 0, may hold values from -6 to 6
- grad_out: bfloat16 [4096, 3584], P(('groups', 'expert')), parts along dimension 0, may hold values from -6 to 6
- route_weight: bfloat16 [4096, 1], P(('groups', 'expert')), parts along dimension 0, may hold values from 0.099609375 to 1
- expert_ids: int32 [4096, 1], P(('groups', 'expert')), parts along dimension 0, may hold values from 0 to 1; in each aligned block of 128 rows (0 to 127, 128 to 255, ...) at most 80 rows name the same one
- w_gate: bfloat16 [16, 3584, 128], P('expert'), may hold values from -0.09375 to 0.09375
- w_up: bfloat16 [16, 3584, 128], P('expert'), may hold values from -0.09375 to 0.09375
- w_down: bfloat16 [16, 128, 3584], P('expert'), may hold values from -0.1875 to 0.1875
Outputs:
- grad_tokens: bfloat16 [4096, 3584], P(('groups', 'expert')), parts along dimension 0
- grad_combine: float32 [4096, 1], P(('groups', 'expert')), parts along dimension 0
- grad_gate: bfloat16 [32, 3584, 128], P(('groups', 'expert')), parts along dimension 0
- grad_up: bfloat16 [32, 3584, 128], P(('groups', 'expert')), parts along dimension 0
- grad_down: bfloat16 [32, 128, 3584], P(('groups', 'expert')), parts along dimension 0
There are 2 independent parts, one for each index of `groups`. A program takes and returns all parts, laid end to end along the dimension named above; an argument that names none is the same for every part. Nothing has to cross between parts.
Inputs may be any that keep to these rules, and one draw needn't show every extreme that they name: `expert_ids`: each row names 1 different experts; within the 128 rows of one device no expert is named more than 80 times, a bound that some block reaches.
All inputs are finite; a program needn't handle non-finite values.
Results may differ from a plain program's by a relative error of at most 0.008.
Values may be sent and summed in bfloat16 or wider, within the bound.
No kernel may reach another device: no remote copies, remote signals or barrier semaphores. Data moves between devices by JAX's collectives and lax.ppermute only.
A program may use at most 192 MiB of HBM per device.

v0:
```python
import jax
import jax.numpy as jnp
from jax import lax
from jax.sharding import PartitionSpec as P

SPLIT = 8


def slot_positions(block_ids, experts):
    flat_ids = block_ids.reshape(-1)
    onehot = (flat_ids[:, None] == jnp.arange(experts, dtype=jnp.int32)[None, :]).astype(jnp.int32)
    before = jnp.cumsum(onehot, axis=0) - onehot
    return (flat_ids, jnp.sum(before * onehot, axis=1))


def expert_pass(rows_x, rows_dy, rows_weight, gate_mat, up_mat, down_mat):
    gate_pre = jnp.dot(rows_x, gate_mat, preferred_element_type=jnp.float32)
    up_pre = jnp.dot(rows_x, up_mat, preferred_element_type=jnp.float32)
    sigma = jax.nn.sigmoid(gate_pre)
    act_silu = gate_pre * sigma
    hidden = act_silu * up_pre
    grad_hidden = lax.dot_general(
        rows_dy, down_mat, (((1,), (1,)), ((), ())), preferred_element_type=jnp.float32
    )
    prob_part = jnp.sum(hidden * grad_hidden, axis=1).astype(jnp.bfloat16)
    row_scale = rows_weight.astype(jnp.float32)[:, None]
    grad_act = row_scale * grad_hidden
    grad_gpre = (grad_act * up_pre * sigma * (1.0 + gate_pre * (1.0 - sigma))).astype(jnp.bfloat16)
    grad_upre = (grad_act * act_silu).astype(jnp.bfloat16)
    rows_part = lax.dot_general(
        grad_gpre, gate_mat, (((1,), (1,)), ((), ())), preferred_element_type=jnp.float32
    )
    rows_part = rows_part + lax.dot_general(
        grad_upre, up_mat, (((1,), (1,)), ((), ())), preferred_element_type=jnp.float32
    )
    rows_part = rows_part.astype(jnp.bfloat16)
    hidden_bf = hidden.astype(jnp.bfloat16)
    scaled_dy = (row_scale * rows_dy.astype(jnp.float32)).astype(jnp.bfloat16)
    grad_gate = lax.dot_general(
        rows_x, grad_gpre, (((0,), (0,)), ((), ())), preferred_element_type=jnp.float32
    )
    grad_up = lax.dot_general(
        rows_x, grad_upre, (((0,), (0,)), ((), ())), preferred_element_type=jnp.float32
    )
    grad_down = lax.dot_general(
        hidden_bf, scaled_dy, (((0,), (0,)), ((), ())), preferred_element_type=jnp.float32
    )
    return (rows_part, prob_part, grad_gate, grad_up, grad_down)


def replicate_slots(source, token_index, filled, experts, capacity):
    features = source.shape[1]
    slots = jnp.where(filled[:, None], source[token_index], jnp.zeros((), source.dtype))
    spread = jnp.broadcast_to(
        slots.reshape(experts, 1, capacity, features), (experts, SPLIT, capacity, features)
    )
    return spread.reshape(experts * SPLIT, capacity, features)


def on_device(tokens, grad_out, route_weight, expert_ids, w_gate, w_up, w_down):
    axis_count = lax.axis_size("expert")
    experts = axis_count // SPLIT
    tok_rows, features = tokens.shape
    top_count = expert_ids.shape[1]
    capacity = min(tok_rows, 5 * tok_rows * top_count // (4 * experts))
    pairs = tok_rows * top_count
    flat_ids, position = slot_positions(expert_ids, experts)
    slot_index = flat_ids * capacity + position
    occupant = (
        jnp.full((experts * capacity,), pairs, jnp.int32)
        .at[slot_index]
        .set(jnp.arange(pairs, dtype=jnp.int32))
    )
    filled = occupant < pairs
    safe_pair = jnp.minimum(occupant, pairs - 1)
    token_index = safe_pair // top_count
    weight_slots = jnp.where(
        filled, route_weight.reshape(-1)[safe_pair], jnp.zeros((), route_weight.dtype)
    )
    send_weight = jnp.broadcast_to(
        weight_slots.reshape(experts, 1, capacity), (experts, SPLIT, capacity)
    ).reshape(axis_count, capacity)
    rows_x = lax.all_to_all(
        replicate_slots(tokens, token_index, filled, experts, capacity),
        "expert",
        split_axis=0,
        concat_axis=0,
        tiled=True,
    )
    rows_dy, rows_weight = (
        lax.all_to_all(
            replicate_slots(grad_out, token_index, filled, experts, capacity),
            "expert",
            split_axis=0,
            concat_axis=0,
            tiled=True,
        ),
        lax.all_to_all(send_weight, "expert", split_axis=0, concat_axis=0, tiled=True),
    )
    rows_count = axis_count * capacity
    rows_part, prob_part, grad_gate, grad_up, grad_down = expert_pass(
        rows_x.reshape(rows_count, features),
        rows_dy.reshape(rows_count, features),
        rows_weight.reshape(rows_count),
        w_gate[0],
        w_up[0],
        w_down[0],
    )
    back_rows, back_prob = (
        lax.all_to_all(
            rows_part.reshape(axis_count, capacity, features),
            "expert",
            split_axis=0,
            concat_axis=0,
            tiled=True,
        ),
        lax.all_to_all(
            prob_part.reshape(axis_count, capacity),
            "expert",
            split_axis=0,
            concat_axis=0,
            tiled=True,
        ),
    )
    slot_rows = jnp.sum(
        back_rows.astype(jnp.float32).reshape(experts, SPLIT, capacity, features), axis=1
    ).reshape(experts * capacity, features)
    slot_prob = jnp.sum(
        back_prob.astype(jnp.float32).reshape(experts, SPLIT, capacity), axis=1
    ).reshape(-1)
    grad_tokens = jnp.sum(
        slot_rows[slot_index].reshape(tok_rows, top_count, features), axis=1
    ).astype(jnp.bfloat16)
    grad_combine = slot_prob[slot_index].reshape(tok_rows, top_count)
    return (
        grad_tokens,
        grad_combine,
        grad_gate.astype(jnp.bfloat16)[None],
        grad_up.astype(jnp.bfloat16)[None],
        grad_down.astype(jnp.bfloat16)[None],
    )


def solution(mesh):
    in_specs = (
        P(("groups", "expert"), None),
        P(("groups", "expert"), None),
        P(("groups", "expert"), None),
        P(("groups", "expert"), None),
        P("expert", None, None),
        P("expert", None, None),
        P("expert", None, None),
    )
    out_specs = (
        P(("groups", "expert"), None),
        P(("groups", "expert"), None),
        P(("groups", "expert"), None, None),
        P(("groups", "expert"), None, None),
        P(("groups", "expert"), None, None),
    )
    return jax.shard_map(
        on_device, mesh=mesh, in_specs=in_specs, out_specs=out_specs, check_vma=False
    )
```

profile of v0, /device:TPU:11, one launch (start us, length us, event | category | flops | bytes accessed | tf_op | source)
XLA Modules:
  0.0 685.2 jit_solution(15857316466931066578)
XLA Ops:
  0.6 0.0 copy-start
  0.6 0.0 copy-start.2
  0.7 0.9 fusion.19
  1.5 0.2 reduce_window_sum.11
  1.7 0.8 select_reduce_fusion
  2.5 0.7 fusion.20
  3.2 1.0 scatter_custom_fusion
  4.2 1.9 gather_fusion
  6.1 0.1 broadcast_in_dim.62
  6.2 0.6 copy.13
  6.8 6.6 all-to-all-start
  13.4 0.1 broadcast_in_dim.64
  13.5 4.7 gather_fusion.2
  18.2 0.0 copy-done.2
  18.2 2.3 gather_fusion.1
  20.5 1.8 broadcast_select_fusion.1
  22.4 0.0 all-to-all-done
  22.4 0.9 broadcast_in_dim.68
  23.2 204.9 %all_to_all.30 = bf16[16,80,3584]{2,1,0:T(8,128)(2,1)} all-to-all(bf16[16,80,3584]{2,1,0:T(8,128)(2,1)S(1)} %bitcast.64), channel_id=1, replica_groups=mesh['groups'=2,'expert'=16] {'expert'}, dimensions={0} | all-to-all | bytes 18350080 | tf_op jit(solution)/shard_map/all_to_all | solution.py:83
  228.2 4.4 broadcast_in_dim.67
  232.6 5.8 all-to-all-start.1
  238.3 0.0 copy-start.3
  238.4 0.1 reshape.119
  238.4 0.0 copy-done
  238.4 6.8 fusion.9
  245.2 0.0 copy-done.3
  245.2 6.7 fusion.12
  252.0 185.6 %all-to-all-done.1 = bf16[16,80,3584]{2,1,0:T(8,128)(2,1)} async-done(((bf16[16,80,3584]{2,1,0:T(8,128)(2,1)}), bf16[16,80,3584]{2,1,0:T(8,128)(2,1)}, u32[]{:S(2)}, u32[]{:S(2)}) %all-to-all-start.1) | async-done | bytes 9175072 | tf_op jit(solution)/shard_map/all_to_all | solution.py:91
  437.5 7.7 %multiply_reduce_fusion = (bf16[1280]{0:T(1024)(128)(2,1)S(1)}, bf16[1280,128]{0,1:T(8,128)(2,1)}, bf16[1280,128]{0,1:T(8,128)(2,1)S(1)}) fusion(f32[1280,128]{0,1:T(8,128)S(1)} %fusion.12, f32[1280,128]{0,1:T(8,128)S(1)} %fusion.9, f32[1280]{0:T(1024)S(1)} %reshape.119, bf16[1280,3584]{1,0:T(8,128)(2,1)} %bitcast.7, bf16[1,128,3584]{2,1,0:T(8,128)(2,1)} %param.13), kind=kOutput, calls=%fused_computation.29 | convolution fusion | flops 1177189120 | bytes 12066304 | tf_op jit(solution)/shard_map/dot_general | solution.py:22
  445.2 0.7 convert_element_type.88
  445.9 4.9 all-to-all-start.4
  450.8 9.8 %fusion.7 = f32[1280,3584]{1,0:T(8,128)} fusion(bf16[1280,128]{0,1:T(8,128)(2,1)} %get-tuple-element.8, bf16[1,3584,128]{2,1,0:T(8,128)(2,1)S(1)} %copy-done), kind=kOutput, calls=%fused_computation.20 | convolution fusion | flops 1174405120 | bytes 19595264 | tf_op jit(solution)/shard_map/dot_general | solution.py:30
  460.7 12.3 %fusion = bf16[1280,3584]{1,0:T(8,128)(2,1)} fusion(f32[1280,3584]{1,0:T(8,128)} %fusion.7, bf16[1280,128]{0,1:T(8,128)(2,1)S(1)} %get-tuple-element.9, bf16[1,3584,128]{2,1,0:T(8,128)(2,1)S(1)} %copy-done.3), kind=kOutput, calls=%fused_computation.9 | convolution fusion | flops 1183580160 | bytes 28770304 | tf_op jit(solution)/shard_map/dot_general | solution.py:33
  472.9 0.0 all-to-all-done.4
  472.9 0.0 copy-start.4
  472.9 6.1 all-to-all-start.3
  479.1 0.0 copy-done.4
  479.1 7.1 %fusion.5 = bf16[1,3584,128]{2,1,0:T(8,128)(2,1)} fusion(bf16[1280,3584]{1,0:T(8,128)(2,1)} %bitcast.59, bf16[1280,128]{0,1:T(8,128)(2,1)S(1)} %copy-done.4), kind=kOutput, calls=%fused_computation.16 | convolution fusion | flops 1174863872 | bytes 10420224 | tf_op jit(solution)/shard_map/dot_general | solution.py:39
  486.2 7.1 %fusion.6 = bf16[1,3584,128]{2,1,0:T(8,128)(2,1)} fusion(bf16[1280,3584]{1,0:T(8,128)(2,1)} %bitcast.60, bf16[1280,128]{0,1:T(8,128)(2,1)S(1)} %get-tuple-element.9), kind=kOutput, calls=%fused_computation.17 | convolution fusion | flops 1174863872 | bytes 10420224 | tf_op jit(solution)/shard_map/dot_general | solution.py:42
  493.4 6.6 fusion.4
  500.0 0.1 reshape.117
  500.1 0.0 copy-start.1
  500.1 1.8 gather_fusion.4
  501.8 176.5 %all-to-all-done.3 = bf16[16,80,3584]{2,1,0:T(8,128)(2,1)} async-done(((bf16[16,80,3584]{2,1,0:T(8,128)(2,1)}), bf16[16,80,3584]{2,1,0:T(8,128)(2,1)}, u32[]{:S(2)}, u32[]{:S(2)}) %all-to-all-start.3) | async-done | bytes 9175072 | tf_op jit(solution)/shard_map/all_to_all | solution.py:110
  678.3 4.8 convert_reduce_fusion
  683.1 2.0 gather_fusion.3
  685.2 0.0 copy-done.1
  (9 shorter events, 0.1 us)
Async XLA Ops:
  0.6 237.8 %copy-start = (bf16[1,3584,128]{2,1,0:T(8,128)(2,1)S(1)}, bf16[1,3584,128]{2,1,0:T(8,128)(2,1)}, u32[]{:S(2)}) copy-start(bf16[1,3584,128]{2,1,0:T(8,128)(2,1)} %param.11) | copy-start | bytes 2752516
  0.6 17.6 %copy-start.2 = (bf16[128,3584]{1,0:T(8,128)(2,1)S(1)}, bf16[128,3584]{1,0:T(8,128)(2,1)}, u32[]{:S(2)}) copy-start(bf16[128,3584]{1,0:T(8,128)(2,1)} %param.8) | copy-start | bytes 2752516
  6.8 15.5 %all-to-all-start = ((bf16[16,1,80]{2,1,0:T(2,128)(2,1)}), bf16[16,1,80]{2,1,0:T(2,128)(2,1)S(1)}, u32[]{:S(2)}, u32[]{:S(2)}) async-start(bf16[16,1,80]{2,1,0:T(2,128)(2,1)} %copy.13), calls=%async_computation | async-start | bytes 16384 | tf_op jit(solution)/shard_map/all_to_all | solution.py:98
  232.6 205.0 %all-to-all-start.1 = ((bf16[16,80,3584]{2,1,0:T(8,128)(2,1)}), bf16[16,80,3584]{2,1,0:T(8,128)(2,1)}, u32[]{:S(2)}, u32[]{:S(2)}) async-start(bf16[16,80,3584]{2,1,0:T(8,128)(2,1)} %bitcast.63), calls=%async_computation.1 | async-start | bytes 18350080 | tf_op jit(solution)/shard_map/all_to_all | solution.py:91
  238.3 6.9 %copy-start.3 = (bf16[1,3584,128]{2,1,0:T(8,128)(2,1)S(1)}, bf16[1,3584,128]{2,1,0:T(8,128)(2,1)}, u32[]{:S(2)}) copy-start(bf16[1,3584,128]{2,1,0:T(8,128)(2,1)} %param.12) | copy-start | bytes 2752516
  445.9 27.0 %all-to-all-start.4 = ((bf16[16,1,80]{2,1,0:T(2,128)(2,1)}), bf16[16,1,80]{2,1,0:T(2,128)(2,1)S(1)}, u32[]{:S(2)}, u32[]{:S(2)}) async-start(bf16[16,1,80]{2,1,0:T(2,128)(2,1)} %convert_element_type.88), calls=%async_computation.4 | async-start | bytes 16384 | tf_op jit(solution)/shard_map/all_to_all | solution.py:117
  472.9 6.2 copy-start.4
  472.9 205.4 %all-to-all-start.3 = ((bf16[16,80,3584]{2,1,0:T(8,128)(2,1)}), bf16[16,80,3584]{2,1,0:T(8,128)(2,1)}, u32[]{:S(2)}, u32[]{:S(2)}) async-start(bf16[16,80,3584]{2,1,0:T(8,128)(2,1)} %bitcast.62), calls=%async_computation.3 | async-start | bytes 18350080 | tf_op jit(solution)/shard_map/all_to_all | solution.py:110
  500.1 185.1 %copy-start.1 = (bf16[1,3584,128]{2,1,0:T(8,128)(2,1)S(1)}, bf16[1,3584,128]{2,1,0:T(8,128)(2,1)}, u32[]{:S(2)}) copy-start(bf16[1,3584,128]{2,1,0:T(8,128)(2,1)} %param.11) | copy-start | bytes 2752516
where the time goes:
time: 686 us; the launch traced here: 685 us
  waiting for transfers between devices  362 us (53%)
  blocking collectives  205 us (30%)
  matrix products  64.1 us (9%)
  starting transfers between devices  23.4 us (3%)
  local copies, waits for them, and re-layouts  20.7 us (3%)
  other arithmetic  9.26 us (1%)
    all_to_all x1, blocking collectives, on_device(): lax.all_to_all(replicate_slots(tokens, token_index, filled, experts, capa...  205 us
    all_to_all x1, waiting for transfers between devices, on_device(): lax.all_to_all(replicate_slots(grad_out, token_index, filled, experts, ca...  186 us
    all_to_all x1, waiting for transfers between devices, on_device(): lax.all_to_all(rows_part.reshape(axis_count, capacity, features), 'expert...  176 us
  transfers between devices with their start and end apart: 4, of which 2 were waited for; matrix products, arithmetic and copies ran while one was open for 10% of the time, Pallas kernels for 0%

commit v1 on v0

v1 whole, which is shorter than its diff:
```python
import jax
import jax.numpy as jnp
from jax import lax
from jax.sharding import PartitionSpec as P

SPLIT = 8
CORE = 1
WEIGHT_BIT = 2
ROW_BIT = 4

F32 = jnp.float32
BF16 = jnp.bfloat16


def dot(a, b, ca, cb):
    return lax.dot_general(a, b, (((ca,), (cb,)), ((), ())), preferred_element_type=F32)


def flip(x, mask):
    n = lax.axis_size("expert")
    return lax.ppermute(x, "expert", [(i, i ^ mask) for i in range(n)])


def add(a, b):
    return (a.astype(F32) + b.astype(F32)).astype(BF16)


def share_rows(a):
    pair = jnp.concatenate([a, flip(a, ROW_BIT)], axis=0)
    return jnp.concatenate([pair, flip(pair, CORE)], axis=0)


def sum_rows(p):
    half = p.shape[0] // 2
    p = add(p[:half], flip(p[half:], CORE))
    half = half // 2
    return add(p[:half], flip(p[half:], ROW_BIT))


def on_device(tokens, grad_out, route_weight, expert_ids, w_gate, w_up, w_down):
    axis_count = lax.axis_size("expert")
    experts = axis_count // SPLIT
    tok_rows, features = tokens.shape
    capacity = min(tok_rows, 5 * tok_rows // (4 * experts))
    hid = w_gate.shape[2]
    mine = lax.axis_index("expert") // SPLIT

    relative = expert_ids[:, 0] ^ mine
    onehot = (relative[:, None] == jnp.arange(experts, dtype=jnp.int32)[None, :]).astype(BF16)
    earlier = (jnp.arange(tok_rows)[:, None] > jnp.arange(tok_rows)[None, :]).astype(BF16)
    before = dot(earlier, onehot, 1, 0)
    position = jnp.sum(before * onehot.astype(F32), axis=1).astype(jnp.int32)
    slot = relative * capacity + position
    select = (jnp.arange(experts * capacity, dtype=jnp.int32)[:, None] == slot[None, :]).astype(BF16)

    weight = route_weight.astype(F32)
    scaled = (weight * grad_out.astype(F32)).astype(BF16)
    slots_x = dot(select, tokens, 1, 0).astype(BF16)
    slots_u = dot(select, scaled, 1, 0).astype(BF16)

    def dispatch(slots):
        parts = [
            flip(slots[k * capacity : (k + 1) * capacity], SPLIT * k) for k in range(1, experts)
        ]
        return parts[0] if experts == 2 else jnp.concatenate(parts, axis=0)

    far_x = dispatch(slots_x)
    far_u = dispatch(slots_u)
    near_x = share_rows(slots_x[:capacity])
    near_u = share_rows(slots_u[:capacity])
    far_x = share_rows(far_x)
    far_u = share_rows(far_u)

    gate = w_gate[0]
    up = w_up[0]
    down = w_down[0]
    gate = jnp.concatenate([gate, flip(gate, WEIGHT_BIT)], axis=1)
    up = jnp.concatenate([up, flip(up, WEIGHT_BIT)], axis=1)
    down = jnp.concatenate([down, flip(down, WEIGHT_BIT)], axis=0)

    def hidden_pass(x, u):
        gate_pre = dot(x, gate, 1, 0)
        up_pre = dot(x, up, 1, 0)
        grad_act = dot(u, down, 1, 1)
        sigma = jax.nn.sigmoid(gate_pre)
        act_silu = gate_pre * sigma
        hidden = act_silu * up_pre
        prob = jnp.sum(hidden * grad_act, axis=1, keepdims=True).astype(BF16)
        grad_gpre = (grad_act * up_pre * sigma * (1.0 + gate_pre * (1.0 - sigma))).astype(BF16)
        grad_upre = (grad_act * act_silu).astype(BF16)
        return hidden.astype(BF16), grad_gpre, grad_upre, prob

    def rows_pass(grad_gpre, grad_upre, prob):
        rows = (dot(grad_gpre, gate, 1, 1) + dot(grad_upre, up, 1, 1)).astype(BF16)
        return jnp.concatenate([rows, jnp.broadcast_to(prob, (rows.shape[0], 128))], axis=1)

    near = hidden_pass(near_x, near_u)
    far = hidden_pass(far_x, far_u)
    far_rows = sum_rows(rows_pass(*far[1:]))
    near_rows = sum_rows(rows_pass(*near[1:]))
    back = [
        flip(far_rows[(k - 1) * capacity : k * capacity], SPLIT * k) for k in range(1, experts)
    ]
    slot_rows = jnp.concatenate([near_rows] + back, axis=0)

    x = jnp.concatenate([near_x, far_x], axis=0)
    u = jnp.concatenate([near_u, far_u], axis=0)
    hidden, grad_gpre, grad_upre = (
        jnp.concatenate([a, b], axis=0) for a, b in zip(near[:3], far[:3])
    )

    def weight_grad(a, b, swap):
        if swap:
            far_part = dot(b[:, hid:], a, 0, 0).astype(BF16)
            near_part = dot(b[:, :hid], a, 0, 0)
        else:
            far_part = dot(a, b[:, hid:], 0, 0).astype(BF16)
            near_part = dot(a, b[:, :hid], 0, 0)
        return (near_part + flip(far_part, WEIGHT_BIT).astype(F32)).astype(BF16)[None]

    grad_down = weight_grad(u, hidden, True)
    grad_gate = weight_grad(x, grad_gpre, False)
    grad_up = weight_grad(x, grad_upre, False)

    out = dot(select, slot_rows, 0, 0)
    grad_tokens = out[:, :features].astype(BF16)
    grad_combine = out[:, features : features + 1] / weight
    return (grad_tokens, grad_combine, grad_gate, grad_up, grad_down)


def solution(mesh):
    rows = P(("groups", "expert"), None)
    blocks = P(("groups", "expert"), None, None)
    weights = P("expert", None, None)
    return jax.shard_map(
        on_device,
        mesh=mesh,
        in_specs=(rows, rows, rows, rows, weights, weights, weights),
        out_specs=(rows, rows, blocks, blocks, blocks),
        check_vma=False,
    )
```

time: 686 us -> 216 us (0.31)
  the two profiles are of different devices: /device:TPU:11 before, /device:TPU:0 now
where the time goes in v1:
time: 216 us; the launch traced here: 215 us
  waiting for transfers between devices  155 us (72%)
  starting transfers between devices  27.9 us (13%)
  matrix products  23.8 us (11%)
  local copies, waits for them, and re-layouts  4.42 us (2%)
  other arithmetic  2.85 us (1%)
    ppermute x21, waiting for transfers between devices, flip(): return lax.ppermute(x, 'expert', [(i, i ^ mask) for i in range(n)])  155 us
    ppermute x21, starting transfers between devices, flip(): return lax.ppermute(x, 'expert', [(i, i ^ mask) for i in range(n)])  27.9 us
    dot_general x20, matrix products, dot(): lax.dot_general(a, b, (((ca,), (cb,)), ((), ())), preferred_element_type=...  23.8 us
  transfers between devices with their start and end apart: 21, of which 10 were waited for; matrix products, arithmetic and copies ran while one was open for 13% of the time, Pallas kernels for 0%

profile of v1, /device:TPU:0, one launch (start us, length us, event | category | flops | bytes accessed | tf_op | source)
XLA Modules:
  0.0 215.4 jit_solution(7996612426378928961)
XLA Ops:
  0.6 3.0 %collective-permute-start.5 = (bf16[3584,128]{1,0:T(8,128)(2,1)}, bf16[3584,128]{1,0:T(8,128)(2,1)S(1)}, u32[]{:S(2)}, u32[]{:S(2)}) collective-permute-start(bf16[3584,128]{1,0:T(8,128)(2,1)} %bitcast.31), channel_id=1, source_target_pairs={{0,2},{1,3},{2,0},{3,1},{4,6},{5,7},{6,4},{7,5},{8,10},{9,11},{10,... | collective-permute-start | bytes 2752520 | tf_op jit(solution)/shard_map/ppermute | solution.py:21
  3.7 0.1 collective-permute-start.2
  3.7 0.7 xor_bitcast_fusion
  4.4 0.1 fusion.26
  4.5 0.7 bitcast_add_fusion
  5.2 0.5 copy-done.7
  5.7 0.4 convolution_convert_fusion
  6.2 1.0 constant_dynamic-update-slice_fusion.8
  7.2 3.0 %collective-permute-start.12 = (bf16[80,3584]{1,0:T(8,128)(2,1)S(1)}, bf16[80,3584]{1,0:T(8,128)(2,1)S(1)}, u32[]{:S(2)}, u32[]{:S(2)}) collective-permute-start(bf16[80,3584]{1,0:T(8,128)(2,1)S(1)} %get-tuple-element.21), channel_id=1, source_target_pairs={{0,8},{1,9},{2,10},{3,11},{4,12},{5,13},{6,14},{7,15},{8,0},{9,1},... | collective-permute-start | bytes 1720328 | tf_op jit(solution)/shard_map/ppermute | solution.py:21
  10.2 1.6 collective-permute-start.3
  11.8 0.1 copy.14
  11.9 0.1 convert_reduce_fusion
  12.1 1.9 convolution_convert_fusion.1
  13.9 0.1 constant_dynamic-update-slice_fusion.14
  14.1 0.4 collective-permute-start.9
  14.5 21.5 %collective-permute-done.3 = bf16[80,3584]{1,0:T(8,128)(2,1)S(1)} collective-permute-done((bf16[80,3584]{1,0:T(8,128)(2,1)S(1)}, bf16[80,3584]{1,0:T(8,128)(2,1)S(1)}, u32[]{:S(2)}, u32[]{:S(2)}) %collective-permute-start.3) | collective-permute-done | bytes 573472 | tf_op jit(solution)/shard_map/ppermute | solution.py:21
  36.0 2.5 %collective-permute-start = (bf16[80,3584]{1,0:T(8,128)(2,1)S(1)}, bf16[80,3584]{1,0:T(8,128)(2,1)S(1)}, u32[]{:S(2)}, u32[]{:S(2)}) collective-permute-start(bf16[80,3584]{1,0:T(8,128)(2,1)S(1)} %get-tuple-element.17), channel_id=1, source_target_pairs={{0,4},{1,5},{2,6},{3,7},{4,0},{5,1},{6,2},{7,3},{8,12},{9,13},{10,... | collective-permute-start | bytes 1720328 | tf_op jit(solution)/shard_map/ppermute | solution.py:21
  38.6 8.3 %collective-permute-done.12 = bf16[80,3584]{1,0:T(8,128)(2,1)S(1)} collective-permute-done((bf16[80,3584]{1,0:T(8,128)(2,1)S(1)}, bf16[80,3584]{1,0:T(8,128)(2,1)S(1)}, u32[]{:S(2)}, u32[]{:S(2)}) %collective-permute-start.12) | collective-permute-done | bytes 573472 | tf_op jit(solution)/shard_map/ppermute | solution.py:21
  46.9 12.8 %collective-permute-done.9 = bf16[80,3584]{1,0:T(8,128)(2,1)S(1)} collective-permute-done((bf16[80,3584]{1,0:T(8,128)(2,1)S(1)}, bf16[80,3584]{1,0:T(8,128)(2,1)S(1)}, u32[]{:S(2)}, u32[]{:S(2)}) %collective-permute-start.9) | collective-permute-done | bytes 573472 | tf_op jit(solution)/shard_map/ppermute | solution.py:21
  59.7 0.6 collective-permute-start.13
  60.3 0.1 collective-permute-done
  60.4 1.3 collective-permute-start.10
  61.9 13.7 %collective-permute-done.13 = bf16[80,3584]{1,0:T(8,128)(2,1)S(1)} collective-permute-done((bf16[80,3584]{1,0:T(8,128)(2,1)S(1)}, bf16[80,3584]{1,0:T(8,128)(2,1)S(1)}, u32[]{:S(2)}, u32[]{:S(2)}) %collective-permute-start.13) | collective-permute-done | bytes 573472 | tf_op jit(solution)/shard_map/ppermute | solution.py:21
  75.7 10.1 %collective-permute-done.10 = bf16[80,3584]{1,0:T(8,128)(2,1)S(1)} collective-permute-done((bf16[80,3584]{1,0:T(8,128)(2,1)S(1)}, bf16[80,3584]{1,0:T(8,128)(2,1)S(1)}, u32[]{:S(2)}, u32[]{:S(2)}) %collective-permute-start.10) | collective-permute-done | bytes 573472 | tf_op jit(solution)/shard_map/ppermute | solution.py:21
  85.7 1.5 collective-permute-start.6
  87.4 0.5 collective-permute-start.11
  87.9 0.8 fusion.28
  88.7 2.0 fusion.8
  90.7 15.7 %collective-permute-done.6 = bf16[3584,128]{1,0:T(8,128)(2,1)S(1)} collective-permute-done((bf16[3584,128]{1,0:T(8,128)(2,1)S(1)}, bf16[3584,128]{1,0:T(8,128)(2,1)S(1)}, u32[]{:S(2)}, u32[]{:S(2)}) %collective-permute-start.6) | collective-permute-done | bytes 917536 | tf_op jit(solution)/shard_map/ppermute | solution.py:21
  106.4 1.0 multiply_convert_fusion.5
  107.4 0.8 fusion.60
  108.2 0.8 fusion
  109.0 0.1 broadcast_in_dim.10
  109.1 0.1 pad_maximum_fusion.5
  109.7 0.2 constant_dynamic-update-slice_fusion.3
  109.9 0.8 fusion.57
  110.7 0.8 fusion.59
  111.4 2.1 multiply_convert_fusion.3
  113.5 1.4 convolution_convert_fusion.4
  115.0 1.4 convolution_convert_fusion.3
  116.4 1.6 collective-permute-start.19
  117.9 0.5 collective-permute-start.18
  118.5 1.1 convolution_convert_fusion.2
  119.6 1.6 collective-permute-start.20
  121.2 0.8 fusion.58
  122.0 0.8 fusion.1
  122.8 0.1 broadcast_in_dim.11
  122.9 0.1 pad_maximum_fusion.4
  123.1 0.3 add_convert_fusion.1
  123.5 2.6 %collective-permute-start.8 = (bf16[80,3712]{1,0:T(8,128)(2,1)S(1)}, bf16[80,3712]{1,0:T(8,128)(2,1)S(1)}, u32[]{:S(2)}, u32[]{:S(2)}) collective-permute-start(bf16[80,3712]{1,0:T(8,128)(2,1)S(1)} %slice.86), channel_id=1, source_target_pairs={{0,4},{1,5},{2,6},{3,7},{4,0},{5,1},{6,2},{7,3},{8,12},{9,13},{10,... | collective-permute-start | bytes 1781768 | tf_op jit(solution)/shard_map/ppermute | solution.py:21
  126.0 13.6 %collective-permute-done.19 = bf16[3584,128]{1,0:T(8,128)(2,1)S(1)} collective-permute-done((bf16[3584,128]{1,0:T(8,128)(2,1)S(1)}, bf16[3584,128]{1,0:T(8,128)(2,1)S(1)}, u32[]{:S(2)}, u32[]{:S(2)}) %collective-permute-start.19) | collective-permute-done | bytes 917536 | tf_op jit(solution)/shard_map/ppermute | solution.py:21
  139.6 2.3 %fusion.6 = bf16[1,3584,128]{2,1,0:T(8,128)(2,1)} fusion(bf16[640,3584]{1,0:T(8,128)(2,1)S(1)} %get-tuple-element.18, bf16[3584,128]{1,0:T(8,128)(2,1)S(1)} %collective-permute-done.19, bf16[320,256]{1,0:T(8,128)(2,1)S(1)} %get-tuple-element.28, bf16[320,256]{1,0:T(8,128)(2,1)S(1)} %get-tuple-element.30), kind=kOutput, calls=%fused_computation.16 | convolution fusion | flops 588906496 | bytes 6750208 | tf_op jit(solution)/shard_map/dot_general | solution.py:16
  141.9 0.3 add_convert_fusion
  142.2 2.6 %collective-permute-start.16 = (bf16[80,3712]{1,0:T(8,128)(2,1)S(1)}, bf16[80,3712]{1,0:T(8,128)(2,1)S(1)}, u32[]{:S(2)}, u32[]{:S(2)}) collective-permute-start(bf16[80,3712]{1,0:T(8,128)(2,1)S(1)} %slice.92), channel_id=1, source_target_pairs={{0,4},{1,5},{2,6},{3,7},{4,0},{5,1},{6,2},{7,3},{8,12},{9,13},{10,... | collective-permute-start | bytes 1781768 | tf_op jit(solution)/shard_map/ppermute | solution.py:21
  144.8 33.7 %collective-permute-done.20 = bf16[128,3584]{1,0:T(8,128)(2,1)S(1)} collective-permute-done((bf16[128,3584]{1,0:T(8,128)(2,1)S(1)}, bf16[128,3584]{1,0:T(8,128)(2,1)S(1)}, u32[]{:S(2)}, u32[]{:S(2)}) %collective-permute-start.20) | collective-permute-done | bytes 917536 | tf_op jit(solution)/shard_map/ppermute | solution.py:21
  178.5 1.8 fusion.5
  180.4 2.3 %fusion.7 = bf16[1,3584,128]{2,1,0:T(8,128)(2,1)} fusion(bf16[640,3584]{1,0:T(8,128)(2,1)S(1)} %get-tuple-element.18, bf16[3584,128]{1,0:T(8,128)(2,1)S(1)} %collective-permute-done.18, bf16[320,256]{1,0:T(8,128)(2,1)S(1)} %get-tuple-element.23, bf16[320,256]{1,0:T(8,128)(2,1)S(1)} %get-tuple-element.25), kind=kOutput, calls=%fused_computation.17 | convolution fusion | flops 588906496 | bytes 6750208 | tf_op jit(solution)/shard_map/dot_general | solution.py:16
  182.7 0.2 add_convert_fusion.2
  182.9 4.4 %collective-permute-start.17 = (bf16[80,3712]{1,0:T(8,128)(2,1)S(1)}, bf16[80,3712]{1,0:T(8,128)(2,1)S(1)}, u32[]{:S(2)}, u32[]{:S(2)}) collective-permute-start(bf16[80,3712]{1,0:T(8,128)(2,1)S(1)} %add_convert_fusion.2), channel_id=1, source_target_pairs={{0,8},{1,9},{2,10},{3,11},{4,12},{5,13},{6,14},{7,15},{8,0},{9,1},... | collective-permute-start | bytes 1781768 | tf_op jit(solution)/shard_map/ppermute | solution.py:21
  187.3 0.2 add_convert_fusion.3
  187.4 25.9 %collective-permute-done.17 = bf16[80,3712]{1,0:T(8,128)(2,1)S(1)} collective-permute-done((bf16[80,3712]{1,0:T(8,128)(2,1)S(1)}, bf16[80,3712]{1,0:T(8,128)(2,1)S(1)}, u32[]{:S(2)}, u32[]{:S(2)}) %collective-permute-start.17) | collective-permute-done | bytes 593952 | tf_op jit(solution)/shard_map/ppermute | solution.py:21
  213.3 0.5 fusion.22
  213.8 1.0 slice.147
  214.8 0.6 copy.15
  (55 shorter events, 1.3 us)
Async XLA Ops:
  0.6 5.1 %copy-start = (bf16[128,3584]{1,0:T(8,128)(2,1)S(1)}, bf16[128,3584]{1,0:T(8,128)(2,1)}, u32[]{:S(2)}) copy-start(bf16[128,3584]{1,0:T(8,128)(2,1)} %param.7) | copy-start | bytes 2752516
  0.6 86.7 %collective-permute-start.5 = (bf16[3584,128]{1,0:T(8,128)(2,1)}, bf16[3584,128]{1,0:T(8,128)(2,1)S(1)}, u32[]{:S(2)}, u32[]{:S(2)}) collective-permute-start(bf16[3584,128]{1,0:T(8,128)(2,1)} %bitcast.31), channel_id=1, source_target_pairs={{0,2},{1,3},{2,0},{3,1},{4,6},{5,7},{6,4},{7,5},{8,10},{9,11},{10,... | collective-permute-start | bytes 2752520 | tf_op jit(solution)/shard_map/ppermute | solution.py:21
  3.7 85.0 %collective-permute-start.2 = (bf16[128,3584]{1,0:T(8,128)(2,1)}, bf16[128,3584]{1,0:T(8,128)(2,1)}, u32[]{:S(2)}, u32[]{:S(2)}) collective-permute-start(bf16[128,3584]{1,0:T(8,128)(2,1)} %bitcast.36), channel_id=1, source_target_pairs={{0,2},{1,3},{2,0},{3,1},{4,6},{5,7},{6,4},{7,5},{8,10},{9,11},{10,... | collective-permute-start | bytes 2752520 | tf_op jit(solution)/shard_map/ppermute | solution.py:21
  5.2 0.5 copy-start.7
  6.2 5.6 %copy-start.10 = (bf16[128,1]{0,1:T(2,128)(2,1)S(1)}, bf16[128,1]{0,1:T(2,128)(2,1)}, u32[]{:S(2)}) copy-start(bf16[128,1]{0,1:T(2,128)(2,1)} %param.9) | copy-start | bytes 772
  6.2 5.9 %copy-start.8 = (s32[128]{0:T(128)S(1)}, s32[128]{0:T(128)}, u32[]{:S(2)}) copy-start(s32[128]{0:T(128)} %copy-done.7) | copy-start | bytes 1540
  7.2 39.7 %collective-permute-start.12 = (bf16[80,3584]{1,0:T(8,128)(2,1)S(1)}, bf16[80,3584]{1,0:T(8,128)(2,1)S(1)}, u32[]{:S(2)}, u32[]{:S(2)}) collective-permute-start(bf16[80,3584]{1,0:T(8,128)(2,1)S(1)} %get-tuple-element.21), channel_id=1, source_target_pairs={{0,8},{1,9},{2,10},{3,11},{4,12},{5,13},{6,14},{7,15},{8,0},{9,1},... | collective-permute-start | bytes 1720328 | tf_op jit(solution)/shard_map/ppermute | solution.py:21
  10.2 25.8 %collective-permute-start.3 = (bf16[80,3584]{1,0:T(8,128)(2,1)S(1)}, bf16[80,3584]{1,0:T(8,128)(2,1)S(1)}, u32[]{:S(2)}, u32[]{:S(2)}) collective-permute-start(bf16[80,3584]{1,0:T(8,128)(2,1)S(1)} %get-tuple-element.22), channel_id=1, source_target_pairs={{0,4},{1,5},{2,6},{3,7},{4,0},{5,1},{6,2},{7,3},{8,12},{9,13},{10,... | collective-permute-start | bytes 1720328 | tf_op jit(solution)/shard_map/ppermute | solution.py:21
  11.9 2.1 copy-start.5
  12.1 26.4 %copy-start.2 = (bf16[640,3584]{1,0:T(8,128)(2,1)S(1)}, bf16[640,3584]{1,0:T(8,128)(2,1)}, u32[]{:S(2)}) copy-start(bf16[640,3584]{1,0:T(8,128)(2,1)} %get-tuple-element.20) | copy-start | bytes 13762564
  14.1 45.6 %collective-permute-start.9 = (bf16[80,3584]{1,0:T(8,128)(2,1)S(1)}, bf16[80,3584]{1,0:T(8,128)(2,1)S(1)}, u32[]{:S(2)}, u32[]{:S(2)}) collective-permute-start(bf16[80,3584]{1,0:T(8,128)(2,1)S(1)} %get-tuple-element.16), channel_id=1, source_target_pairs={{0,8},{1,9},{2,10},{3,11},{4,12},{5,13},{6,14},{7,15},{8,0},{9,1},... | collective-permute-start | bytes 1720328 | tf_op jit(solution)/shard_map/ppermute | solution.py:21
  36.0 24.4 %collective-permute-start = (bf16[80,3584]{1,0:T(8,128)(2,1)S(1)}, bf16[80,3584]{1,0:T(8,128)(2,1)S(1)}, u32[]{:S(2)}, u32[]{:S(2)}) collective-permute-start(bf16[80,3584]{1,0:T(8,128)(2,1)S(1)} %get-tuple-element.17), channel_id=1, source_target_pairs={{0,4},{1,5},{2,6},{3,7},{4,0},{5,1},{6,2},{7,3},{8,12},{9,13},{10,... | collective-permute-start | bytes 1720328 | tf_op jit(solution)/shard_map/ppermute | solution.py:21
  46.9 40.6 %collective-permute-start.4 = (bf16[160,3584]{1,0:T(8,128)(2,1)S(1)}, bf16[160,3584]{1,0:T(8,128)(2,1)S(1)}, u32[]{:S(2)}, u32[]{:S(2)}) collective-permute-start(bf16[160,3584]{1,0:T(8,128)(2,1)S(1)} %pad_maximum_fusion.9), channel_id=1, source_target_pairs={{0,1},{1,0},{2,3},{3,2},{4,5},{5,4},{6,7},{7,6},{8,9},{9,8},{10,11... | collective-permute-start | bytes 3440648 | tf_op jit(solution)/shard_map/ppermute | solution.py:21
  59.7 15.9 %collective-permute-start.13 = (bf16[80,3584]{1,0:T(8,128)(2,1)S(1)}, bf16[80,3584]{1,0:T(8,128)(2,1)S(1)}, u32[]{:S(2)}, u32[]{:S(2)}) collective-permute-start(bf16[80,3584]{1,0:T(8,128)(2,1)S(1)} %collective-permute-done.12), channel_id=1, source_target_pairs={{0,4},{1,5},{2,6},{3,7},{4,0},{5,1},{6,2},{7,3},{8,12},{9,13},{10,... | collective-permute-start | bytes 1720328 | tf_op jit(solution)/shard_map/ppermute | solution.py:21
  60.4 25.3 %collective-permute-start.10 = (bf16[80,3584]{1,0:T(8,128)(2,1)S(1)}, bf16[80,3584]{1,0:T(8,128)(2,1)S(1)}, u32[]{:S(2)}, u32[]{:S(2)}) collective-permute-start(bf16[80,3584]{1,0:T(8,128)(2,1)S(1)} %collective-permute-done.9), channel_id=1, source_target_pairs={{0,4},{1,5},{2,6},{3,7},{4,0},{5,1},{6,2},{7,3},{8,12},{9,13},{10,... | collective-permute-start | bytes 1720328 | tf_op jit(solution)/shard_map/ppermute | solution.py:21
  61.8 23.9 %copy-start.3 = (bf16[1,3584,128]{2,1,0:T(8,128)(2,1)S(1)}, bf16[1,3584,128]{2,1,0:T(8,128)(2,1)}, u32[]{:S(2)}) copy-start(bf16[1,3584,128]{2,1,0:T(8,128)(2,1)} %param.11) | copy-start | bytes 2752516
  61.8 26.1 %copy-start.4 = (bf16[1,3584,128]{2,1,0:T(8,128)(2,1)S(1)}, bf16[1,3584,128]{2,1,0:T(8,128)(2,1)}, u32[]{:S(2)}) copy-start(bf16[1,3584,128]{2,1,0:T(8,128)(2,1)} %param.12) | copy-start | bytes 2752516
  75.6 13.1 %collective-permute-start.1 = (bf16[160,3584]{1,0:T(8,128)(2,1)S(1)}, bf16[160,3584]{1,0:T(8,128)(2,1)S(1)}, u32[]{:S(2)}, u32[]{:S(2)}) collective-permute-start(bf16[160,3584]{1,0:T(8,128)(2,1)S(1)} %pad_maximum_fusion.8), channel_id=1, source_target_pairs={{0,1},{1,0},{2,3},{3,2},{4,5},{5,4},{6,7},{7,6},{8,9},{9,8},{10,11... | collective-permute-start | bytes 3440648 | tf_op jit(solution)/shard_map/ppermute | solution.py:21
  85.7 20.7 %collective-permute-start.6 = (bf16[3584,128]{1,0:T(8,128)(2,1)S(1)}, bf16[3584,128]{1,0:T(8,128)(2,1)S(1)}, u32[]{:S(2)}, u32[]{:S(2)}) collective-permute-start(bf16[3584,128]{1,0:T(8,128)(2,1)S(1)} %bitcast.26), channel_id=1, source_target_pairs={{0,2},{1,3},{2,0},{3,1},{4,6},{5,7},{6,4},{7,5},{8,10},{9,11},{10,... | collective-permute-start | bytes 2752520 | tf_op jit(solution)/shard_map/ppermute | solution.py:21
  87.3 1.4 copy-start.11
  87.3 22.4 %collective-permute-start.14 = (bf16[160,3584]{1,0:T(8,128)(2,1)S(1)}, bf16[160,3584]{1,0:T(8,128)(2,1)S(1)}, u32[]{:S(2)}, u32[]{:S(2)}) collective-permute-start(bf16[160,3584]{1,0:T(8,128)(2,1)S(1)} %pad_maximum_fusion.11), channel_id=1, source_target_pairs={{0,1},{1,0},{2,3},{3,2},{4,5},{5,4},{6,7},{7,6},{8,9},{9,8},{10,11... | collective-permute-start | bytes 3440648 | tf_op jit(solution)/shard_map/ppermute | solution.py:21
  87.4 24.0 %collective-permute-start.11 = (bf16[160,3584]{1,0:T(8,128)(2,1)S(1)}, bf16[160,3584]{1,0:T(8,128)(2,1)S(1)}, u32[]{:S(2)}, u32[]{:S(2)}) collective-permute-start(bf16[160,3584]{1,0:T(8,128)(2,1)S(1)} %pad_maximum_fusion.10), channel_id=1, source_target_pairs={{0,1},{1,0},{2,3},{3,2},{4,5},{5,4},{6,7},{7,6},{8,9},{9,8},{10,11... | collective-permute-start | bytes 3440648 | tf_op jit(solution)/shard_map/ppermute | solution.py:21
  109.2 13.9 %collective-permute-start.7 = (bf16[160,3712]{1,0:T(8,128)(2,1)S(1)}, bf16[160,3712]{1,0:T(8,128)(2,1)S(1)}, u32[]{:S(2)}, u32[]{:S(2)}) collective-permute-start(bf16[160,3712]{1,0:T(8,128)(2,1)S(1)} %pad_maximum_fusion.5), channel_id=1, source_target_pairs={{0,1},{1,0},{2,3},{3,2},{4,5},{5,4},{6,7},{7,6},{8,9},{9,8},{10,11... | collective-permute-start | bytes 3563528 | tf_op jit(solution)/shard_map/ppermute | solution.py:21
  116.4 23.2 %collective-permute-start.19 = (bf16[3584,128]{1,0:T(8,128)(2,1)S(1)}, bf16[3584,128]{1,0:T(8,128)(2,1)S(1)}, u32[]{:S(2)}, u32[]{:S(2)}) collective-permute-start(bf16[3584,128]{1,0:T(8,128)(2,1)S(1)} %convolution_convert_fusion.3), channel_id=1, source_target_pairs={{0,2},{1,3},{2,0},{3,1},{4,6},{5,7},{6,4},{7,5},{8,10},{9,11},{10,... | collective-permute-start | bytes 2752520 | tf_op jit(solution)/shard_map/ppermute | solution.py:21
  117.9 62.4 %collective-permute-start.18 = (bf16[3584,128]{1,0:T(8,128)(2,1)S(1)}, bf16[3584,128]{1,0:T(8,128)(2,1)S(1)}, u32[]{:S(2)}, u32[]{:S(2)}) collective-permute-start(bf16[3584,128]{1,0:T(8,128)(2,1)S(1)} %convolution_convert_fusion.4), channel_id=1, source_target_pairs={{0,2},{1,3},{2,0},{3,1},{4,6},{5,7},{6,4},{7,5},{8,10},{9,11},{10,... | collective-permute-start | bytes 2752520 | tf_op jit(solution)/shard_map/ppermute | solution.py:21
  119.6 58.9 %collective-permute-start.20 = (bf16[128,3584]{1,0:T(8,128)(2,1)S(1)}, bf16[128,3584]{1,0:T(8,128)(2,1)S(1)}, u32[]{:S(2)}, u32[]{:S(2)}) collective-permute-start(bf16[128,3584]{1,0:T(8,128)(2,1)S(1)} %convolution_convert_fusion.2), channel_id=1, source_target_pairs={{0,2},{1,3},{2,0},{3,1},{4,6},{5,7},{6,4},{7,5},{8,10},{9,11},{10,... | collective-permute-start | bytes 2752520 | tf_op jit(solution)/shard_map/ppermute | solution.py:21
  123.0 18.9 %collective-permute-start.15 = (bf16[160,3712]{1,0:T(8,128)(2,1)S(1)}, bf16[160,3712]{1,0:T(8,128)(2,1)S(1)}, u32[]{:S(2)}, u32[]{:S(2)}) collective-permute-start(bf16[160,3712]{1,0:T(8,128)(2,1)S(1)} %pad_maximum_fusion.4), channel_id=1, source_target_pairs={{0,1},{1,0},{2,3},{3,2},{4,5},{5,4},{6,7},{7,6},{8,9},{9,8},{10,11... | collective-permute-start | bytes 3563528 | tf_op jit(solution)/shard_map/ppermute | solution.py:21
  123.5 63.8 %collective-permute-start.8 = (bf16[80,3712]{1,0:T(8,128)(2,1)S(1)}, bf16[80,3712]{1,0:T(8,128)(2,1)S(1)}, u32[]{:S(2)}, u32[]{:S(2)}) collective-permute-start(bf16[80,3712]{1,0:T(8,128)(2,1)S(1)} %slice.86), channel_id=1, source_target_pairs={{0,4},{1,5},{2,6},{3,7},{4,0},{5,1},{6,2},{7,3},{8,12},{9,13},{10,... | collective-permute-start | bytes 1781768 | tf_op jit(solution)/shard_map/ppermute | solution.py:21
  142.2 40.4 %collective-permute-start.16 = (bf16[80,3712]{1,0:T(8,128)(2,1)S(1)}, bf16[80,3712]{1,0:T(8,128)(2,1)S(1)}, u32[]{:S(2)}, u32[]{:S(2)}) collective-permute-start(bf16[80,3712]{1,0:T(8,128)(2,1)S(1)} %slice.92), channel_id=1, source_target_pairs={{0,4},{1,5},{2,6},{3,7},{4,0},{5,1},{6,2},{7,3},{8,12},{9,13},{10,... | collective-permute-start | bytes 1781768 | tf_op jit(solution)/shard_map/ppermute | solution.py:21
  182.7 30.6 %copy-start.9 = (s32[128]{0:T(128)S(1)}, s32[128]{0:T(128)}, u32[]{:S(2)}) copy-start(s32[128]{0:T(128)} %copy-done.7) | copy-start | bytes 1540
  182.8 30.9 %copy-start.6 = (bf16[128,1]{1,0:T(8,128)(2,1)S(1)}, bf16[128,1]{1,0:T(8,128)(2,1)}, u32[]{:S(2)}) copy-start(bf16[128,1]{1,0:T(8,128)(2,1)} %copy-done.5) | copy-start | bytes 772
  182.9 30.4 %collective-permute-start.17 = (bf16[80,3712]{1,0:T(8,128)(2,1)S(1)}, bf16[80,3712]{1,0:T(8,128)(2,1)S(1)}, u32[]{:S(2)}, u32[]{:S(2)}) collective-permute-start(bf16[80,3712]{1,0:T(8,128)(2,1)S(1)} %add_convert_fusion.2), channel_id=1, source_target_pairs={{0,8},{1,9},{2,10},{3,11},{4,12},{5,13},{6,14},{7,15},{8,0},{9,1},... | collective-permute-start | bytes 1781768 | tf_op jit(solution)/shard_map/ppermute | solution.py:21
  187.3 28.1 %copy-start.1 = (bf16[128,3584]{1,0:T(8,128)(2,1)S(1)}, bf16[128,3584]{1,0:T(8,128)(2,1)}, u32[]{:S(2)}) copy-start(bf16[128,3584]{1,0:T(8,128)(2,1)} %param.7) | copy-start | bytes 2752516

commit v2 on v1

--- a/solution.py
+++ b/solution.py
@@ -65,18 +65,17 @@
         return parts[0] if experts == 2 else jnp.concatenate(parts, axis=0)
 
     far_x = dispatch(slots_x)
+    near = share_rows(jnp.concatenate([slots_x[:capacity], slots_u[:capacity]], axis=1))
     far_u = dispatch(slots_u)
-    near_x = share_rows(slots_x[:capacity])
-    near_u = share_rows(slots_u[:capacity])
+    near_x, near_u = near[:, :features], near[:, features:]
     far_x = share_rows(far_x)
     far_u = share_rows(far_u)
 
-    gate = w_gate[0]
-    up = w_up[0]
-    down = w_down[0]
-    gate = jnp.concatenate([gate, flip(gate, WEIGHT_BIT)], axis=1)
-    up = jnp.concatenate([up, flip(up, WEIGHT_BIT)], axis=1)
-    down = jnp.concatenate([down, flip(down, WEIGHT_BIT)], axis=0)
+    gate, up, down = w_gate[0], w_up[0], w_down[0]
+    other = flip(jnp.concatenate([gate, up, down.reshape(features, hid)], axis=0), WEIGHT_BIT)
+    gate = jnp.concatenate([gate, other[:features]], axis=1)
+    up = jnp.concatenate([up, other[features : 2 * features]], axis=1)
+    down = jnp.concatenate([down, other[2 * features :].reshape(hid, features)], axis=0)
 
     def hidden_pass(x, u):
         gate_pre = dot(x, gate, 1, 0)
@@ -101,26 +100,24 @@
     back = [
         flip(far_rows[(k - 1) * capacity : k * capacity], SPLIT * k) for k in range(1, experts)
     ]
-    slot_rows = jnp.concatenate([near_rows] + back, axis=0)
 
     x = jnp.concatenate([near_x, far_x], axis=0)
     u = jnp.concatenate([near_u, far_u], axis=0)
     hidden, grad_gpre, grad_upre = (
         jnp.concatenate([a, b], axis=0) for a, b in zip(near[:3], far[:3])
     )
-
-    def weight_grad(a, b, swap):
-        if swap:
-            far_part = dot(b[:, hid:], a, 0, 0).astype(BF16)
-            near_part = dot(b[:, :hid], a, 0, 0)
-        else:
-            far_part = dot(a, b[:, hid:], 0, 0).astype(BF16)
-            near_part = dot(a, b[:, :hid], 0, 0)
-        return (near_part + flip(far_part, WEIGHT_BIT).astype(F32)).astype(BF16)[None]
-
-    grad_down = weight_grad(u, hidden, True)
-    grad_gate = weight_grad(x, grad_gpre, False)
-    grad_up = weight_grad(x, grad_upre, False)
+    theirs = jnp.concatenate([grad_gpre[:, hid:], grad_upre[:, hid:]], axis=1)
+    ours = jnp.concatenate([grad_gpre[:, :hid], grad_upre[:, :hid]], axis=1)
+    got_both = flip(dot(x, theirs, 0, 0).astype(BF16), WEIGHT_BIT)
+    got_down = flip(dot(hidden[:, hid:], u, 0, 0).astype(BF16), WEIGHT_BIT)
+    near_rows, back, got_both, got_down = lax.optimization_barrier(
+        (near_rows, back, got_both, got_down)
+    )
+    both = (dot(x, ours, 0, 0) + got_both.astype(F32)).astype(BF16)
+    grad_gate = both[:, :hid][None]
+    grad_up = both[:, hid:][None]
+    grad_down = (dot(hidden[:, :hid], u, 0, 0) + got_down.astype(F32)).astype(BF16)[None]
+    slot_rows = jnp.concatenate([near_rows] + back, axis=0)
 
     out = dot(select, slot_rows, 0, 0)
     grad_tokens = out[:, :features].astype(BF16)

time: 216 us -> 208 us (0.963)
  waiting for transfers between devices: 155 us -> 120 us
  other arithmetic: 2.85 us -> 24.8 us
  local copies, waits for them, and re-layouts: 4.42 us -> 17.4 us
  starting transfers between devices: 27.9 us -> 18.8 us
    ppermute x21 -> x16, waiting for transfers between devices: 155 us -> 120 us  [flip(): return lax.ppermute(x, 'expert', [(i, i ^ mask) for i in range(n)])]
    concatenate x0 -> x4, other arithmetic: none -> 16.1 us  [the longest x1 9.16 us: on_device(): jnp.concatenate([gate, up, down.reshape(features, hid)], axis=0)]
    ppermute x21 -> x16, starting transfers between devices: 27.9 us -> 18.8 us  [flip(): return lax.ppermute(x, 'expert', [(i, i ^ mask) for i in range(n)])]
    concatenate x4 -> x3, other arithmetic: 0.3 us -> 5.27 us  [share_rows(): pair = jnp.concatenate([a, flip(a, ROW_BIT)], axis=0)]
    slice x0 -> x4, local copies, waits for them, and re-layouts: none -> 3.51 us  [the longest x2 1.77 us: dispatch(): slots[k * capacity:(k + 1) * capacity]]
    another operation x0 -> x1, local copies, waits for them, and re-layouts: none -> 2.99 us  [on_device(): down.reshape(features, hid)]
    reshape x0 -> x1, local copies, waits for them, and re-layouts: none -> 2.87 us  [on_device(): other[2 * features:].reshape(hid, features)]
    unnamed x36 -> x92, local copies, waits for them, and re-layouts: 2.85 us -> 4.96 us
  transfers between devices with their start and end apart: 21 -> 16, of which waited for: 10 -> 8; matrix products, arithmetic and copies ran while one was open for 13% -> 23% of each run, Pallas kernels for 0% -> 0%
where the time goes in v2:
time: 208 us; the launch traced here: 207 us
  waiting for transfers between devices  120 us (58%)
  other arithmetic  24.8 us (12%)
  matrix products  24.6 us (12%)
  starting transfers between devices  18.8 us (9%)
  local copies, waits for them, and re-layouts  17.4 us (8%)
    ppermute x16, waiting for transfers between devices, flip(): return lax.ppermute(x, 'expert', [(i, i ^ mask) for i in range(n)])  120 us
    dot_general x18, matrix products, dot(): lax.dot_general(a, b, (((ca,), (cb,)), ((), ())), preferred_element_type=...  24.6 us
    ppermute x16, starting transfers between devices, flip(): return lax.ppermute(x, 'expert', [(i, i ^ mask) for i in range(n)])  18.8 us
    concatenate x1, other arithmetic, on_device(): jnp.concatenate([gate, up, down.reshape(features, hid)], axis=0)  9.16 us
    concatenate x1, other arithmetic, share_rows(): return jnp.concatenate([pair, flip(pair, CORE)], axis=0)  5.78 us
    concatenate x3, other arithmetic, share_rows(): pair = jnp.concatenate([a, flip(a, ROW_BIT)], axis=0)  5.27 us
    unnamed x92, local copies, waits for them, and re-layouts  4.96 us
  transfers between devices with their start and end apart: 16, of which 8 were waited for; matrix products, arithmetic and copies ran while one was open for 23% of the time, Pallas kernels for 0%

profile of v2, /device:TPU:0, one launch (start us, length us, event | category | flops | bytes accessed | tf_op | source)
XLA Modules:
  0.0 207.3 jit_solution(17702062791854431992)
XLA Ops:
  0.7 0.8 xor_bitcast_fusion
  1.6 0.7 bitcast_add_fusion
  2.3 0.4 convolution_convert_fusion.2
  2.8 0.9 fusion.63
  3.6 4.0 %collective-permute-start.8 = (bf16[80,3584]{1,0:T(8,128)(2,1)}, bf16[80,3584]{1,0:T(8,128)(2,1)S(1)}, u32[]{:S(2)}, u32[]{:S(2)}) collective-permute-start(bf16[80,3584]{1,0:T(8,128)(2,1)} %get-tuple-element.30), channel_id=1, source_target_pairs={{0,8},{1,9},{2,10},{3,11},{4,12},{5,13},{6,14},{7,15},{8,0},{9,1},... | collective-permute-start | bytes 1720328 | tf_op jit(solution)/shard_map/ppermute | solution.py:21
  7.9 0.5 convolution_convert_fusion.1
  8.5 0.9 fusion.64
  9.4 1.2 pad_maximum_fusion.12
  10.6 1.6 collective-permute-start
  12.1 0.3 collective-permute-start.5
  12.5 3.0 %reshape_squeeze.3 = bf16[3584,128]{1,0:T(8,128)(2,1)} reshape(bf16[1,128,3584]{2,1,0:T(8,128)(2,1)} %param.13) | data formatting | bytes 1835008 | tf_op jit(solution)/shard_map/reshape;squeeze | solution.py:75
  15.5 18.6 %collective-permute-done.8 = bf16[80,3584]{1,0:T(8,128)(2,1)S(1)} collective-permute-done((bf16[80,3584]{1,0:T(8,128)(2,1)}, bf16[80,3584]{1,0:T(8,128)(2,1)S(1)}, u32[]{:S(2)}, u32[]{:S(2)}) %collective-permute-start.8) | collective-permute-done | bytes 573472 | tf_op jit(solution)/shard_map/ppermute | solution.py:21
  34.1 9.2 %pad_maximum_fusion.3 = bf16[10752,128]{1,0:T(8,128)(2,1)S(1)} fusion(bf16[3584,128]{1,0:T(8,128)(2,1)} %reshape_squeeze.3, bf16[3584,128]{1,0:T(8,128)(2,1)S(1)} %bitcast.25, bf16[3584,128]{1,0:T(8,128)(2,1)S(1)} %bitcast.20), kind=kLoop, calls=%fused_computation.16 | loop fusion | flops 8257536 | bytes 5505024 | tf_op jit(solution)/shard_map/concatenate | solution.py:75
  43.3 1.9 collective-permute-start.2
  45.2 13.1 %collective-permute-done.5 = bf16[80,3584]{1,0:T(8,128)(2,1)} collective-permute-done((bf16[80,3584]{1,0:T(8,128)(2,1)}, bf16[80,3584]{1,0:T(8,128)(2,1)}, u32[]{:S(2)}, u32[]{:S(2)}) %collective-permute-start.5) | collective-permute-done | bytes 573472 | tf_op jit(solution)/shard_map/ppermute | solution.py:21
  58.3 2.3 %collective-permute-start.6 = (bf16[80,3584]{1,0:T(8,128)(2,1)}, bf16[80,3584]{1,0:T(8,128)(2,1)S(1)}, u32[]{:S(2)}, u32[]{:S(2)}) collective-permute-start(bf16[80,3584]{1,0:T(8,128)(2,1)} %collective-permute-done.5), channel_id=1, source_target_pairs={{0,4},{1,5},{2,6},{3,7},{4,0},{5,1},{6,2},{7,3},{8,12},{9,13},{10,... | collective-permute-start | bytes 1720328 | tf_op jit(solution)/shard_map/ppermute | solution.py:21
  60.6 14.1 %collective-permute-done.9 = bf16[80,3584]{1,0:T(8,128)(2,1)S(1)} collective-permute-done((bf16[80,3584]{1,0:T(8,128)(2,1)S(1)}, bf16[80,3584]{1,0:T(8,128)(2,1)S(1)}, u32[]{:S(2)}, u32[]{:S(2)}) %collective-permute-start.9) | collective-permute-done | bytes 573472 | tf_op jit(solution)/shard_map/ppermute | solution.py:21
  74.8 2.9 %pad_maximum_fusion.4 = bf16[160,7168]{1,0:T(8,128)(2,1)} fusion(bf16[80,7168]{1,0:T(8,128)(2,1)} %collective-permute-done, bf16[80,3584]{1,0:T(8,128)(2,1)S(1)} %get-tuple-element.33, bf16[80,3584]{1,0:T(8,128)(2,1)S(1)} %get-tuple-element.31), kind=kLoop, calls=%fused_computation.23 | loop fusion | flops 6881280 | bytes 4587520 | tf_op jit(solution)/shard_map/concatenate | solution.py:29
  77.7 0.4 collective-permute-start.1
  78.1 7.3 %collective-permute-done.6 = bf16[80,3584]{1,0:T(8,128)(2,1)S(1)} collective-permute-done((bf16[80,3584]{1,0:T(8,128)(2,1)}, bf16[80,3584]{1,0:T(8,128)(2,1)S(1)}, u32[]{:S(2)}, u32[]{:S(2)}) %collective-permute-start.6) | collective-permute-done | bytes 573472 | tf_op jit(solution)/shard_map/ppermute | solution.py:21
  85.5 2.3 %pad_maximum_fusion.13 = bf16[160,3584]{1,0:T(8,128)(2,1)} fusion(bf16[80,3584]{1,0:T(8,128)(2,1)S(1)} %collective-permute-done.6, bf16[80,3584]{1,0:T(8,128)(2,1)} %collective-permute-done.5), kind=kLoop, calls=%fused_computation.47 | loop fusion | flops 2293760 | bytes 2293760 | tf_op jit(solution)/shard_map/concatenate | solution.py:29
  88.0 16.6 %collective-permute-done.2 = bf16[10752,128]{1,0:T(8,128)(2,1)S(1)} collective-permute-done((bf16[10752,128]{1,0:T(8,128)(2,1)S(1)}, bf16[10752,128]{1,0:T(8,128)(2,1)S(1)}, u32[]{:S(2)}, u32[]{:S(2)}) %collective-permute-start.2) | collective-permute-done | bytes 2752544 | tf_op jit(solution)/shard_map/ppermute | solution.py:21
  104.6 1.4 fusion.62
  106.0 2.9 %reshape.35 = bf16[128,3584]{1,0:T(8,128)(2,1)} reshape(bf16[3584,128]{1,0:T(8,128)(2,1)} %get-tuple-element.27) | data formatting | bytes 1835008 | tf_op jit(solution)/shard_map/reshape | solution.py:78
  108.9 2.5 %fusion.52 = f32[320,256]{1,0:T(8,128)S(1)} fusion(bf16[320,3584]{1,0:T(8,128)(2,1)} %copy-done.32, bf16[3584,128]{1,0:T(8,128)(2,1)S(1)} %get-tuple-element.25, bf16[3584,128]{1,0:T(8,128)(2,1)S(1)} %bitcast.21), kind=kOutput, calls=%fused_computation.112 | convolution fusion | flops 590872576 | bytes 4456448 | tf_op jit(solution)/shard_map/dot_general | solution.py:16
  111.4 0.3 copy-done.33
  111.8 0.8 fusion.55
  112.5 0.4 copy-done.21
  112.9 0.3 copy-done.22
  113.2 0.2 copy-done.28
  113.4 2.4 %multiply_convert_fusion.3 = (bf16[320,256]{1,0:T(8,128)(2,1)S(1)}, bf16[320]{0:T(512)(128)(2,1)S(1)}, bf16[320,256]{1,0:T(8,128)(2,1)S(1)}, bf16[320,256]{1,0:T(8,128)(2,1)S(1)}) fusion(f32[320,256]{1,0:T(8,128)S(1)} %fusion.52, f32[320,256]{1,0:T(8,128)S(1)} %fusion.55, bf16[128,3584]{1,0:T(8,128)(2,1)S(1)} %copy-done.22, ...), kind=kOutput, calls=%fused_computation.73 | convolution fusion | flops 599146176 | bytes 5276288 | tf_op jit(solution)/shard_map/dot_general | solution.py:16
  115.7 0.8 fusion.54
  116.5 0.9 fusion.1
  117.7 5.8 %pad_maximum_fusion = bf16[320,7168]{1,0:T(8,128)(2,1)S(1)} fusion(bf16[160,7168]{1,0:T(8,128)(2,1)} %collective-permute-done.1, bf16[80,7168]{1,0:T(8,128)(2,1)} %collective-permute-done, bf16[80,3584]{1,0:T(8,128)(2,1)S(1)} %get-tuple-element.33, bf16[80,3584]{1,0:T(8,128)(2,1)S(1)} %get-tuple-element.31), kind=kLoop, calls=%fused_computation.13 | loop fusion | flops 18350080 | bytes 9175040 | tf_op jit(solution)/shard_map/concatenate | solution.py:30
  123.5 0.8 fusion.17
  124.3 0.8 fusion.57
  125.1 0.3 fusion.61
  125.4 1.0 multiply_convert_fusion.5
  126.5 0.8 fusion.56
  127.3 0.9 fusion
  128.4 0.4 collective-permute-start.3
  128.8 0.5 copy-done.13
  129.3 0.4 copy-done.15
  129.7 2.1 %convolution_convert_fusion = bf16[3584,256]{1,0:T(8,128)(2,1)S(1)} fusion(bf16[160,3584]{1,0:T(8,128)(2,1)S(1)} %copy-done.15, bf16[80,3584]{1,0:T(8,128)(2,1)S(1)} %copy-done.13, bf16[80,3584]{1,0:T(8,128)(2,1)S(1)} %collective-permute-done.8, bf16[320,3584]{1,0:T(8,128)(2,1)S(1)} %get-tuple-element.24, bf16[640,128]{1,0:T(8,128)(2,1)S(1)} %get-tuple-element.42, ...), kind=kOutput, calls=%fused_computation.5 | convolution fusion | flops 1194328064 | bytes 6750208 | tf_op jit(solution)/shard_map/dot_general | solution.py:16
  131.8 1.5 collective-permute-start.14
  133.4 2.3 %convolution_convert_fusion.3 = bf16[128,3584]{1,0:T(8,128)(2,1)S(1)} fusion(bf16[160,3584]{1,0:T(8,128)(2,1)} %collective-permute-done.7, bf16[80,3584]{1,0:T(8,128)(2,1)S(1)} %copy-done.28, bf16[80,3584]{1,0:T(8,128)(2,1)} %collective-permute-done.5, bf16[320,3584]{1,0:T(8,128)(2,1)S(1)} %get-tuple-element.23, ...), kind=kOutput, calls=%fused_computation.11 | convolution fusion | flops 606339072 | bytes 5832704 | tf_op jit(solution)/shard_map/dot_general | solution.py:16
  135.7 0.6 collective-permute-start.15
  136.3 0.3 add_convert_fusion
  136.7 0.5 collective-permute-start.12
  137.2 0.3 add_convert_fusion.1
  137.6 1.7 collective-permute-start.4
  139.3 13.8 %collective-permute-done.12 = bf16[80,3712]{1,0:T(8,128)(2,1)S(1)} collective-permute-done((bf16[80,3712]{1,0:T(8,128)(2,1)S(1)}, bf16[80,3712]{1,0:T(8,128)(2,1)S(1)}, u32[]{:S(2)}, u32[]{:S(2)}) %collective-permute-start.12) | collective-permute-done | bytes 593952 | tf_op jit(solution)/shard_map/ppermute | solution.py:21
  153.3 3.3 %collective-permute-start.13 = (bf16[80,3712]{1,0:T(8,128)(2,1)S(1)}, bf16[80,3712]{1,0:T(8,128)(2,1)S(1)}, u32[]{:S(2)}, u32[]{:S(2)}) collective-permute-start(bf16[80,3712]{1,0:T(8,128)(2,1)S(1)} %add_convert_fusion.2), channel_id=1, source_target_pairs={{0,8},{1,9},{2,10},{3,11},{4,12},{5,13},{6,14},{7,15},{8,0},{9,1},... | collective-permute-start | bytes 1781768 | tf_op jit(solution)/shard_map/ppermute | solution.py:21
  156.6 20.3 %collective-permute-done.4 = bf16[80,3712]{1,0:T(8,128)(2,1)S(1)} collective-permute-done((bf16[80,3712]{1,0:T(8,128)(2,1)S(1)}, bf16[80,3712]{1,0:T(8,128)(2,1)S(1)}, u32[]{:S(2)}, u32[]{:S(2)}) %collective-permute-start.4) | collective-permute-done | bytes 593952 | tf_op jit(solution)/shard_map/ppermute | solution.py:21
  176.9 0.1 add_convert_fusion.3
  177.1 16.7 %collective-permute-done.15 = bf16[128,3584]{1,0:T(8,128)(2,1)S(1)} collective-permute-done((bf16[128,3584]{1,0:T(8,128)(2,1)S(1)}, bf16[128,3584]{1,0:T(8,128)(2,1)S(1)}, u32[]{:S(2)}, u32[]{:S(2)}) %collective-permute-start.15) | collective-permute-done | bytes 917536 | tf_op jit(solution)/shard_map/ppermute | solution.py:21
  193.8 0.5 fusion.13
  194.3 1.3 slice.184
  195.6 0.6 convert_divide_fusion
  196.3 1.4 copy.15
  197.7 3.7 %fusion.2 = bf16[3584,256]{1,0:T(8,128)(2,1)S(1)} fusion(bf16[3584,256]{1,0:T(8,128)(2,1)} %copy-done.37, bf16[160,3584]{1,0:T(8,128)(2,1)} %copy-done.14, bf16[80,3584]{1,0:T(8,128)(2,1)} %copy-done.12, bf16[80,3584]{1,0:T(8,128)(2,1)S(1)} %copy-done.11, bf16[320,3584]{1,0:T(8,128)(2,1)S(1)} %copy-done.9, bf16[320,256]{1,0:T(8,128)(2,1)S(1)} %copy-done.19, ...), kind=kOutput, calls=%fused_computation.6 | convolution fusion | flops 1197309952 | bytes 8912896 | tf_op jit(solution)/shard_map/dot_general | solution.py:16
  201.5 1.3 slice_bitcast_fusion
  202.9 0.9 copy-done.7
  204.0 3.3 %fusion.4 = bf16[1,128,3584]{2,1,0:T(8,128)(2,1)} fusion(bf16[128,3584]{1,0:T(8,128)(2,1)S(1)} %copy-done.39, bf16[160,3584]{1,0:T(8,128)(2,1)} %collective-permute-done.7, bf16[80,3584]{1,0:T(8,128)(2,1)S(1)} %copy-done.29, bf16[80,3584]{1,0:T(8,128)(2,1)} %collective-permute-done.5, bf16[320,3584]{1,0:T(8,128)(2,1)S(1)} %copy-done.7, ...), kind=kOutput, calls=%fused_computation.12 | convolution fusion | flops 607256576 | bytes 6750208 | tf_op jit(solution)/shard_map/dot_general | solution.py:16
  (108 shorter events, 1.8 us)
Async XLA Ops:
  0.6 1.7 copy-start
  0.6 7.0 %copy-start.36 = (bf16[128,1]{0,1:T(2,128)(2,1)S(1)}, bf16[128,1]{0,1:T(2,128)(2,1)}, u32[]{:S(2)}) copy-start(bf16[128,1]{0,1:T(2,128)(2,1)} %param.9) | copy-start | bytes 772
  0.7 7.3 %copy-start.20 = (bf16[128,3584]{1,0:T(8,128)(2,1)S(1)}, bf16[128,3584]{1,0:T(8,128)(2,1)}, u32[]{:S(2)}) copy-start(bf16[128,3584]{1,0:T(8,128)(2,1)} %param.8) | copy-start | bytes 2752516
  2.3 6.2 %copy-start.34 = (s32[128]{0:T(128)}, s32[128]{0:T(128)S(1)}, u32[]{:S(2)}) copy-start(s32[128]{0:T(128)S(1)} %bitcast_add_fusion) | copy-start | bytes 1540
  3.6 30.4 %collective-permute-start.8 = (bf16[80,3584]{1,0:T(8,128)(2,1)}, bf16[80,3584]{1,0:T(8,128)(2,1)S(1)}, u32[]{:S(2)}, u32[]{:S(2)}) collective-permute-start(bf16[80,3584]{1,0:T(8,128)(2,1)} %get-tuple-element.30), channel_id=1, source_target_pairs={{0,8},{1,9},{2,10},{3,11},{4,12},{5,13},{6,14},{7,15},{8,0},{9,1},... | collective-permute-start | bytes 1720328 | tf_op jit(solution)/shard_map/ppermute | solution.py:21
  7.8 0.7 copy-start.30
  9.4 24.7 %copy-start.2 = (bf16[1,3584,128]{2,1,0:T(8,128)(2,1)S(1)}, bf16[1,3584,128]{2,1,0:T(8,128)(2,1)}, u32[]{:S(2)}) copy-start(bf16[1,3584,128]{2,1,0:T(8,128)(2,1)} %param.11) | copy-start | bytes 2752516
  9.4 24.7 %copy-start.3 = (bf16[1,3584,128]{2,1,0:T(8,128)(2,1)S(1)}, bf16[1,3584,128]{2,1,0:T(8,128)(2,1)}, u32[]{:S(2)}) copy-start(bf16[1,3584,128]{2,1,0:T(8,128)(2,1)} %param.12) | copy-start | bytes 2752516
  10.6 64.3 %collective-permute-start = (bf16[80,7168]{1,0:T(8,128)(2,1)}, bf16[80,7168]{1,0:T(8,128)(2,1)}, u32[]{:S(2)}, u32[]{:S(2)}) collective-permute-start(bf16[80,7168]{1,0:T(8,128)(2,1)} %pad_maximum_fusion.12), channel_id=1, source_target_pairs={{0,4},{1,5},{2,6},{3,7},{4,0},{5,1},{6,2},{7,3},{8,12},{9,13},{10,... | collective-permute-start | bytes 3440648 | tf_op jit(solution)/shard_map/ppermute | solution.py:21
  12.1 46.2 %collective-permute-start.5 = (bf16[80,3584]{1,0:T(8,128)(2,1)}, bf16[80,3584]{1,0:T(8,128)(2,1)}, u32[]{:S(2)}, u32[]{:S(2)}) collective-permute-start(bf16[80,3584]{1,0:T(8,128)(2,1)} %get-tuple-element.32), channel_id=1, source_target_pairs={{0,8},{1,9},{2,10},{3,11},{4,12},{5,13},{6,14},{7,15},{8,0},{9,1},... | collective-permute-start | bytes 1720328 | tf_op jit(solution)/shard_map/ppermute | solution.py:21
  34.1 94.7 %copy-start.10 = (bf16[80,3584]{1,0:T(8,128)(2,1)}, bf16[80,3584]{1,0:T(8,128)(2,1)S(1)}, u32[]{:S(2)}) copy-start(bf16[80,3584]{1,0:T(8,128)(2,1)S(1)} %collective-permute-done.8) | copy-start | bytes 1720324
  34.1 40.6 %collective-permute-start.9 = (bf16[80,3584]{1,0:T(8,128)(2,1)S(1)}, bf16[80,3584]{1,0:T(8,128)(2,1)S(1)}, u32[]{:S(2)}, u32[]{:S(2)}) collective-permute-start(bf16[80,3584]{1,0:T(8,128)(2,1)S(1)} %collective-permute-done.8), channel_id=1, source_target_pairs={{0,4},{1,5},{2,6},{3,7},{4,0},{5,1},{6,2},{7,3},{8,12},{9,13},{10,... | collective-permute-start | bytes 1720328 | tf_op jit(solution)/shard_map/ppermute | solution.py:21
  43.3 61.3 %collective-permute-start.2 = (bf16[10752,128]{1,0:T(8,128)(2,1)S(1)}, bf16[10752,128]{1,0:T(8,128)(2,1)S(1)}, u32[]{:S(2)}, u32[]{:S(2)}) collective-permute-start(bf16[10752,128]{1,0:T(8,128)(2,1)S(1)} %pad_maximum_fusion.3), channel_id=1, source_target_pairs={{0,2},{1,3},{2,0},{3,1},{4,6},{5,7},{6,4},{7,5},{8,10},{9,11},{10,... | collective-permute-start | bytes 8257544 | tf_op jit(solution)/shard_map/ppermute | solution.py:21
  58.3 27.2 %collective-permute-start.6 = (bf16[80,3584]{1,0:T(8,128)(2,1)}, bf16[80,3584]{1,0:T(8,128)(2,1)S(1)}, u32[]{:S(2)}, u32[]{:S(2)}) collective-permute-start(bf16[80,3584]{1,0:T(8,128)(2,1)} %collective-permute-done.5), channel_id=1, source_target_pairs={{0,4},{1,5},{2,6},{3,7},{4,0},{5,1},{6,2},{7,3},{8,12},{9,13},{10,... | collective-permute-start | bytes 1720328 | tf_op jit(solution)/shard_map/ppermute | solution.py:21
  74.7 31.3 %copy-start.12 = (bf16[80,3584]{1,0:T(8,128)(2,1)}, bf16[80,3584]{1,0:T(8,128)(2,1)S(1)}, u32[]{:S(2)}) copy-start(bf16[80,3584]{1,0:T(8,128)(2,1)S(1)} %collective-permute-done.9) | copy-start | bytes 1720324
  74.7 13.1 %collective-permute-start.10 = (bf16[160,3584]{1,0:T(8,128)(2,1)S(1)}, bf16[160,3584]{1,0:T(8,128)(2,1)S(1)}, u32[]{:S(2)}, u32[]{:S(2)}) collective-permute-start(bf16[160,3584]{1,0:T(8,128)(2,1)S(1)} %pad_maximum_fusion.14), channel_id=1, source_target_pairs={{0,1},{1,0},{2,3},{3,2},{4,5},{5,4},{6,7},{7,6},{8,9},{9,8},{10,11... | collective-permute-start | bytes 3440648 | tf_op jit(solution)/shard_map/ppermute | solution.py:21
  77.7 40.0 %collective-permute-start.1 = (bf16[160,7168]{1,0:T(8,128)(2,1)}, bf16[160,7168]{1,0:T(8,128)(2,1)}, u32[]{:S(2)}, u32[]{:S(2)}) collective-permute-start(bf16[160,7168]{1,0:T(8,128)(2,1)} %pad_maximum_fusion.4), channel_id=1, source_target_pairs={{0,1},{1,0},{2,3},{3,2},{4,5},{5,4},{6,7},{7,6},{8,9},{9,8},{10,11... | collective-permute-start | bytes 6881288 | tf_op jit(solution)/shard_map/ppermute | solution.py:21
  85.5 2.5 %copy-start.27 = (bf16[80,3584]{1,0:T(8,128)(2,1)}, bf16[80,3584]{1,0:T(8,128)(2,1)S(1)}, u32[]{:S(2)}) copy-start(bf16[80,3584]{1,0:T(8,128)(2,1)S(1)} %collective-permute-done.6) | copy-start | bytes 1720324
  87.8 24.7 %collective-permute-start.7 = (bf16[160,3584]{1,0:T(8,128)(2,1)}, bf16[160,3584]{1,0:T(8,128)(2,1)}, u32[]{:S(2)}, u32[]{:S(2)}) collective-permute-start(bf16[160,3584]{1,0:T(8,128)(2,1)} %pad_maximum_fusion.13), channel_id=1, source_target_pairs={{0,1},{1,0},{2,3},{3,2},{4,5},{5,4},{6,7},{7,6},{8,9},{9,8},{10,11... | collective-permute-start | bytes 3440648 | tf_op jit(solution)/shard_map/ppermute | solution.py:21
  87.8 18.1 %copy-start.14 = (bf16[160,3584]{1,0:T(8,128)(2,1)}, bf16[160,3584]{1,0:T(8,128)(2,1)S(1)}, u32[]{:S(2)}) copy-start(bf16[160,3584]{1,0:T(8,128)(2,1)S(1)} %collective-permute-done.10) | copy-start | bytes 3440644
  88.0 18.0 %copy-start.32 = (bf16[320,3584]{1,0:T(8,128)(2,1)}, bf16[320,3584]{1,0:T(8,128)(2,1)S(1)}, u32[]{:S(2)}) copy-start(bf16[320,3584]{1,0:T(8,128)(2,1)S(1)} %constant_dynamic-update-slice_fusion) | copy-start | bytes 6881284
  108.8 2.6 %copy-start.4 = (bf16[1,3584,128]{2,1,0:T(8,128)(2,1)S(1)}, bf16[1,3584,128]{2,1,0:T(8,128)(2,1)}, u32[]{:S(2)}) copy-start(bf16[1,3584,128]{2,1,0:T(8,128)(2,1)} %param.12) | copy-start | bytes 2752516
  108.8 2.6 %copy-start.5 = (bf16[3584,128]{1,0:T(8,128)(2,1)S(1)}, bf16[3584,128]{1,0:T(8,128)(2,1)}, u32[]{:S(2)}) copy-start(bf16[3584,128]{1,0:T(8,128)(2,1)} %get-tuple-element.26) | copy-start | bytes 2752516
  108.8 2.9 %copy-start.33 = (bf16[320,3584]{1,0:T(8,128)(2,1)S(1)}, bf16[320,3584]{1,0:T(8,128)(2,1)}, u32[]{:S(2)}) copy-start(bf16[320,3584]{1,0:T(8,128)(2,1)} %copy-done.32) | copy-start | bytes 6881284
  111.7 1.2 copy-start.21
  111.8 1.5 copy-start.22
  111.8 1.6 copy-start.28
  115.7 13.0 %copy-start.16 = (bf16[320,256]{1,0:T(8,128)(2,1)}, bf16[320,256]{1,0:T(8,128)(2,1)S(1)}, u32[]{:S(2)}) copy-start(bf16[320,256]{1,0:T(8,128)(2,1)S(1)} %get-tuple-element.34) | copy-start | bytes 491524
  115.7 13.0 %copy-start.23 = (bf16[320,256]{1,0:T(8,128)(2,1)}, bf16[320,256]{1,0:T(8,128)(2,1)S(1)}, u32[]{:S(2)}) copy-start(bf16[320,256]{1,0:T(8,128)(2,1)S(1)} %get-tuple-element.39) | copy-start | bytes 491524
  115.7 17.6 %copy-start.42 = (bf16[320,256]{1,0:T(8,128)(2,1)}, bf16[320,256]{1,0:T(8,128)(2,1)S(1)}, u32[]{:S(2)}) copy-start(bf16[320,256]{1,0:T(8,128)(2,1)S(1)} %get-tuple-element.38) | copy-start | bytes 491524
  117.6 18.7 %collective-permute-start.11 = (bf16[160,3712]{1,0:T(8,128)(2,1)S(1)}, bf16[160,3712]{1,0:T(8,128)(2,1)S(1)}, u32[]{:S(2)}, u32[]{:S(2)}) collective-permute-start(bf16[160,3712]{1,0:T(8,128)(2,1)S(1)} %pad_maximum_fusion.8), channel_id=1, source_target_pairs={{0,1},{1,0},{2,3},{3,2},{4,5},{5,4},{6,7},{7,6},{8,9},{9,8},{10,11... | collective-permute-start | bytes 3563528 | tf_op jit(solution)/shard_map/ppermute | solution.py:21
  125.4 3.4 %copy-start.8 = (bf16[320,3584]{1,0:T(8,128)(2,1)}, bf16[320,3584]{1,0:T(8,128)(2,1)S(1)}, u32[]{:S(2)}) copy-start(bf16[320,3584]{1,0:T(8,128)(2,1)S(1)} %get-tuple-element.24) | copy-start | bytes 6881284
  125.4 8.0 %copy-start.6 = (bf16[320,3584]{1,0:T(8,128)(2,1)}, bf16[320,3584]{1,0:T(8,128)(2,1)S(1)}, u32[]{:S(2)}) copy-start(bf16[320,3584]{1,0:T(8,128)(2,1)S(1)} %get-tuple-element.23) | copy-start | bytes 6881284
  126.4 2.3 %copy-start.18 = (bf16[320,256]{1,0:T(8,128)(2,1)}, bf16[320,256]{1,0:T(8,128)(2,1)S(1)}, u32[]{:S(2)}) copy-start(bf16[320,256]{1,0:T(8,128)(2,1)S(1)} %get-tuple-element.36) | copy-start | bytes 491524
  126.4 2.3 %copy-start.25 = (bf16[320,256]{1,0:T(8,128)(2,1)}, bf16[320,256]{1,0:T(8,128)(2,1)S(1)}, u32[]{:S(2)}) copy-start(bf16[320,256]{1,0:T(8,128)(2,1)S(1)} %get-tuple-element.41) | copy-start | bytes 491524
  126.5 6.9 %copy-start.40 = (bf16[320,256]{1,0:T(8,128)(2,1)}, bf16[320,256]{1,0:T(8,128)(2,1)S(1)}, u32[]{:S(2)}) copy-start(bf16[320,256]{1,0:T(8,128)(2,1)S(1)} %get-tuple-element.40) | copy-start | bytes 491524
  128.3 1.1 copy-start.13
  128.3 1.4 copy-start.15
  128.4 8.9 %collective-permute-start.3 = (bf16[160,3712]{1,0:T(8,128)(2,1)S(1)}, bf16[160,3712]{1,0:T(8,128)(2,1)S(1)}, u32[]{:S(2)}, u32[]{:S(2)}) collective-permute-start(bf16[160,3712]{1,0:T(8,128)(2,1)S(1)} %pad_maximum_fusion.9), channel_id=1, source_target_pairs={{0,1},{1,0},{2,3},{3,2},{4,5},{5,4},{6,7},{7,6},{8,9},{9,8},{10,11... | collective-permute-start | bytes 3563528 | tf_op jit(solution)/shard_map/ppermute | solution.py:21
  131.8 61.9 %collective-permute-start.14 = (bf16[3584,256]{1,0:T(8,128)(2,1)S(1)}, bf16[3584,256]{1,0:T(8,128)(2,1)S(1)}, u32[]{:S(2)}, u32[]{:S(2)}) collective-permute-start(bf16[3584,256]{1,0:T(8,128)(2,1)S(1)} %convolution_convert_fusion), channel_id=1, source_target_pairs={{0,2},{1,3},{2,0},{3,1},{4,6},{5,7},{6,4},{7,5},{8,10},{9,11},{10,... | collective-permute-start | bytes 5505032 | tf_op jit(solution)/shard_map/ppermute | solution.py:21
  135.7 58.1 %collective-permute-start.15 = (bf16[128,3584]{1,0:T(8,128)(2,1)S(1)}, bf16[128,3584]{1,0:T(8,128)(2,1)S(1)}, u32[]{:S(2)}, u32[]{:S(2)}) collective-permute-start(bf16[128,3584]{1,0:T(8,128)(2,1)S(1)} %convolution_convert_fusion.3), channel_id=1, source_target_pairs={{0,2},{1,3},{2,0},{3,1},{4,6},{5,7},{6,4},{7,5},{8,10},{9,11},{10,... | collective-permute-start | bytes 2752520 | tf_op jit(solution)/shard_map/ppermute | solution.py:21
  136.7 16.4 %collective-permute-start.12 = (bf16[80,3712]{1,0:T(8,128)(2,1)S(1)}, bf16[80,3712]{1,0:T(8,128)(2,1)S(1)}, u32[]{:S(2)}, u32[]{:S(2)}) collective-permute-start(bf16[80,3712]{1,0:T(8,128)(2,1)S(1)} %slice.125), channel_id=1, source_target_pairs={{0,4},{1,5},{2,6},{3,7},{4,0},{5,1},{6,2},{7,3},{8,12},{9,13},{10,... | collective-permute-start | bytes 1781768 | tf_op jit(solution)/shard_map/ppermute | solution.py:21
  137.6 56.2 %copy-start.35 = (s32[128]{0:T(128)S(1)}, s32[128]{0:T(128)}, u32[]{:S(2)}) copy-start(s32[128]{0:T(128)} %copy-done.34) | copy-start | bytes 1540
  137.6 39.2 %collective-permute-start.4 = (bf16[80,3712]{1,0:T(8,128)(2,1)S(1)}, bf16[80,3712]{1,0:T(8,128)(2,1)S(1)}, u32[]{:S(2)}, u32[]{:S(2)}) collective-permute-start(bf16[80,3712]{1,0:T(8,128)(2,1)S(1)} %slice.119), channel_id=1, source_target_pairs={{0,4},{1,5},{2,6},{3,7},{4,0},{5,1},{6,2},{7,3},{8,12},{9,13},{10,... | collective-permute-start | bytes 1781768 | tf_op jit(solution)/shard_map/ppermute | solution.py:21
  153.3 40.5 %collective-permute-start.13 = (bf16[80,3712]{1,0:T(8,128)(2,1)S(1)}, bf16[80,3712]{1,0:T(8,128)(2,1)S(1)}, u32[]{:S(2)}, u32[]{:S(2)}) collective-permute-start(bf16[80,3712]{1,0:T(8,128)(2,1)S(1)} %add_convert_fusion.2), channel_id=1, source_target_pairs={{0,8},{1,9},{2,10},{3,11},{4,12},{5,13},{6,14},{7,15},{8,0},{9,1},... | collective-permute-start | bytes 1781768 | tf_op jit(solution)/shard_map/ppermute | solution.py:21
  177.0 18.6 %copy-start.31 = (bf16[128,1]{1,0:T(8,128)(2,1)S(1)}, bf16[128,1]{1,0:T(8,128)(2,1)}, u32[]{:S(2)}) copy-start(bf16[128,1]{1,0:T(8,128)(2,1)} %copy-done.30) | copy-start | bytes 772
  177.0 20.6 %copy-start.9 = (bf16[320,3584]{1,0:T(8,128)(2,1)S(1)}, bf16[320,3584]{1,0:T(8,128)(2,1)}, u32[]{:S(2)}) copy-start(bf16[320,3584]{1,0:T(8,128)(2,1)} %copy-done.8) | copy-start | bytes 6881284
  177.0 20.6 %copy-start.11 = (bf16[80,3584]{1,0:T(8,128)(2,1)S(1)}, bf16[80,3584]{1,0:T(8,128)(2,1)}, u32[]{:S(2)}) copy-start(bf16[80,3584]{1,0:T(8,128)(2,1)} %copy-done.10) | copy-start | bytes 1720324
  177.1 20.6 %copy-start.17 = (bf16[320,256]{1,0:T(8,128)(2,1)S(1)}, bf16[320,256]{1,0:T(8,128)(2,1)}, u32[]{:S(2)}) copy-start(bf16[320,256]{1,0:T(8,128)(2,1)} %copy-done.16) | copy-start | bytes 491524
  177.1 20.6 %copy-start.19 = (bf16[320,256]{1,0:T(8,128)(2,1)S(1)}, bf16[320,256]{1,0:T(8,128)(2,1)}, u32[]{:S(2)}) copy-start(bf16[320,256]{1,0:T(8,128)(2,1)} %copy-done.18) | copy-start | bytes 491524
  177.1 20.6 %copy-start.24 = (bf16[320,256]{1,0:T(8,128)(2,1)S(1)}, bf16[320,256]{1,0:T(8,128)(2,1)}, u32[]{:S(2)}) copy-start(bf16[320,256]{1,0:T(8,128)(2,1)} %copy-done.23) | copy-start | bytes 491524
  177.1 20.6 %copy-start.26 = (bf16[320,256]{1,0:T(8,128)(2,1)S(1)}, bf16[320,256]{1,0:T(8,128)(2,1)}, u32[]{:S(2)}) copy-start(bf16[320,256]{1,0:T(8,128)(2,1)} %copy-done.25) | copy-start | bytes 491524
  193.8 1.8 copy-start.38
  193.8 1.8 copy-start.37
  197.7 5.2 %copy-start.39 = (bf16[128,3584]{1,0:T(8,128)(2,1)S(1)}, bf16[128,3584]{1,0:T(8,128)(2,1)}, u32[]{:S(2)}) copy-start(bf16[128,3584]{1,0:T(8,128)(2,1)} %copy-done.38) | copy-start | bytes 2752516
  201.5 2.3 %copy-start.7 = (bf16[320,3584]{1,0:T(8,128)(2,1)S(1)}, bf16[320,3584]{1,0:T(8,128)(2,1)}, u32[]{:S(2)}) copy-start(bf16[320,3584]{1,0:T(8,128)(2,1)} %copy-done.6) | copy-start | bytes 6881284
  201.5 2.4 %copy-start.29 = (bf16[80,3584]{1,0:T(8,128)(2,1)S(1)}, bf16[80,3584]{1,0:T(8,128)(2,1)}, u32[]{:S(2)}) copy-start(bf16[80,3584]{1,0:T(8,128)(2,1)} %copy-done.27) | copy-start | bytes 1720324
  201.5 2.4 %copy-start.41 = (bf16[320,256]{1,0:T(8,128)(2,1)S(1)}, bf16[320,256]{1,0:T(8,128)(2,1)}, u32[]{:S(2)}) copy-start(bf16[320,256]{1,0:T(8,128)(2,1)} %copy-done.40) | copy-start | bytes 491524
  201.5 2.5 %copy-start.43 = (bf16[320,256]{1,0:T(8,128)(2,1)S(1)}, bf16[320,256]{1,0:T(8,128)(2,1)}, u32[]{:S(2)}) copy-start(bf16[320,256]{1,0:T(8,128)(2,1)} %copy-done.42) | copy-start | bytes 491524
  204.0 3.3 %copy-start.1 = (bf16[128,3584]{1,0:T(8,128)(2,1)S(1)}, bf16[128,3584]{1,0:T(8,128)(2,1)}, u32[]{:S(2)}) copy-start(bf16[128,3584]{1,0:T(8,128)(2,1)} %param.7) | copy-start | bytes 2752516

commit v3 on v2

--- a/solution.py
+++ b/solution.py
@@ -25,8 +25,12 @@
     return (a.astype(F32) + b.astype(F32)).astype(BF16)
 
 
-def share_rows(a):
-    pair = jnp.concatenate([a, flip(a, ROW_BIT)], axis=0)
+def after(x, *others):
+    return lax.optimization_barrier((x,) + others)[0]
+
+
+def share_core(a, b):
+    pair = jnp.concatenate([a, b], axis=0)
     return jnp.concatenate([pair, flip(pair, CORE)], axis=0)
 
 
@@ -41,8 +45,9 @@
     axis_count = lax.axis_size("expert")
     experts = axis_count // SPLIT
     tok_rows, features = tokens.shape
+    hid = w_gate.shape[2]
     capacity = min(tok_rows, 5 * tok_rows // (4 * experts))
-    hid = w_gate.shape[2]
+    capacity = -(-capacity // 16) * 16
     mine = lax.axis_index("expert") // SPLIT
 
     relative = expert_ids[:, 0] ^ mine
@@ -55,27 +60,40 @@
 
     weight = route_weight.astype(F32)
     scaled = (weight * grad_out.astype(F32)).astype(BF16)
-    slots_x = dot(select, tokens, 1, 0).astype(BF16)
-    slots_u = dot(select, scaled, 1, 0).astype(BF16)
 
-    def dispatch(slots):
-        parts = [
-            flip(slots[k * capacity : (k + 1) * capacity], SPLIT * k) for k in range(1, experts)
-        ]
-        return parts[0] if experts == 2 else jnp.concatenate(parts, axis=0)
+    def pick(source):
+        parts = [select[k * capacity : (k + 1) * capacity] for k in range(experts)]
+        return [dot(part, source, 1, 0).astype(BF16) for part in parts]
 
-    far_x = dispatch(slots_x)
-    near = share_rows(jnp.concatenate([slots_x[:capacity], slots_u[:capacity]], axis=1))
-    far_u = dispatch(slots_u)
-    near_x, near_u = near[:, :features], near[:, features:]
-    far_x = share_rows(far_x)
-    far_u = share_rows(far_u)
+    def dispatch(parts):
+        got = [flip(part, SPLIT * k) for k, part in enumerate(parts, 1)]
+        return got[0] if experts == 2 else jnp.concatenate(got, axis=0)
 
+    near_x, *far_x = pick(tokens)
+    near_u, *far_u = pick(scaled)
     gate, up, down = w_gate[0], w_up[0], w_down[0]
-    other = flip(jnp.concatenate([gate, up, down.reshape(features, hid)], axis=0), WEIGHT_BIT)
-    gate = jnp.concatenate([gate, other[:features]], axis=1)
-    up = jnp.concatenate([up, other[features : 2 * features]], axis=1)
-    down = jnp.concatenate([down, other[2 * features :].reshape(hid, features)], axis=0)
+    gate_b, up_b = flip(gate, WEIGHT_BIT), flip(up, WEIGHT_BIT)
+
+    far_x = dispatch(far_x)
+    near_x2 = flip(near_x, ROW_BIT)
+    far_x, near_x2, near_u, down_send, *far_u = lax.optimization_barrier(
+        (far_x, near_x2, near_u, down, *far_u)
+    )
+    far_u = dispatch(far_u)
+    far_x2 = flip(far_x, ROW_BIT)
+    down_b = flip(down_send, WEIGHT_BIT)
+    far_u, gate_b, up_b = lax.optimization_barrier((far_u, gate_b, up_b))
+    far_u2 = flip(far_u, ROW_BIT)
+    near_u, down_b, far_u2 = lax.optimization_barrier((near_u, down_b, far_u2))
+    near_u2 = flip(near_u, ROW_BIT)
+
+    far_x = share_core(far_x, far_x2)
+    far_u = share_core(far_u, far_u2)
+    near_x = share_core(near_x, near_x2)
+
+    gate = jnp.concatenate([gate, gate_b], axis=1)
+    up = jnp.concatenate([up, up_b], axis=1)
+    down = jnp.concatenate([down, down_b], axis=0)
 
     def hidden_pass(x, u):
         gate_pre = dot(x, gate, 1, 0)
@@ -93,32 +111,33 @@
         rows = (dot(grad_gpre, gate, 1, 1) + dot(grad_upre, up, 1, 1)).astype(BF16)
         return jnp.concatenate([rows, jnp.broadcast_to(prob, (rows.shape[0], 128))], axis=1)
 
-    near = hidden_pass(near_x, near_u)
     far = hidden_pass(far_x, far_u)
-    far_rows = sum_rows(rows_pass(*far[1:]))
-    near_rows = sum_rows(rows_pass(*near[1:]))
+    far_rows, near_u2 = lax.optimization_barrier((rows_pass(*far[1:]), near_u2))
+    near_u = share_core(near_u, near_u2)
+    far_rows = sum_rows(far_rows)
     back = [
         flip(far_rows[(k - 1) * capacity : k * capacity], SPLIT * k) for k in range(1, experts)
     ]
+    near = hidden_pass(near_x, near_u)
+    near_rows = sum_rows(rows_pass(*near[1:]))
 
     x = jnp.concatenate([near_x, far_x], axis=0)
     u = jnp.concatenate([near_u, far_u], axis=0)
     hidden, grad_gpre, grad_upre = (
         jnp.concatenate([a, b], axis=0) for a, b in zip(near[:3], far[:3])
     )
-    theirs = jnp.concatenate([grad_gpre[:, hid:], grad_upre[:, hid:]], axis=1)
-    ours = jnp.concatenate([grad_gpre[:, :hid], grad_upre[:, :hid]], axis=1)
-    got_both = flip(dot(x, theirs, 0, 0).astype(BF16), WEIGHT_BIT)
-    got_down = flip(dot(hidden[:, hid:], u, 0, 0).astype(BF16), WEIGHT_BIT)
-    near_rows, back, got_both, got_down = lax.optimization_barrier(
-        (near_rows, back, got_both, got_down)
+    def weight_grads(at):
+        return (
+            dot(x, grad_gpre[:, at], 0, 0), dot(x, grad_upre[:, at], 0, 0), dot(hidden[:, at], u, 0, 0)
+        )
+
+    got = [flip(g.astype(BF16), WEIGHT_BIT) for g in weight_grads(slice(hid, None))]
+    kept = lax.optimization_barrier(weight_grads(slice(0, hid)))
+    near_rows, back, got, kept = lax.optimization_barrier((near_rows, back, got, kept))
+    grad_gate, grad_up, grad_down = (
+        (a + b.astype(F32)).astype(BF16)[None] for a, b in zip(kept, got)
     )
-    both = (dot(x, ours, 0, 0) + got_both.astype(F32)).astype(BF16)
-    grad_gate = both[:, :hid][None]
-    grad_up = both[:, hid:][None]
-    grad_down = (dot(hidden[:, :hid], u, 0, 0) + got_down.astype(F32)).astype(BF16)[None]
     slot_rows = jnp.concatenate([near_rows] + back, axis=0)
-
     out = dot(select, slot_rows, 0, 0)
     grad_tokens = out[:, :features].astype(BF16)
     grad_combine = out[:, features : features + 1] / weight

time: 208 us -> 176 us (0.85)
  other arithmetic: 24.8 us -> 9.72 us
  waiting for transfers between devices: 120 us -> 106 us
  local copies, waits for them, and re-layouts: 17.4 us -> 5.85 us
  matrix products: 24.6 us -> 31.5 us
  starting transfers between devices: 18.8 us -> 21.8 us
    concatenate x7 -> x4, other arithmetic: 21.4 us -> 2.42 us  [share_core(): pair = jnp.concatenate([a, b], axis=0)]
    ppermute x16 -> x21, waiting for transfers between devices: 120 us -> 106 us  [flip(): return lax.ppermute(x, 'expert', [(i, i ^ mask) for i in range(n)])]
    dot_general x18 -> x22, matrix products: 24.6 us -> 31.5 us  [dot(): lax.dot_general(a, b, (((ca,), (cb,)), ((), ())), preferred_element_type=...]
    broadcast_in_dim x0 -> x2, other arithmetic: none -> 4.54 us  [on_device(): (a + b.astype(F32)).astype(BF16)[None]]
    slice x4 -> x1, local copies, waits for them, and re-layouts: 3.51 us -> 0.08 us  [sum_rows(): p = add(p[:half], flip(p[half:], CORE))]
    another operation x1 -> x0, local copies, waits for them, and re-layouts: 2.99 us -> none  [on_device(): down.reshape(features, hid)]
    ppermute x16 -> x21, starting transfers between devices: 18.8 us -> 21.8 us  [flip(): return lax.ppermute(x, 'expert', [(i, i ^ mask) for i in range(n)])]
    reshape x1 -> x0, local copies, waits for them, and re-layouts: 2.87 us -> none  [on_device(): other[2 * features:].reshape(hid, features)]
  transfers between devices with their start and end apart: 16 -> 21, of which waited for: 8 -> 12; matrix products, arithmetic and copies ran while one was open for 23% -> 21% of each run, Pallas kernels for 0% -> 0%
where the time goes in v3:
time: 176 us
  waiting for transfers between devices  106 us (60%)
  matrix products  31.5 us (18%)
  starting transfers between devices  21.8 us (12%)
  other arithmetic  9.72 us (6%)
  local copies, waits for them, and re-layouts  5.85 us (3%)
    ppermute x21, waiting for transfers between devices, flip(): return lax.ppermute(x, 'expert', [(i, i ^ mask) for i in range(n)])  106 us
    dot_general x22, matrix products, dot(): lax.dot_general(a, b, (((ca,), (cb,)), ((), ())), preferred_element_type=...  31.5 us
    ppermute x21, starting transfers between devices, flip(): return lax.ppermute(x, 'expert', [(i, i ^ mask) for i in range(n)])  21.8 us
    broadcast_in_dim x2, other arithmetic, on_device(): (a + b.astype(F32)).astype(BF16)[None]  4.54 us
    unnamed x41, local copies, waits for them, and re-layouts  4.23 us
  transfers between devices with their start and end apart: 21, of which 12 were waited for; matrix products, arithmetic and copies ran while one was open for 21% of the time, Pallas kernels for 0%

profile of v3, /device:TPU:0, one launch (start us, length us, event | category | flops | bytes accessed | tf_op | source)
XLA Modules:
  0.0 175.9 jit_solution(6381110509304732133)
XLA Ops:
  0.7 0.8 xor_bitcast_fusion
  1.6 0.7 bitcast_add_fusion
  2.3 1.1 convolution_convert_fusion.6
  3.5 4.0 %collective-permute-start = (bf16[80,3584]{1,0:T(8,128)(2,1)}, bf16[80,3584]{1,0:T(8,128)(2,1)}, u32[]{:S(2)}, u32[]{:S(2)}) collective-permute-start(bf16[80,3584]{1,0:T(8,128)(2,1)} %convolution_convert_fusion.6), channel_id=1, source_target_pairs={{0,8},{1,9},{2,10},{3,11},{4,12},{5,13},{6,14},{7,15},{8,0},{9,1},... | collective-permute-start | bytes 1720328 | tf_op jit(solution)/shard_map/ppermute | solution.py:21
  7.5 1.1 constant_dynamic-update-slice_fusion.8
  8.6 1.6 collective-permute-start.1
  10.2 1.5 collective-permute-start.4
  11.7 0.5 collective-permute-start.5
  12.5 1.7 convolution_convert_fusion.4
  14.2 1.6 convolution_convert_fusion.3
  15.8 17.4 %collective-permute-done = bf16[80,3584]{1,0:T(8,128)(2,1)} collective-permute-done((bf16[80,3584]{1,0:T(8,128)(2,1)}, bf16[80,3584]{1,0:T(8,128)(2,1)}, u32[]{:S(2)}, u32[]{:S(2)}) %collective-permute-start) | collective-permute-done | bytes 573472 | tf_op jit(solution)/shard_map/ppermute | solution.py:21
  33.2 1.1 collective-permute-done.1
  34.3 0.5 collective-permute-start.3
  34.7 1.5 collective-permute-start.2
  36.2 2.6 %collective-permute-start.8 = (bf16[80,3584]{1,0:T(8,128)(2,1)}, bf16[80,3584]{1,0:T(8,128)(2,1)S(1)}, u32[]{:S(2)}, u32[]{:S(2)}) collective-permute-start(bf16[80,3584]{1,0:T(8,128)(2,1)} %collective-permute-done), channel_id=1, source_target_pairs={{0,4},{1,5},{2,6},{3,7},{4,0},{5,1},{6,2},{7,3},{8,12},{9,13},{10,... | collective-permute-start | bytes 1720328 | tf_op jit(solution)/shard_map/ppermute | solution.py:21
  38.8 1.1 pad_maximum_fusion.11
  40.1 13.3 %collective-permute-done.5 = bf16[3584,128]{1,0:T(8,128)(2,1)S(1)} collective-permute-done((bf16[3584,128]{1,0:T(8,128)(2,1)S(1)}, bf16[3584,128]{1,0:T(8,128)(2,1)S(1)}, u32[]{:S(2)}, u32[]{:S(2)}) %collective-permute-start.5) | collective-permute-done | bytes 917536 | tf_op jit(solution)/shard_map/ppermute | solution.py:21
  53.4 7.2 %collective-permute-done.3 = bf16[80,3584]{1,0:T(8,128)(2,1)S(1)} collective-permute-done((bf16[80,3584]{1,0:T(8,128)(2,1)S(1)}, bf16[80,3584]{1,0:T(8,128)(2,1)S(1)}, u32[]{:S(2)}, u32[]{:S(2)}) %collective-permute-start.3) | collective-permute-done | bytes 573472 | tf_op jit(solution)/shard_map/ppermute | solution.py:21
  60.6 1.1 constant_dynamic-update-slice_fusion.7
  61.7 1.0 collective-permute-done.8
  62.7 1.1 pad_maximum_fusion.9
  63.9 7.4 %collective-permute-done.2 = bf16[128,3584]{1,0:T(8,128)(2,1)S(1)} collective-permute-done((bf16[128,3584]{1,0:T(8,128)(2,1)}, bf16[128,3584]{1,0:T(8,128)(2,1)S(1)}, u32[]{:S(2)}, u32[]{:S(2)}) %collective-permute-start.2) | collective-permute-done | bytes 917536 | tf_op jit(solution)/shard_map/ppermute | solution.py:21
  71.3 3.1 %collective-permute-done.6 = bf16[80,3584]{1,0:T(8,128)(2,1)S(1)} collective-permute-done((bf16[80,3584]{1,0:T(8,128)(2,1)S(1)}, bf16[80,3584]{1,0:T(8,128)(2,1)S(1)}, u32[]{:S(2)}, u32[]{:S(2)}) %collective-permute-start.6) | collective-permute-done | bytes 573472 | tf_op jit(solution)/shard_map/ppermute | solution.py:21
  74.5 0.6 collective-permute-start.10
  75.2 1.1 constant_dynamic-update-slice_fusion.5
  76.6 0.8 fusion.59
  77.4 0.4 copy-done.14
  77.7 0.8 fusion.2
  78.5 2.5 %multiply_convert_fusion.6 = (bf16[320,256]{1,0:T(8,128)(2,1)S(1)}, bf16[320]{0:T(512)(128)(2,1)S(1)}, bf16[320,256]{1,0:T(8,128)(2,1)S(1)}, bf16[320,256]{1,0:T(8,128)(2,1)S(1)}) fusion(f32[320,256]{1,0:T(8,128)S(1)} %fusion.2, f32[320,256]{1,0:T(8,128)S(1)} %fusion.59, bf16[320,3584]{1,0:T(8,128)(2,1)S(1)} %get-tuple-element.64, ...), kind=kOutput, calls=%fused_computation.69 | convolution fusion | flops 592264896 | bytes 5276288 | tf_op jit(solution)/shard_map/dot_general | solution.py:16
  81.0 2.3 %fusion.57 = f32[320,3584]{1,0:T(8,128)S(1)} fusion(bf16[320,256]{1,0:T(8,128)(2,1)S(1)} %get-tuple-element.67, bf16[3584,128]{1,0:T(8,128)(2,1)} %collective-permute-done.4, bf16[3584,128]{1,0:T(8,128)(2,1)} %bitcast.3), kind=kOutput, calls=%fused_computation.126 | convolution fusion | flops 590872576 | bytes 6586368 | tf_op jit(solution)/shard_map/dot_general | solution.py:16
  83.3 0.8 fusion
  84.2 0.2 pad_maximum_fusion
  84.3 5.6 %collective-permute-done.10 = bf16[80,3584]{1,0:T(8,128)(2,1)S(1)} collective-permute-done((bf16[80,3584]{1,0:T(8,128)(2,1)S(1)}, bf16[80,3584]{1,0:T(8,128)(2,1)S(1)}, u32[]{:S(2)}, u32[]{:S(2)}) %collective-permute-start.10) | collective-permute-done | bytes 573472 | tf_op jit(solution)/shard_map/ppermute | solution.py:21
  90.1 1.8 %fusion.21 = f32[320,256]{1,0:T(8,128)S(1)} fusion(bf16[160,3584]{1,0:T(8,128)(2,1)S(1)} %collective-permute-done.12, bf16[80,3584]{1,0:T(8,128)(2,1)} %collective-permute-done.1, bf16[80,3584]{1,0:T(8,128)(2,1)S(1)} %get-tuple-element.78, bf16[3584,128]{1,0:T(8,128)(2,1)S(1)} %collective-permute-done.5, bf16[3584,128]{1,0:T(8,128)(2,1)S(1)} %bitcast.30), kind=kOutput, calls=%fused_computation.52 | convolution fusion | flops 597753856 | bytes 4456448 | tf_op jit(solution)/shard_map/dot_general | solution.py:16
  92.0 0.6 collective-permute-start.15
  92.6 0.2 collective-permute-done.11
  92.9 0.8 fusion.8
  93.7 2.6 %multiply_convert_fusion.4 = (bf16[320,256]{1,0:T(8,128)(2,1)S(1)}, bf16[320]{0:T(512)(128)(2,1)S(1)}, bf16[320,256]{1,0:T(8,128)(2,1)S(1)}, bf16[320,256]{1,0:T(8,128)(2,1)S(1)}) fusion(f32[320,256]{1,0:T(8,128)S(1)} %fusion.8, f32[320,256]{1,0:T(8,128)S(1)} %fusion.21, bf16[3584,128]{1,0:T(8,128)(2,1)} %collective-permute-done.4, ...), kind=kOutput, calls=%fused_computation.64 | convolution fusion | flops 599146176 | bytes 5276288 | tf_op jit(solution)/shard_map/dot_general | solution.py:16
  96.3 2.3 %fusion.56 = f32[320,3584]{1,0:T(8,128)S(1)} fusion(bf16[320,256]{1,0:T(8,128)(2,1)S(1)} %get-tuple-element.65, bf16[3584,128]{1,0:T(8,128)(2,1)} %collective-permute-done.4, bf16[3584,128]{1,0:T(8,128)(2,1)} %bitcast.3), kind=kOutput, calls=%fused_computation.125 | convolution fusion | flops 590872576 | bytes 6586368 | tf_op jit(solution)/shard_map/dot_general | solution.py:16
  98.5 1.4 convolution_convert_fusion.2
  99.9 1.4 fusion.37
  101.3 1.6 convolution_convert_fusion.1
  102.9 2.7 %fusion.35 = f32[3584,128]{1,0:T(8,128)} fusion(bf16[640,3584]{1,0:T(8,128)(2,1)S(1)} %get-tuple-element.63, bf16[320,256]{1,0:T(8,128)(2,1)S(1)} %get-tuple-element.70, bf16[320,256]{1,0:T(8,128)(2,1)S(1)} %get-tuple-element.72), kind=kOutput, calls=%fused_computation.79 | convolution fusion | flops 587530240 | bytes 6750208 | tf_op jit(solution)/shard_map/dot_general | solution.py:16
  105.6 0.8 fusion.1
  106.6 0.2 collective-permute-start.13
  106.8 0.4 collective-permute-start.18
  107.2 1.7 collective-permute-start.19
  109.1 2.1 %fusion.33 = f32[128,3584]{1,0:T(8,128)} fusion(bf16[640,3584]{1,0:T(8,128)(2,1)S(1)} %constant_dynamic-update-slice_fusion.9, bf16[320,256]{1,0:T(8,128)(2,1)S(1)} %get-tuple-element.69, bf16[320,256]{1,0:T(8,128)(2,1)S(1)} %get-tuple-element.71), kind=kOutput, calls=%fused_computation.76 | convolution fusion | flops 587530240 | bytes 6750208 | tf_op jit(solution)/shard_map/dot_general | solution.py:16
  111.2 0.9 convolution_convert_fusion
  112.1 0.4 collective-permute-start.20
  112.6 0.3 add_convert_fusion
  112.9 1.7 collective-permute-start.16
  114.6 0.3 add_convert_fusion.1
  115.0 0.5 collective-permute-start.14
  115.4 13.9 %collective-permute-done.16 = bf16[80,3712]{1,0:T(8,128)(2,1)S(1)} collective-permute-done((bf16[80,3712]{1,0:T(8,128)(2,1)S(1)}, bf16[80,3712]{1,0:T(8,128)(2,1)S(1)}, u32[]{:S(2)}, u32[]{:S(2)}) %collective-permute-start.16) | collective-permute-done | bytes 593952 | tf_op jit(solution)/shard_map/ppermute | solution.py:21
  129.4 3.3 %collective-permute-start.17 = (bf16[80,3712]{1,0:T(8,128)(2,1)S(1)}, bf16[80,3712]{1,0:T(8,128)(2,1)S(1)}, u32[]{:S(2)}, u32[]{:S(2)}) collective-permute-start(bf16[80,3712]{1,0:T(8,128)(2,1)S(1)} %add_convert_fusion.5), channel_id=1, source_target_pairs={{0,8},{1,9},{2,10},{3,11},{4,12},{5,13},{6,14},{7,15},{8,0},{9,1},... | collective-permute-start | bytes 1781768 | tf_op jit(solution)/shard_map/ppermute | solution.py:21
  132.8 20.3 %collective-permute-done.14 = bf16[80,3712]{1,0:T(8,128)(2,1)S(1)} collective-permute-done((bf16[80,3712]{1,0:T(8,128)(2,1)S(1)}, bf16[80,3712]{1,0:T(8,128)(2,1)S(1)}, u32[]{:S(2)}, u32[]{:S(2)}) %collective-permute-start.14) | collective-permute-done | bytes 593952 | tf_op jit(solution)/shard_map/ppermute | solution.py:21
  153.3 15.5 %collective-permute-done.20 = bf16[128,3584]{1,0:T(8,128)(2,1)S(1)} collective-permute-done((bf16[128,3584]{1,0:T(8,128)(2,1)S(1)}, bf16[128,3584]{1,0:T(8,128)(2,1)S(1)}, u32[]{:S(2)}, u32[]{:S(2)}) %collective-permute-start.20) | collective-permute-done | bytes 917536 | tf_op jit(solution)/shard_map/ppermute | solution.py:21
  168.8 0.5 fusion.15
  169.2 0.5 copy-done.12
  169.7 1.0 slice.136
  170.7 0.6 copy.15
  171.3 3.0 %fusion.24 = bf16[1,128,3584]{2,1,0:T(8,128)(2,1)} fusion(f32[128,3584]{1,0:T(8,128)} %fusion.33, bf16[128,3584]{1,0:T(8,128)(2,1)} %copy-done.12), kind=kLoop, calls=%fused_computation.55 | loop fusion | flops 1376256 | bytes 3670016 | tf_op jit(solution)/shard_map/broadcast_in_dim | solution.py:138
  174.3 1.6 fusion.22
  (66 shorter events, 2.3 us)
Async XLA Ops:
  0.6 1.7 copy-start
  0.6 11.0 %copy-start.4 = (bf16[1,3584,128]{2,1,0:T(8,128)(2,1)S(1)}, bf16[1,3584,128]{2,1,0:T(8,128)(2,1)}, u32[]{:S(2)}) copy-start(bf16[1,3584,128]{2,1,0:T(8,128)(2,1)} %param.12) | copy-start | bytes 2752516
  0.7 11.6 %copy-start.13 = (bf16[128,1]{0,1:T(2,128)(2,1)S(1)}, bf16[128,1]{0,1:T(2,128)(2,1)}, u32[]{:S(2)}) copy-start(bf16[128,1]{0,1:T(2,128)(2,1)} %param.9) | copy-start | bytes 772
  3.5 29.7 %collective-permute-start = (bf16[80,3584]{1,0:T(8,128)(2,1)}, bf16[80,3584]{1,0:T(8,128)(2,1)}, u32[]{:S(2)}, u32[]{:S(2)}) collective-permute-start(bf16[80,3584]{1,0:T(8,128)(2,1)} %convolution_convert_fusion.6), channel_id=1, source_target_pairs={{0,8},{1,9},{2,10},{3,11},{4,12},{5,13},{6,14},{7,15},{8,0},{9,1},... | collective-permute-start | bytes 1720328 | tf_op jit(solution)/shard_map/ppermute | solution.py:21
  8.6 25.7 %collective-permute-start.1 = (bf16[80,3584]{1,0:T(8,128)(2,1)S(1)}, bf16[80,3584]{1,0:T(8,128)(2,1)}, u32[]{:S(2)}, u32[]{:S(2)}) collective-permute-start(bf16[80,3584]{1,0:T(8,128)(2,1)S(1)} %get-tuple-element.78), channel_id=1, source_target_pairs={{0,4},{1,5},{2,6},{3,7},{4,0},{5,1},{6,2},{7,3},{8,12},{9,13},{10,... | collective-permute-start | bytes 1720328 | tf_op jit(solution)/shard_map/ppermute | solution.py:21
  10.2 29.8 %collective-permute-start.4 = (bf16[3584,128]{1,0:T(8,128)(2,1)}, bf16[3584,128]{1,0:T(8,128)(2,1)}, u32[]{:S(2)}, u32[]{:S(2)}) collective-permute-start(bf16[3584,128]{1,0:T(8,128)(2,1)} %bitcast.3), channel_id=1, source_target_pairs={{0,2},{1,3},{2,0},{3,1},{4,6},{5,7},{6,4},{7,5},{8,10},{9,11},{10,... | collective-permute-start | bytes 2752520 | tf_op jit(solution)/shard_map/ppermute | solution.py:21
  11.7 41.7 %collective-permute-start.5 = (bf16[3584,128]{1,0:T(8,128)(2,1)S(1)}, bf16[3584,128]{1,0:T(8,128)(2,1)S(1)}, u32[]{:S(2)}, u32[]{:S(2)}) collective-permute-start(bf16[3584,128]{1,0:T(8,128)(2,1)S(1)} %bitcast.27), channel_id=1, source_target_pairs={{0,2},{1,3},{2,0},{3,1},{4,6},{5,7},{6,4},{7,5},{8,10},{9,11},{10,... | collective-permute-start | bytes 2752520 | tf_op jit(solution)/shard_map/ppermute | solution.py:21
  12.5 48.1 %copy-start.2 = (bf16[640,3584]{1,0:T(8,128)(2,1)S(1)}, bf16[640,3584]{1,0:T(8,128)(2,1)}, u32[]{:S(2)}) copy-start(bf16[640,3584]{1,0:T(8,128)(2,1)} %get-tuple-element.77) | copy-start | bytes 13762564
  34.3 26.3 %collective-permute-start.3 = (bf16[80,3584]{1,0:T(8,128)(2,1)S(1)}, bf16[80,3584]{1,0:T(8,128)(2,1)S(1)}, u32[]{:S(2)}, u32[]{:S(2)}) collective-permute-start(bf16[80,3584]{1,0:T(8,128)(2,1)S(1)} %convolution_convert_fusion.3), channel_id=1, source_target_pairs={{0,8},{1,9},{2,10},{3,11},{4,12},{5,13},{6,14},{7,15},{8,0},{9,1},... | collective-permute-start | bytes 1720328 | tf_op jit(solution)/shard_map/ppermute | solution.py:21
  34.7 36.5 %collective-permute-start.2 = (bf16[128,3584]{1,0:T(8,128)(2,1)}, bf16[128,3584]{1,0:T(8,128)(2,1)S(1)}, u32[]{:S(2)}, u32[]{:S(2)}) collective-permute-start(bf16[128,3584]{1,0:T(8,128)(2,1)} %bitcast.32), channel_id=1, source_target_pairs={{0,2},{1,3},{2,0},{3,1},{4,6},{5,7},{6,4},{7,5},{8,10},{9,11},{10,... | collective-permute-start | bytes 2752520 | tf_op jit(solution)/shard_map/ppermute | solution.py:21
  36.2 26.4 %collective-permute-start.8 = (bf16[80,3584]{1,0:T(8,128)(2,1)}, bf16[80,3584]{1,0:T(8,128)(2,1)S(1)}, u32[]{:S(2)}, u32[]{:S(2)}) collective-permute-start(bf16[80,3584]{1,0:T(8,128)(2,1)} %collective-permute-done), channel_id=1, source_target_pairs={{0,4},{1,5},{2,6},{3,7},{4,0},{5,1},{6,2},{7,3},{8,12},{9,13},{10,... | collective-permute-start | bytes 1720328 | tf_op jit(solution)/shard_map/ppermute | solution.py:21
  40.0 35.1 %collective-permute-start.12 = (bf16[160,3584]{1,0:T(8,128)(2,1)S(1)}, bf16[160,3584]{1,0:T(8,128)(2,1)S(1)}, u32[]{:S(2)}, u32[]{:S(2)}) collective-permute-start(bf16[160,3584]{1,0:T(8,128)(2,1)S(1)} %pad_maximum_fusion.11), channel_id=1, source_target_pairs={{0,1},{1,0},{2,3},{3,2},{4,5},{5,4},{6,7},{7,6},{8,9},{9,8},{10,11... | collective-permute-start | bytes 3440648 | tf_op jit(solution)/shard_map/ppermute | solution.py:21
  53.4 36.7 %copy-start.6 = (bf16[3584,128]{1,0:T(8,128)(2,1)}, bf16[3584,128]{1,0:T(8,128)(2,1)S(1)}, u32[]{:S(2)}) copy-start(bf16[3584,128]{1,0:T(8,128)(2,1)S(1)} %collective-permute-done.5) | copy-start | bytes 2752516
  60.6 13.8 %collective-permute-start.6 = (bf16[80,3584]{1,0:T(8,128)(2,1)S(1)}, bf16[80,3584]{1,0:T(8,128)(2,1)S(1)}, u32[]{:S(2)}, u32[]{:S(2)}) collective-permute-start(bf16[80,3584]{1,0:T(8,128)(2,1)S(1)} %collective-permute-done.3), channel_id=1, source_target_pairs={{0,4},{1,5},{2,6},{3,7},{4,0},{5,1},{6,2},{7,3},{8,12},{9,13},{10,... | collective-permute-start | bytes 1720328 | tf_op jit(solution)/shard_map/ppermute | solution.py:21
  63.8 12.6 %collective-permute-start.9 = (bf16[160,3584]{1,0:T(8,128)(2,1)S(1)}, bf16[160,3584]{1,0:T(8,128)(2,1)S(1)}, u32[]{:S(2)}, u32[]{:S(2)}) collective-permute-start(bf16[160,3584]{1,0:T(8,128)(2,1)S(1)} %pad_maximum_fusion.9), channel_id=1, source_target_pairs={{0,1},{1,0},{2,3},{3,2},{4,5},{5,4},{6,7},{7,6},{8,9},{9,8},{10,11... | collective-permute-start | bytes 3440648 | tf_op jit(solution)/shard_map/ppermute | solution.py:21
  74.4 2.9 %collective-permute-start.7 = (bf16[160,3584]{1,0:T(8,128)(2,1)S(1)}, bf16[160,3584]{1,0:T(8,128)(2,1)S(1)}, u32[]{:S(2)}, u32[]{:S(2)}) collective-permute-start(bf16[160,3584]{1,0:T(8,128)(2,1)S(1)} %pad_maximum_fusion.8), channel_id=1, source_target_pairs={{0,1},{1,0},{2,3},{3,2},{4,5},{5,4},{6,7},{7,6},{8,9},{9,8},{10,11... | collective-permute-start | bytes 3440648 | tf_op jit(solution)/shard_map/ppermute | solution.py:21
  74.5 15.4 %collective-permute-start.10 = (bf16[80,3584]{1,0:T(8,128)(2,1)S(1)}, bf16[80,3584]{1,0:T(8,128)(2,1)S(1)}, u32[]{:S(2)}, u32[]{:S(2)}) collective-permute-start(bf16[80,3584]{1,0:T(8,128)(2,1)S(1)} %convolution_convert_fusion.4), channel_id=1, source_target_pairs={{0,4},{1,5},{2,6},{3,7},{4,0},{5,1},{6,2},{7,3},{8,12},{9,13},{10,... | collective-permute-start | bytes 1720328 | tf_op jit(solution)/shard_map/ppermute | solution.py:21
  76.6 1.2 copy-start.14
  90.0 2.9 %collective-permute-start.11 = (bf16[160,3584]{1,0:T(8,128)(2,1)S(1)}, bf16[160,3584]{1,0:T(8,128)(2,1)S(1)}, u32[]{:S(2)}, u32[]{:S(2)}) collective-permute-start(bf16[160,3584]{1,0:T(8,128)(2,1)S(1)} %pad_maximum_fusion.10), channel_id=1, source_target_pairs={{0,1},{1,0},{2,3},{3,2},{4,5},{5,4},{6,7},{7,6},{8,9},{9,8},{10,11... | collective-permute-start | bytes 3440648 | tf_op jit(solution)/shard_map/ppermute | solution.py:21
  92.0 20.5 %collective-permute-start.15 = (bf16[160,3712]{1,0:T(8,128)(2,1)S(1)}, bf16[160,3712]{1,0:T(8,128)(2,1)S(1)}, u32[]{:S(2)}, u32[]{:S(2)}) collective-permute-start(bf16[160,3712]{1,0:T(8,128)(2,1)S(1)} %slice.64), channel_id=1, source_target_pairs={{0,1},{1,0},{2,3},{3,2},{4,5},{5,4},{6,7},{7,6},{8,9},{9,8},{10,11... | collective-permute-start | bytes 3563528 | tf_op jit(solution)/shard_map/ppermute | solution.py:21
  102.9 2.7 %copy-start.5 = (bf16[1,3584,128]{2,1,0:T(8,128)(2,1)S(1)}, bf16[1,3584,128]{2,1,0:T(8,128)(2,1)}, u32[]{:S(2)}) copy-start(bf16[1,3584,128]{2,1,0:T(8,128)(2,1)} %param.12) | copy-start | bytes 2752516
  102.9 2.7 %copy-start.7 = (bf16[3584,128]{1,0:T(8,128)(2,1)S(1)}, bf16[3584,128]{1,0:T(8,128)(2,1)}, u32[]{:S(2)}) copy-start(bf16[3584,128]{1,0:T(8,128)(2,1)} %copy-done.6) | copy-start | bytes 2752516
  106.6 8.0 %collective-permute-start.13 = (bf16[160,3712]{1,0:T(8,128)(2,1)S(1)}, bf16[160,3712]{1,0:T(8,128)(2,1)S(1)}, u32[]{:S(2)}, u32[]{:S(2)}) collective-permute-start(bf16[160,3712]{1,0:T(8,128)(2,1)S(1)} %pad_maximum_fusion.5), channel_id=1, source_target_pairs={{0,1},{1,0},{2,3},{3,2},{4,5},{5,4},{6,7},{7,6},{8,9},{9,8},{10,11... | collective-permute-start | bytes 3563528 | tf_op jit(solution)/shard_map/ppermute | solution.py:21
  106.8 46.4 %collective-permute-start.18 = (bf16[3584,128]{1,0:T(8,128)(2,1)S(1)}, bf16[3584,128]{1,0:T(8,128)(2,1)S(1)}, u32[]{:S(2)}, u32[]{:S(2)}) collective-permute-start(bf16[3584,128]{1,0:T(8,128)(2,1)S(1)} %convolution_convert_fusion.2), channel_id=1, source_target_pairs={{0,2},{1,3},{2,0},{3,1},{4,6},{5,7},{6,4},{7,5},{8,10},{9,11},{10,... | collective-permute-start | bytes 2752520 | tf_op jit(solution)/shard_map/ppermute | solution.py:21
  107.2 46.1 %collective-permute-start.19 = (bf16[3584,128]{1,0:T(8,128)(2,1)S(1)}, bf16[3584,128]{1,0:T(8,128)(2,1)S(1)}, u32[]{:S(2)}, u32[]{:S(2)}) collective-permute-start(bf16[3584,128]{1,0:T(8,128)(2,1)S(1)} %convolution_convert_fusion.1), channel_id=1, source_target_pairs={{0,2},{1,3},{2,0},{3,1},{4,6},{5,7},{6,4},{7,5},{8,10},{9,11},{10,... | collective-permute-start | bytes 2752520 | tf_op jit(solution)/shard_map/ppermute | solution.py:21
  112.1 56.6 %collective-permute-start.20 = (bf16[128,3584]{1,0:T(8,128)(2,1)S(1)}, bf16[128,3584]{1,0:T(8,128)(2,1)S(1)}, u32[]{:S(2)}, u32[]{:S(2)}) collective-permute-start(bf16[128,3584]{1,0:T(8,128)(2,1)S(1)} %convolution_convert_fusion), channel_id=1, source_target_pairs={{0,2},{1,3},{2,0},{3,1},{4,6},{5,7},{6,4},{7,5},{8,10},{9,11},{10,... | collective-permute-start | bytes 2752520 | tf_op jit(solution)/shard_map/ppermute | solution.py:21
  112.9 16.4 %collective-permute-start.16 = (bf16[80,3712]{1,0:T(8,128)(2,1)S(1)}, bf16[80,3712]{1,0:T(8,128)(2,1)S(1)}, u32[]{:S(2)}, u32[]{:S(2)}) collective-permute-start(bf16[80,3712]{1,0:T(8,128)(2,1)S(1)} %slice.82), channel_id=1, source_target_pairs={{0,4},{1,5},{2,6},{3,7},{4,0},{5,1},{6,2},{7,3},{8,12},{9,13},{10,... | collective-permute-start | bytes 1781768 | tf_op jit(solution)/shard_map/ppermute | solution.py:21
  115.0 38.1 %collective-permute-start.14 = (bf16[80,3712]{1,0:T(8,128)(2,1)S(1)}, bf16[80,3712]{1,0:T(8,128)(2,1)S(1)}, u32[]{:S(2)}, u32[]{:S(2)}) collective-permute-start(bf16[80,3712]{1,0:T(8,128)(2,1)S(1)} %slice.80), channel_id=1, source_target_pairs={{0,4},{1,5},{2,6},{3,7},{4,0},{5,1},{6,2},{7,3},{8,12},{9,13},{10,... | collective-permute-start | bytes 1781768 | tf_op jit(solution)/shard_map/ppermute | solution.py:21
  129.4 39.3 %collective-permute-start.17 = (bf16[80,3712]{1,0:T(8,128)(2,1)S(1)}, bf16[80,3712]{1,0:T(8,128)(2,1)S(1)}, u32[]{:S(2)}, u32[]{:S(2)}) collective-permute-start(bf16[80,3712]{1,0:T(8,128)(2,1)S(1)} %add_convert_fusion.5), channel_id=1, source_target_pairs={{0,8},{1,9},{2,10},{3,11},{4,12},{5,13},{6,14},{7,15},{8,0},{9,1},... | collective-permute-start | bytes 1781768 | tf_op jit(solution)/shard_map/ppermute | solution.py:21
  153.2 17.5 %copy-start.8 = (bf16[3584,128]{1,0:T(8,128)(2,1)}, bf16[3584,128]{1,0:T(8,128)(2,1)S(1)}, u32[]{:S(2)}) copy-start(bf16[3584,128]{1,0:T(8,128)(2,1)S(1)} %collective-permute-done.18) | copy-start | bytes 2752516
  153.3 17.5 %copy-start.10 = (bf16[3584,128]{1,0:T(8,128)(2,1)}, bf16[3584,128]{1,0:T(8,128)(2,1)S(1)}, u32[]{:S(2)}) copy-start(bf16[3584,128]{1,0:T(8,128)(2,1)S(1)} %collective-permute-done.19) | copy-start | bytes 2752516
  168.8 0.9 copy-start.12
  171.3 3.0 %copy-start.3 = (f32[3584,128]{1,0:T(8,128)S(1)}, f32[3584,128]{1,0:T(8,128)}, u32[]{:S(2)}) copy-start(f32[3584,128]{1,0:T(8,128)} %fusion.35) | copy-start | bytes 5505028
  171.3 3.0 %copy-start.9 = (bf16[3584,128]{1,0:T(8,128)(2,1)S(1)}, bf16[3584,128]{1,0:T(8,128)(2,1)}, u32[]{:S(2)}) copy-start(bf16[3584,128]{1,0:T(8,128)(2,1)} %copy-done.8) | copy-start | bytes 2752516
  171.3 3.0 %copy-start.11 = (bf16[3584,128]{1,0:T(8,128)(2,1)S(1)}, bf16[3584,128]{1,0:T(8,128)(2,1)}, u32[]{:S(2)}) copy-start(bf16[3584,128]{1,0:T(8,128)(2,1)} %copy-done.10) | copy-start | bytes 2752516
  171.3 4.6 %copy-start.1 = (bf16[128,3584]{1,0:T(8,128)(2,1)S(1)}, bf16[128,3584]{1,0:T(8,128)(2,1)}, u32[]{:S(2)}) copy-start(bf16[128,3584]{1,0:T(8,128)(2,1)} %param.7) | copy-start | bytes 2752516

commit v4 on v3

--- a/solution.py
+++ b/solution.py
@@ -132,15 +132,22 @@
         )
 
     got = [flip(g.astype(BF16), WEIGHT_BIT) for g in weight_grads(slice(hid, None))]
-    kept = lax.optimization_barrier(weight_grads(slice(0, hid)))
-    near_rows, back, got, kept = lax.optimization_barrier((near_rows, back, got, kept))
-    grad_gate, grad_up, grad_down = (
-        (a + b.astype(F32)).astype(BF16)[None] for a, b in zip(kept, got)
-    )
     slot_rows = jnp.concatenate([near_rows] + back, axis=0)
     out = dot(select, slot_rows, 0, 0)
     grad_tokens = out[:, :features].astype(BF16)
     grad_combine = out[:, features : features + 1] / weight
+
+    grads = []
+    before = grad_tokens
+    for own, other in zip(weight_grads(slice(0, hid)), got):
+        other, before = lax.optimization_barrier((other, before))
+        if not grads:
+            grad_tokens = before
+        else:
+            grads[-1] = before
+        before = (own + other.astype(F32)).astype(BF16)
+        grads.append(before)
+    grad_gate, grad_up, grad_down = (g[None] for g in grads)
     return (grad_tokens, grad_combine, grad_gate, grad_up, grad_down)
 
 

time: 176 us -> 168 us (0.955)
  other arithmetic: 9.72 us -> 5.17 us
  starting transfers between devices: 21.8 us -> 19.6 us
    broadcast_in_dim x2 -> x0, other arithmetic: 4.54 us -> none  [on_device(): (a + b.astype(F32)).astype(BF16)[None]]
    ppermute x21, starting transfers between devices: 21.8 us -> 19.6 us  [flip(): return lax.ppermute(x, 'expert', [(i, i ^ mask) for i in range(n)])]
    unnamed x41 -> x25, local copies, waits for them, and re-layouts: 4.23 us -> 3.73 us
where the time goes in v4:
time: 168 us; the launch traced here: 167 us
  waiting for transfers between devices  105 us (62%)
  matrix products  30.7 us (18%)
  starting transfers between devices  19.6 us (12%)
  local copies, waits for them, and re-layouts  5.36 us (3%)
  other arithmetic  5.17 us (3%)
    ppermute x21, waiting for transfers between devices, flip(): return lax.ppermute(x, 'expert', [(i, i ^ mask) for i in range(n)])  105 us
    dot_general x22, matrix products, dot(): lax.dot_general(a, b, (((ca,), (cb,)), ((), ())), preferred_element_type=...  30.7 us
    ppermute x21, starting transfers between devices, flip(): return lax.ppermute(x, 'expert', [(i, i ^ mask) for i in range(n)])  19.6 us
    unnamed x25, local copies, waits for them, and re-layouts  3.73 us
  transfers between devices with their start and end apart: 21, of which 12 were waited for; matrix products, arithmetic and copies ran while one was open for 21% of the time, Pallas kernels for 0%

profile of v4, /device:TPU:0, one launch (start us, length us, event | category | flops | bytes accessed | tf_op | source)
XLA Modules:
  0.0 167.2 jit_solution(6347384189124938838)
XLA Ops:
  0.7 0.8 xor_bitcast_fusion
  1.5 0.1 fusion.23
  1.7 0.7 bitcast_add_fusion
  2.4 1.1 constant_dynamic-update-slice_fusion.5
  3.5 3.0 %collective-permute-start.1 = (bf16[80,3584]{1,0:T(8,128)(2,1)S(1)}, bf16[80,3584]{1,0:T(8,128)(2,1)}, u32[]{:S(2)}, u32[]{:S(2)}) collective-permute-start(bf16[80,3584]{1,0:T(8,128)(2,1)S(1)} %get-tuple-element.68), channel_id=1, source_target_pairs={{0,4},{1,5},{2,6},{3,7},{4,0},{5,1},{6,2},{7,3},{8,12},{9,13},{10,... | collective-permute-start | bytes 1720328 | tf_op jit(solution)/shard_map/ppermute | solution.py:21
  6.5 1.1 convolution_convert_fusion.5
  7.6 2.6 %collective-permute-start = (bf16[80,3584]{1,0:T(8,128)(2,1)}, bf16[80,3584]{1,0:T(8,128)(2,1)}, u32[]{:S(2)}, u32[]{:S(2)}) collective-permute-start(bf16[80,3584]{1,0:T(8,128)(2,1)} %convolution_convert_fusion.5), channel_id=1, source_target_pairs={{0,8},{1,9},{2,10},{3,11},{4,12},{5,13},{6,14},{7,15},{8,0},{9,1},... | collective-permute-start | bytes 1720328 | tf_op jit(solution)/shard_map/ppermute | solution.py:21
  10.2 1.5 collective-permute-start.7
  11.7 0.5 collective-permute-start.8
  12.5 1.7 %convolution_convert_fusion.3 = bf16[80,3584]{1,0:T(8,128)(2,1)S(1)} fusion(bf16[128,3584]{1,0:T(8,128)(2,1)} %param.8, f32[128]{0:T(128)S(1)} %convert_reduce_fusion, pred[160,128]{1,0:T(8,128)(4,1)S(1)} %iota_compare_fusion), kind=kOutput, calls=%fused_computation.14 | convolution fusion | flops 75063296 | bytes 1501696 | tf_op jit(solution)/shard_map/dot_general | solution.py:16
  14.2 1.6 convolution_convert_fusion.4
  15.8 14.6 %collective-permute-done.1 = bf16[80,3584]{1,0:T(8,128)(2,1)} collective-permute-done((bf16[80,3584]{1,0:T(8,128)(2,1)S(1)}, bf16[80,3584]{1,0:T(8,128)(2,1)}, u32[]{:S(2)}, u32[]{:S(2)}) %collective-permute-start.1) | collective-permute-done | bytes 573472 | tf_op jit(solution)/shard_map/ppermute | solution.py:21
  30.4 5.2 %collective-permute-done = bf16[80,3584]{1,0:T(8,128)(2,1)} collective-permute-done((bf16[80,3584]{1,0:T(8,128)(2,1)}, bf16[80,3584]{1,0:T(8,128)(2,1)}, u32[]{:S(2)}, u32[]{:S(2)}) %collective-permute-start) | collective-permute-done | bytes 573472 | tf_op jit(solution)/shard_map/ppermute | solution.py:21
  35.6 3.0 %collective-permute-start.3 = (bf16[80,3584]{1,0:T(8,128)(2,1)}, bf16[80,3584]{1,0:T(8,128)(2,1)S(1)}, u32[]{:S(2)}, u32[]{:S(2)}) collective-permute-start(bf16[80,3584]{1,0:T(8,128)(2,1)} %collective-permute-done), channel_id=1, source_target_pairs={{0,4},{1,5},{2,6},{3,7},{4,0},{5,1},{6,2},{7,3},{8,12},{9,13},{10,... | collective-permute-start | bytes 1720328 | tf_op jit(solution)/shard_map/ppermute | solution.py:21
  38.7 1.1 pad_maximum_fusion.8
  39.9 1.6 collective-permute-start.5
  41.4 11.7 %collective-permute-done.8 = bf16[3584,128]{1,0:T(8,128)(2,1)S(1)} collective-permute-done((bf16[3584,128]{1,0:T(8,128)(2,1)S(1)}, bf16[3584,128]{1,0:T(8,128)(2,1)S(1)}, u32[]{:S(2)}, u32[]{:S(2)}) %collective-permute-start.8) | collective-permute-done | bytes 917536 | tf_op jit(solution)/shard_map/ppermute | solution.py:21
  53.2 9.1 %collective-permute-done.6 = bf16[80,3584]{1,0:T(8,128)(2,1)S(1)} collective-permute-done((bf16[80,3584]{1,0:T(8,128)(2,1)S(1)}, bf16[80,3584]{1,0:T(8,128)(2,1)S(1)}, u32[]{:S(2)}, u32[]{:S(2)}) %collective-permute-start.6) | collective-permute-done | bytes 573472 | tf_op jit(solution)/shard_map/ppermute | solution.py:21
  62.3 1.1 constant_dynamic-update-slice_fusion.4
  63.4 1.1 pad_maximum_fusion.9
  64.7 6.4 %collective-permute-done.5 = bf16[128,3584]{1,0:T(8,128)(2,1)S(1)} collective-permute-done((bf16[128,3584]{1,0:T(8,128)(2,1)}, bf16[128,3584]{1,0:T(8,128)(2,1)S(1)}, u32[]{:S(2)}, u32[]{:S(2)}) %collective-permute-start.5) | collective-permute-done | bytes 917536 | tf_op jit(solution)/shard_map/ppermute | solution.py:21
  71.1 6.1 %collective-permute-done.9 = bf16[80,3584]{1,0:T(8,128)(2,1)S(1)} collective-permute-done((bf16[80,3584]{1,0:T(8,128)(2,1)S(1)}, bf16[80,3584]{1,0:T(8,128)(2,1)S(1)}, u32[]{:S(2)}, u32[]{:S(2)}) %collective-permute-start.9) | collective-permute-done | bytes 573472 | tf_op jit(solution)/shard_map/ppermute | solution.py:21
  77.3 0.3 collective-permute-start.11
  77.8 1.1 constant_dynamic-update-slice_fusion.8
  79.0 2.1 %fusion.24 = f32[320,256]{1,0:T(8,128)S(1)} fusion(bf16[160,3584]{1,0:T(8,128)(2,1)S(1)} %collective-permute-done.2, bf16[80,3584]{1,0:T(8,128)(2,1)} %collective-permute-done.1, bf16[80,3584]{1,0:T(8,128)(2,1)S(1)} %get-tuple-element.68, bf16[3584,128]{1,0:T(8,128)(2,1)} %collective-permute-done.7, bf16[3584,128]{1,0:T(8,128)(2,1)S(1)} %bitcast.31), kind=kOutput, calls=%fused_computation.55 | convolution fusion | flops 597753856 | bytes 4456448 | tf_op jit(solution)/shard_map/dot_general | solution.py:16
  81.1 0.2 constant_dynamic-update-slice_fusion.6
  81.3 0.8 fusion.57
  82.1 0.4 copy-done.6
  82.4 0.8 fusion.6
  83.2 2.2 %multiply_convert_fusion.6 = (bf16[320,256]{1,0:T(8,128)(2,1)S(1)}, bf16[320]{0:T(512)(128)(2,1)S(1)}, bf16[320,256]{1,0:T(8,128)(2,1)S(1)}, bf16[320,256]{1,0:T(8,128)(2,1)S(1)}) fusion(f32[320,256]{1,0:T(8,128)S(1)} %fusion.6, f32[320,256]{1,0:T(8,128)S(1)} %fusion.57, bf16[320,3584]{1,0:T(8,128)(2,1)S(1)} %get-tuple-element.53, ...), kind=kOutput, calls=%fused_computation.70 | convolution fusion | flops 592264896 | bytes 5276288 | tf_op jit(solution)/shard_map/dot_general | solution.py:16
  85.4 2.0 %fusion.55 = f32[320,3584]{1,0:T(8,128)S(1)} fusion(bf16[320,256]{1,0:T(8,128)(2,1)S(1)} %get-tuple-element.57, bf16[3584,128]{1,0:T(8,128)(2,1)} %collective-permute-done.7, bf16[3584,128]{1,0:T(8,128)(2,1)S(1)} %bitcast.33), kind=kOutput, calls=%fused_computation.124 | convolution fusion | flops 590872576 | bytes 6586368 | tf_op jit(solution)/shard_map/dot_general | solution.py:16
  87.4 0.8 fusion
  88.3 0.2 pad_maximum_fusion
  88.5 4.2 %collective-permute-done.11 = bf16[80,3584]{1,0:T(8,128)(2,1)S(1)} collective-permute-done((bf16[80,3584]{1,0:T(8,128)(2,1)S(1)}, bf16[80,3584]{1,0:T(8,128)(2,1)S(1)}, u32[]{:S(2)}, u32[]{:S(2)}) %collective-permute-start.11) | collective-permute-done | bytes 573472 | tf_op jit(solution)/shard_map/ppermute | solution.py:21
  92.9 1.8 %fusion.25 = f32[320,256]{1,0:T(8,128)S(1)} fusion(bf16[160,3584]{1,0:T(8,128)(2,1)S(1)} %collective-permute-done.2, bf16[80,3584]{1,0:T(8,128)(2,1)} %collective-permute-done.1, bf16[80,3584]{1,0:T(8,128)(2,1)S(1)} %get-tuple-element.68, bf16[3584,128]{1,0:T(8,128)(2,1)S(1)} %collective-permute-done.8, bf16[3584,128]{1,0:T(8,128)(2,1)S(1)} %bitcast.28), kind=kOutput, calls=%fused_computation.56 | convolution fusion | flops 597753856 | bytes 4456448 | tf_op jit(solution)/shard_map/dot_general | solution.py:16
  94.8 0.6 collective-permute-start.16
  95.4 0.2 collective-permute-done.12
  95.7 0.9 multiply_reduce_fusion
  96.6 2.0 %fusion.54 = f32[320,3584]{1,0:T(8,128)S(1)} fusion(bf16[320,256]{1,0:T(8,128)(2,1)S(1)} %get-tuple-element.56, bf16[3584,128]{1,0:T(8,128)(2,1)} %collective-permute-done.7, bf16[3584,128]{1,0:T(8,128)(2,1)S(1)} %bitcast.34), kind=kOutput, calls=%fused_computation.123 | convolution fusion | flops 590872576 | bytes 6586368 | tf_op jit(solution)/shard_map/dot_general | solution.py:16
  98.6 1.4 convolution_convert_fusion.2
  100.0 1.4 convolution_convert_fusion.1
  101.4 1.0 fusion.1
  102.6 0.2 collective-permute-start.14
  102.8 1.5 collective-permute-start.13
  104.3 0.5 collective-permute-start.19
  105.1 0.9 convolution_convert_fusion
  106.0 1.5 collective-permute-start.20
  107.5 0.3 add_convert_fusion
  107.9 0.4 collective-permute-start.17
  108.2 0.3 add_convert_fusion.1
  108.6 1.8 %collective-permute-start.15 = (bf16[80,3712]{1,0:T(8,128)(2,1)S(1)}, bf16[80,3712]{1,0:T(8,128)(2,1)S(1)}, u32[]{:S(2)}, u32[]{:S(2)}) collective-permute-start(bf16[80,3712]{1,0:T(8,128)(2,1)S(1)} %slice.82), channel_id=1, source_target_pairs={{0,4},{1,5},{2,6},{3,7},{4,0},{5,1},{6,2},{7,3},{8,12},{9,13},{10,... | collective-permute-start | bytes 1781768 | tf_op jit(solution)/shard_map/ppermute | solution.py:21
  110.4 13.9 %collective-permute-done.17 = bf16[80,3712]{1,0:T(8,128)(2,1)S(1)} collective-permute-done((bf16[80,3712]{1,0:T(8,128)(2,1)S(1)}, bf16[80,3712]{1,0:T(8,128)(2,1)S(1)}, u32[]{:S(2)}, u32[]{:S(2)}) %collective-permute-start.17) | collective-permute-done | bytes 593952 | tf_op jit(solution)/shard_map/ppermute | solution.py:21
  124.3 0.1 add_convert_fusion.2
  124.4 0.3 collective-permute-start.18
  124.7 20.9 %collective-permute-done.15 = bf16[80,3712]{1,0:T(8,128)(2,1)S(1)} collective-permute-done((bf16[80,3712]{1,0:T(8,128)(2,1)S(1)}, bf16[80,3712]{1,0:T(8,128)(2,1)S(1)}, u32[]{:S(2)}, u32[]{:S(2)}) %collective-permute-start.15) | collective-permute-done | bytes 593952 | tf_op jit(solution)/shard_map/ppermute | solution.py:21
  145.6 0.1 add_convert_fusion.3
  145.8 4.8 %collective-permute-done.18 = bf16[80,3712]{1,0:T(8,128)(2,1)S(1)} collective-permute-done((bf16[80,3712]{1,0:T(8,128)(2,1)S(1)}, bf16[80,3712]{1,0:T(8,128)(2,1)S(1)}, u32[]{:S(2)}, u32[]{:S(2)}) %collective-permute-start.18) | collective-permute-done | bytes 593952 | tf_op jit(solution)/shard_map/ppermute | solution.py:21
  150.6 0.5 fusion.19
  151.1 1.0 slice.136
  152.1 2.3 %fusion.2 = bf16[3584,128]{1,0:T(8,128)(2,1)} fusion(bf16[640,3584]{1,0:T(8,128)(2,1)S(1)} %get-tuple-element.54, bf16[3584,128]{1,0:T(8,128)(2,1)S(1)} %collective-permute-done.13, bf16[320,256]{1,0:T(8,128)(2,1)S(1)} %get-tuple-element.57, bf16[320,256]{1,0:T(8,128)(2,1)S(1)} %get-tuple-element.56), kind=kOutput, calls=%fused_computation.7 | convolution fusion | flops 588906496 | bytes 6750208 | tf_op jit(solution)/shard_map/dot_general | solution.py:16
  154.4 2.3 %fusion.3 = bf16[3584,128]{1,0:T(8,128)(2,1)} fusion(bf16[640,3584]{1,0:T(8,128)(2,1)S(1)} %get-tuple-element.54, bf16[3584,128]{1,0:T(8,128)(2,1)S(1)} %collective-permute-done.19, bf16[320,256]{1,0:T(8,128)(2,1)S(1)} %get-tuple-element.60, bf16[320,256]{1,0:T(8,128)(2,1)S(1)} %get-tuple-element.62), kind=kOutput, calls=%fused_computation.8 | convolution fusion | flops 588906496 | bytes 6750208 | tf_op jit(solution)/shard_map/dot_general | solution.py:16
  156.8 8.0 %collective-permute-done.20 = bf16[128,3584]{1,0:T(8,128)(2,1)S(1)} collective-permute-done((bf16[128,3584]{1,0:T(8,128)(2,1)S(1)}, bf16[128,3584]{1,0:T(8,128)(2,1)S(1)}, u32[]{:S(2)}, u32[]{:S(2)}) %collective-permute-start.20) | collective-permute-done | bytes 917536 | tf_op jit(solution)/shard_map/ppermute | solution.py:21
  164.7 1.8 %fusion.5 = bf16[1,128,3584]{2,1,0:T(8,128)(2,1)} fusion(bf16[640,3584]{1,0:T(8,128)(2,1)S(1)} %constant_dynamic-update-slice_fusion.9, bf16[128,3584]{1,0:T(8,128)(2,1)S(1)} %collective-permute-done.20, bf16[320,256]{1,0:T(8,128)(2,1)S(1)} %get-tuple-element.59, bf16[320,256]{1,0:T(8,128)(2,1)S(1)} %get-tuple-element.61), kind=kOutput, calls=%fused_computation.13 | convolution fusion | flops 588906496 | bytes 6750208 | tf_op jit(solution)/shard_map/dot_general | solution.py:16
  166.6 0.6 copy.15
  (48 shorter events, 1.7 us)
Async XLA Ops:
  0.6 1.7 %copy-start = (bf16[128,3584]{1,0:T(8,128)(2,1)S(1)}, bf16[128,3584]{1,0:T(8,128)(2,1)}, u32[]{:S(2)}) copy-start(bf16[128,3584]{1,0:T(8,128)(2,1)} %param.7) | copy-start | bytes 2752516
  0.6 9.6 %copy-start.4 = (bf16[1,3584,128]{2,1,0:T(8,128)(2,1)S(1)}, bf16[1,3584,128]{2,1,0:T(8,128)(2,1)}, u32[]{:S(2)}) copy-start(bf16[1,3584,128]{2,1,0:T(8,128)(2,1)} %param.11) | copy-start | bytes 2752516
  0.7 11.1 %copy-start.3 = (bf16[1,3584,128]{2,1,0:T(8,128)(2,1)S(1)}, bf16[1,3584,128]{2,1,0:T(8,128)(2,1)}, u32[]{:S(2)}) copy-start(bf16[1,3584,128]{2,1,0:T(8,128)(2,1)} %param.12) | copy-start | bytes 2752516
  0.7 11.6 %copy-start.5 = (bf16[128,1]{0,1:T(2,128)(2,1)S(1)}, bf16[128,1]{0,1:T(2,128)(2,1)}, u32[]{:S(2)}) copy-start(bf16[128,1]{0,1:T(2,128)(2,1)} %param.9) | copy-start | bytes 772
  3.5 26.9 %collective-permute-start.1 = (bf16[80,3584]{1,0:T(8,128)(2,1)S(1)}, bf16[80,3584]{1,0:T(8,128)(2,1)}, u32[]{:S(2)}, u32[]{:S(2)}) collective-permute-start(bf16[80,3584]{1,0:T(8,128)(2,1)S(1)} %get-tuple-element.68), channel_id=1, source_target_pairs={{0,4},{1,5},{2,6},{3,7},{4,0},{5,1},{6,2},{7,3},{8,12},{9,13},{10,... | collective-permute-start | bytes 1720328 | tf_op jit(solution)/shard_map/ppermute | solution.py:21
  7.6 28.0 %collective-permute-start = (bf16[80,3584]{1,0:T(8,128)(2,1)}, bf16[80,3584]{1,0:T(8,128)(2,1)}, u32[]{:S(2)}, u32[]{:S(2)}) collective-permute-start(bf16[80,3584]{1,0:T(8,128)(2,1)} %convolution_convert_fusion.5), channel_id=1, source_target_pairs={{0,8},{1,9},{2,10},{3,11},{4,12},{5,13},{6,14},{7,15},{8,0},{9,1},... | collective-permute-start | bytes 1720328 | tf_op jit(solution)/shard_map/ppermute | solution.py:21
  10.2 29.7 %collective-permute-start.7 = (bf16[3584,128]{1,0:T(8,128)(2,1)S(1)}, bf16[3584,128]{1,0:T(8,128)(2,1)}, u32[]{:S(2)}, u32[]{:S(2)}) collective-permute-start(bf16[3584,128]{1,0:T(8,128)(2,1)S(1)} %bitcast.30), channel_id=1, source_target_pairs={{0,2},{1,3},{2,0},{3,1},{4,6},{5,7},{6,4},{7,5},{8,10},{9,11},{10,... | collective-permute-start | bytes 2752520 | tf_op jit(solution)/shard_map/ppermute | solution.py:21
  11.7 41.5 %collective-permute-start.8 = (bf16[3584,128]{1,0:T(8,128)(2,1)S(1)}, bf16[3584,128]{1,0:T(8,128)(2,1)S(1)}, u32[]{:S(2)}, u32[]{:S(2)}) collective-permute-start(bf16[3584,128]{1,0:T(8,128)(2,1)S(1)} %bitcast.25), channel_id=1, source_target_pairs={{0,2},{1,3},{2,0},{3,1},{4,6},{5,7},{6,4},{7,5},{8,10},{9,11},{10,... | collective-permute-start | bytes 2752520 | tf_op jit(solution)/shard_map/ppermute | solution.py:21
  12.5 49.8 %copy-start.2 = (bf16[640,3584]{1,0:T(8,128)(2,1)S(1)}, bf16[640,3584]{1,0:T(8,128)(2,1)}, u32[]{:S(2)}) copy-start(bf16[640,3584]{1,0:T(8,128)(2,1)} %get-tuple-element.67) | copy-start | bytes 13762564
  35.6 26.7 %collective-permute-start.6 = (bf16[80,3584]{1,0:T(8,128)(2,1)S(1)}, bf16[80,3584]{1,0:T(8,128)(2,1)S(1)}, u32[]{:S(2)}, u32[]{:S(2)}) collective-permute-start(bf16[80,3584]{1,0:T(8,128)(2,1)S(1)} %convolution_convert_fusion.3), channel_id=1, source_target_pairs={{0,8},{1,9},{2,10},{3,11},{4,12},{5,13},{6,14},{7,15},{8,0},{9,1},... | collective-permute-start | bytes 1720328 | tf_op jit(solution)/shard_map/ppermute | solution.py:21
  35.6 27.8 %collective-permute-start.3 = (bf16[80,3584]{1,0:T(8,128)(2,1)}, bf16[80,3584]{1,0:T(8,128)(2,1)S(1)}, u32[]{:S(2)}, u32[]{:S(2)}) collective-permute-start(bf16[80,3584]{1,0:T(8,128)(2,1)} %collective-permute-done), channel_id=1, source_target_pairs={{0,4},{1,5},{2,6},{3,7},{4,0},{5,1},{6,2},{7,3},{8,12},{9,13},{10,... | collective-permute-start | bytes 1720328 | tf_op jit(solution)/shard_map/ppermute | solution.py:21
  39.8 37.9 %collective-permute-start.2 = (bf16[160,3584]{1,0:T(8,128)(2,1)S(1)}, bf16[160,3584]{1,0:T(8,128)(2,1)S(1)}, u32[]{:S(2)}, u32[]{:S(2)}) collective-permute-start(bf16[160,3584]{1,0:T(8,128)(2,1)S(1)} %pad_maximum_fusion.8), channel_id=1, source_target_pairs={{0,1},{1,0},{2,3},{3,2},{4,5},{5,4},{6,7},{7,6},{8,9},{9,8},{10,11... | collective-permute-start | bytes 3440648 | tf_op jit(solution)/shard_map/ppermute | solution.py:21
  39.9 31.2 %collective-permute-start.5 = (bf16[128,3584]{1,0:T(8,128)(2,1)}, bf16[128,3584]{1,0:T(8,128)(2,1)S(1)}, u32[]{:S(2)}, u32[]{:S(2)}) collective-permute-start(bf16[128,3584]{1,0:T(8,128)(2,1)} %bitcast.37), channel_id=1, source_target_pairs={{0,2},{1,3},{2,0},{3,1},{4,6},{5,7},{6,4},{7,5},{8,10},{9,11},{10,... | collective-permute-start | bytes 2752520 | tf_op jit(solution)/shard_map/ppermute | solution.py:21
  62.3 14.8 %collective-permute-start.9 = (bf16[80,3584]{1,0:T(8,128)(2,1)S(1)}, bf16[80,3584]{1,0:T(8,128)(2,1)S(1)}, u32[]{:S(2)}, u32[]{:S(2)}) collective-permute-start(bf16[80,3584]{1,0:T(8,128)(2,1)S(1)} %collective-permute-done.6), channel_id=1, source_target_pairs={{0,4},{1,5},{2,6},{3,7},{4,0},{5,1},{6,2},{7,3},{8,12},{9,13},{10,... | collective-permute-start | bytes 1720328 | tf_op jit(solution)/shard_map/ppermute | solution.py:21
  64.6 16.5 %collective-permute-start.4 = (bf16[160,3584]{1,0:T(8,128)(2,1)S(1)}, bf16[160,3584]{1,0:T(8,128)(2,1)S(1)}, u32[]{:S(2)}, u32[]{:S(2)}) collective-permute-start(bf16[160,3584]{1,0:T(8,128)(2,1)S(1)} %pad_maximum_fusion.9), channel_id=1, source_target_pairs={{0,1},{1,0},{2,3},{3,2},{4,5},{5,4},{6,7},{7,6},{8,9},{9,8},{10,11... | collective-permute-start | bytes 3440648 | tf_op jit(solution)/shard_map/ppermute | solution.py:21
  77.2 4.8 %collective-permute-start.10 = (bf16[160,3584]{1,0:T(8,128)(2,1)S(1)}, bf16[160,3584]{1,0:T(8,128)(2,1)S(1)}, u32[]{:S(2)}, u32[]{:S(2)}) collective-permute-start(bf16[160,3584]{1,0:T(8,128)(2,1)S(1)} %pad_maximum_fusion.10), channel_id=1, source_target_pairs={{0,1},{1,0},{2,3},{3,2},{4,5},{5,4},{6,7},{7,6},{8,9},{9,8},{10,11... | collective-permute-start | bytes 3440648 | tf_op jit(solution)/shard_map/ppermute | solution.py:21
  77.3 15.4 %collective-permute-start.11 = (bf16[80,3584]{1,0:T(8,128)(2,1)S(1)}, bf16[80,3584]{1,0:T(8,128)(2,1)S(1)}, u32[]{:S(2)}, u32[]{:S(2)}) collective-permute-start(bf16[80,3584]{1,0:T(8,128)(2,1)S(1)} %convolution_convert_fusion.4), channel_id=1, source_target_pairs={{0,4},{1,5},{2,6},{3,7},{4,0},{5,1},{6,2},{7,3},{8,12},{9,13},{10,... | collective-permute-start | bytes 1720328 | tf_op jit(solution)/shard_map/ppermute | solution.py:21
  81.3 1.2 copy-start.6
  92.8 2.9 %collective-permute-start.12 = (bf16[160,3584]{1,0:T(8,128)(2,1)S(1)}, bf16[160,3584]{1,0:T(8,128)(2,1)S(1)}, u32[]{:S(2)}, u32[]{:S(2)}) collective-permute-start(bf16[160,3584]{1,0:T(8,128)(2,1)S(1)} %pad_maximum_fusion.11), channel_id=1, source_target_pairs={{0,1},{1,0},{2,3},{3,2},{4,5},{5,4},{6,7},{7,6},{8,9},{9,8},{10,11... | collective-permute-start | bytes 3440648 | tf_op jit(solution)/shard_map/ppermute | solution.py:21
  94.8 12.7 %collective-permute-start.16 = (bf16[160,3712]{1,0:T(8,128)(2,1)S(1)}, bf16[160,3712]{1,0:T(8,128)(2,1)S(1)}, u32[]{:S(2)}, u32[]{:S(2)}) collective-permute-start(bf16[160,3712]{1,0:T(8,128)(2,1)S(1)} %slice.65), channel_id=1, source_target_pairs={{0,1},{1,0},{2,3},{3,2},{4,5},{5,4},{6,7},{7,6},{8,9},{9,8},{10,11... | collective-permute-start | bytes 3563528 | tf_op jit(solution)/shard_map/ppermute | solution.py:21
  102.6 5.6 %collective-permute-start.14 = (bf16[160,3712]{1,0:T(8,128)(2,1)S(1)}, bf16[160,3712]{1,0:T(8,128)(2,1)S(1)}, u32[]{:S(2)}, u32[]{:S(2)}) collective-permute-start(bf16[160,3712]{1,0:T(8,128)(2,1)S(1)} %pad_maximum_fusion.5), channel_id=1, source_target_pairs={{0,1},{1,0},{2,3},{3,2},{4,5},{5,4},{6,7},{7,6},{8,9},{9,8},{10,11... | collective-permute-start | bytes 3563528 | tf_op jit(solution)/shard_map/ppermute | solution.py:21
  102.8 49.3 %collective-permute-start.13 = (bf16[3584,128]{1,0:T(8,128)(2,1)S(1)}, bf16[3584,128]{1,0:T(8,128)(2,1)S(1)}, u32[]{:S(2)}, u32[]{:S(2)}) collective-permute-start(bf16[3584,128]{1,0:T(8,128)(2,1)S(1)} %convolution_convert_fusion.2), channel_id=1, source_target_pairs={{0,2},{1,3},{2,0},{3,1},{4,6},{5,7},{6,4},{7,5},{8,10},{9,11},{10,... | collective-permute-start | bytes 2752520 | tf_op jit(solution)/shard_map/ppermute | solution.py:21
  104.3 50.1 %collective-permute-start.19 = (bf16[3584,128]{1,0:T(8,128)(2,1)S(1)}, bf16[3584,128]{1,0:T(8,128)(2,1)S(1)}, u32[]{:S(2)}, u32[]{:S(2)}) collective-permute-start(bf16[3584,128]{1,0:T(8,128)(2,1)S(1)} %convolution_convert_fusion.1), channel_id=1, source_target_pairs={{0,2},{1,3},{2,0},{3,1},{4,6},{5,7},{6,4},{7,5},{8,10},{9,11},{10,... | collective-permute-start | bytes 2752520 | tf_op jit(solution)/shard_map/ppermute | solution.py:21
  106.0 58.7 %collective-permute-start.20 = (bf16[128,3584]{1,0:T(8,128)(2,1)S(1)}, bf16[128,3584]{1,0:T(8,128)(2,1)S(1)}, u32[]{:S(2)}, u32[]{:S(2)}) collective-permute-start(bf16[128,3584]{1,0:T(8,128)(2,1)S(1)} %convolution_convert_fusion), channel_id=1, source_target_pairs={{0,2},{1,3},{2,0},{3,1},{4,6},{5,7},{6,4},{7,5},{8,10},{9,11},{10,... | collective-permute-start | bytes 2752520 | tf_op jit(solution)/shard_map/ppermute | solution.py:21
  107.9 16.4 %collective-permute-start.17 = (bf16[80,3712]{1,0:T(8,128)(2,1)S(1)}, bf16[80,3712]{1,0:T(8,128)(2,1)S(1)}, u32[]{:S(2)}, u32[]{:S(2)}) collective-permute-start(bf16[80,3712]{1,0:T(8,128)(2,1)S(1)} %slice.84), channel_id=1, source_target_pairs={{0,4},{1,5},{2,6},{3,7},{4,0},{5,1},{6,2},{7,3},{8,12},{9,13},{10,... | collective-permute-start | bytes 1781768 | tf_op jit(solution)/shard_map/ppermute | solution.py:21
  108.6 37.0 %collective-permute-start.15 = (bf16[80,3712]{1,0:T(8,128)(2,1)S(1)}, bf16[80,3712]{1,0:T(8,128)(2,1)S(1)}, u32[]{:S(2)}, u32[]{:S(2)}) collective-permute-start(bf16[80,3712]{1,0:T(8,128)(2,1)S(1)} %slice.82), channel_id=1, source_target_pairs={{0,4},{1,5},{2,6},{3,7},{4,0},{5,1},{6,2},{7,3},{8,12},{9,13},{10,... | collective-permute-start | bytes 1781768 | tf_op jit(solution)/shard_map/ppermute | solution.py:21
  124.4 26.2 %collective-permute-start.18 = (bf16[80,3712]{1,0:T(8,128)(2,1)S(1)}, bf16[80,3712]{1,0:T(8,128)(2,1)S(1)}, u32[]{:S(2)}, u32[]{:S(2)}) collective-permute-start(bf16[80,3712]{1,0:T(8,128)(2,1)S(1)} %add_convert_fusion.2), channel_id=1, source_target_pairs={{0,8},{1,9},{2,10},{3,11},{4,12},{5,13},{6,14},{7,15},{8,0},{9,1},... | collective-permute-start | bytes 1781768 | tf_op jit(solution)/shard_map/ppermute | solution.py:21
  154.4 12.7 %copy-start.1 = (bf16[128,3584]{1,0:T(8,128)(2,1)S(1)}, bf16[128,3584]{1,0:T(8,128)(2,1)}, u32[]{:S(2)}) copy-start(bf16[128,3584]{1,0:T(8,128)(2,1)} %param.7) | copy-start | bytes 2752516

commit v5 on v3

--- a/solution.py
+++ b/solution.py
@@ -7,6 +7,7 @@
 CORE = 1
 WEIGHT_BIT = 2
 ROW_BIT = 4
+SHARED_PART = 3
 
 F32 = jnp.float32
 BF16 = jnp.bfloat16
@@ -29,8 +30,7 @@
     return lax.optimization_barrier((x,) + others)[0]
 
 
-def share_core(a, b):
-    pair = jnp.concatenate([a, b], axis=0)
+def share_core(pair):
     return jnp.concatenate([pair, flip(pair, CORE)], axis=0)
 
 
@@ -46,6 +46,7 @@
     experts = axis_count // SPLIT
     tok_rows, features = tokens.shape
     hid = w_gate.shape[2]
+    shared = features * SHARED_PART // 7 // 128 * 128
     capacity = min(tok_rows, 5 * tok_rows // (4 * experts))
     capacity = -(-capacity // 16) * 16
     mine = lax.axis_index("expert") // SPLIT
@@ -76,20 +77,27 @@
 
     far_x = dispatch(far_x)
     near_x2 = flip(near_x, ROW_BIT)
-    far_x, near_x2, near_u, down_send, *far_u = lax.optimization_barrier(
-        (far_x, near_x2, near_u, down, *far_u)
+    far_x, near_x2, near_u, gate_b, *far_u = lax.optimization_barrier(
+        (far_x, near_x2, near_u, gate_b, *far_u)
     )
+    up_b, down_send = lax.optimization_barrier((up_b, down))
     far_u = dispatch(far_u)
     far_x2 = flip(far_x, ROW_BIT)
     down_b = flip(down_send, WEIGHT_BIT)
-    far_u, gate_b, up_b = lax.optimization_barrier((far_u, gate_b, up_b))
+    near_x = jnp.concatenate([near_x, near_x2], axis=0)
+    far_x2, near_p = lax.optimization_barrier((far_x2, near_x[:, :shared]))
+    near_p = flip(near_p, WEIGHT_BIT)
     far_u2 = flip(far_u, ROW_BIT)
-    near_u, down_b, far_u2 = lax.optimization_barrier((near_u, down_b, far_u2))
+    far_x = jnp.concatenate([far_x, far_x2], axis=0)
+    near_u, down_b, far_u2, near_p, far_p = lax.optimization_barrier(
+        (near_u, down_b, far_u2, near_p, far_x[:, :shared])
+    )
+    far_p = flip(far_p, WEIGHT_BIT)
     near_u2 = flip(near_u, ROW_BIT)
 
-    far_x = share_core(far_x, far_x2)
-    far_u = share_core(far_u, far_u2)
-    near_x = share_core(near_x, near_x2)
+    far_x = share_core(far_x)
+    far_u = share_core(jnp.concatenate([far_u, far_u2], axis=0))
+    near_x = share_core(near_x)
 
     gate = jnp.concatenate([gate, gate_b], axis=1)
     up = jnp.concatenate([up, up_b], axis=1)
@@ -112,8 +120,8 @@
         return jnp.concatenate([rows, jnp.broadcast_to(prob, (rows.shape[0], 128))], axis=1)
 
     far = hidden_pass(far_x, far_u)
-    far_rows, near_u2 = lax.optimization_barrier((rows_pass(*far[1:]), near_u2))
-    near_u = share_core(near_u, near_u2)
+    far_rows, near_u2, far_p = lax.optimization_barrier((rows_pass(*far[1:]), near_u2, far_p))
+    near_u = share_core(jnp.concatenate([near_u, near_u2], axis=0))
     far_rows = sum_rows(far_rows)
     back = [
         flip(far_rows[(k - 1) * capacity : k * capacity], SPLIT * k) for k in range(1, experts)
@@ -126,21 +134,35 @@
     hidden, grad_gpre, grad_upre = (
         jnp.concatenate([a, b], axis=0) for a, b in zip(near[:3], far[:3])
     )
-    def weight_grads(at):
-        return (
-            dot(x, grad_gpre[:, at], 0, 0), dot(x, grad_upre[:, at], 0, 0), dot(hidden[:, at], u, 0, 0)
-        )
+    both = jnp.concatenate([grad_gpre[:, :hid], grad_upre[:, :hid]], axis=1)
+    both_p = jnp.concatenate([grad_gpre[:, hid:], grad_upre[:, hid:]], axis=1)
+    got_both = flip(both_p, WEIGHT_BIT)
+    rest_p = dot(x[:, shared:], both_p, 0, 0).astype(BF16)
+    down_p = dot(hidden[:, hid:], u, 0, 0).astype(BF16)
+    x_p = jnp.concatenate([near_p, far_p], axis=0)
+    rest_p, down_p, x_p = lax.optimization_barrier((rest_p, down_p, x_p))
+    x_p_core = flip(x_p, CORE)
+    at = x_p.shape[0] // 2
+    x_p = jnp.concatenate([x_p[:at], x_p_core[:at], x_p[at:], x_p_core[at:]], axis=0)
+    got_rest = flip(rest_p, WEIGHT_BIT)
+    got_down = flip(down_p, WEIGHT_BIT)
 
-    got = [flip(g.astype(BF16), WEIGHT_BIT) for g in weight_grads(slice(hid, None))]
-    kept = lax.optimization_barrier(weight_grads(slice(0, hid)))
-    near_rows, back, got, kept = lax.optimization_barrier((near_rows, back, got, kept))
-    grad_gate, grad_up, grad_down = (
-        (a + b.astype(F32)).astype(BF16)[None] for a, b in zip(kept, got)
-    )
     slot_rows = jnp.concatenate([near_rows] + back, axis=0)
     out = dot(select, slot_rows, 0, 0)
     grad_tokens = out[:, :features].astype(BF16)
     grad_combine = out[:, features : features + 1] / weight
+
+    first = (dot(x[:, :shared], both, 0, 0) + dot(x_p, got_both, 0, 0)).astype(BF16)
+    got_rest, first, grad_tokens = lax.optimization_barrier((got_rest, first, grad_tokens))
+    rest = (dot(x[:, shared:], both, 0, 0) + got_rest.astype(F32)).astype(BF16)
+    grad_gate, grad_up = (
+        jnp.concatenate([first[:, at], rest[:, at]], axis=0)[None]
+        for at in (slice(0, hid), slice(hid, None))
+    )
+    got_down, grad_gate, grad_up, grad_combine = lax.optimization_barrier(
+        (got_down, grad_gate, grad_up, grad_combine)
+    )
+    grad_down = (dot(hidden[:, :hid], u, 0, 0) + got_down.astype(F32)).astype(BF16)[None]
     return (grad_tokens, grad_combine, grad_gate, grad_up, grad_down)
 
 

time: 176 us -> 155 us (0.88)
  matrix products: 31.5 us -> 21.3 us
  waiting for transfers between devices: 106 us -> 99 us
  other arithmetic: 9.72 us -> 5.01 us
  starting transfers between devices: 21.8 us -> 24 us
    dot_general x22, matrix products: 31.5 us -> 21.3 us  [dot(): lax.dot_general(a, b, (((ca,), (cb,)), ((), ())), preferred_element_type=...]
    ppermute x21 -> x24, waiting for transfers between devices: 106 us -> 99 us  [flip(): return lax.ppermute(x, 'expert', [(i, i ^ mask) for i in range(n)])]
    broadcast_in_dim x2, other arithmetic: 4.54 us -> 1.96 us  [on_device(): jnp.concatenate([first[:, at], rest[:, at]], axis=0)[None]]
    ppermute x21 -> x24, starting transfers between devices: 21.8 us -> 24 us  [flip(): return lax.ppermute(x, 'expert', [(i, i ^ mask) for i in range(n)])]
    concatenate x4 -> x7, other arithmetic: 2.42 us -> 0.4 us  [the longest x2 0.11 us: on_device(): near_x = jnp.concatenate([near_x, near_x2], axis=0)]
    unnamed x41 -> x25, local copies, waits for them, and re-layouts: 4.23 us -> 2.73 us
  transfers between devices with their start and end apart: 21 -> 24, of which waited for: 12 -> 11; matrix products, arithmetic and copies ran while one was open for 21% -> 18% of each run, Pallas kernels for 0% -> 0%
where the time goes in v5:
time: 155 us
  waiting for transfers between devices  99 us (64%)
  starting transfers between devices  24 us (15%)
  matrix products  21.3 us (14%)
  other arithmetic  5.01 us (3%)
  local copies, waits for them, and re-layouts  4.67 us (3%)
    ppermute x24, waiting for transfers between devices, flip(): return lax.ppermute(x, 'expert', [(i, i ^ mask) for i in range(n)])  99 us
    ppermute x24, starting transfers between devices, flip(): return lax.ppermute(x, 'expert', [(i, i ^ mask) for i in range(n)])  24 us
    dot_general x22, matrix products, dot(): lax.dot_general(a, b, (((ca,), (cb,)), ((), ())), preferred_element_type=...  21.3 us
  transfers between devices with their start and end apart: 24, of which 11 were waited for; matrix products, arithmetic and copies ran while one was open for 18% of the time, Pallas kernels for 0%

profile of v5, /device:TPU:0, one launch (start us, length us, event | category | flops | bytes accessed | tf_op | source)
XLA Modules:
  0.0 155.1 jit_solution(14363800985222939877)
XLA Ops:
  0.7 3.0 %collective-permute-start.2 = (bf16[3584,128]{1,0:T(8,128)(2,1)}, bf16[3584,128]{1,0:T(8,128)(2,1)S(1)}, u32[]{:S(2)}, u32[]{:S(2)}) collective-permute-start(bf16[3584,128]{1,0:T(8,128)(2,1)} %bitcast.29), channel_id=1, source_target_pairs={{0,2},{1,3},{2,0},{3,1},{4,6},{5,7},{6,4},{7,5},{8,10},{9,11},{10,... | collective-permute-start | bytes 2752520 | tf_op jit(solution)/shard_map/ppermute | solution.py:22
  3.7 0.7 xor_bitcast_fusion
  4.3 0.1 fusion.34
  4.5 0.7 bitcast_add_fusion
  5.2 1.1 convolution_convert_fusion.3
  6.3 2.6 %collective-permute-start = (bf16[80,3584]{1,0:T(8,128)(2,1)}, bf16[80,3584]{1,0:T(8,128)(2,1)}, u32[]{:S(2)}, u32[]{:S(2)}) collective-permute-start(bf16[80,3584]{1,0:T(8,128)(2,1)} %convolution_convert_fusion.3), channel_id=1, source_target_pairs={{0,8},{1,9},{2,10},{3,11},{4,12},{5,13},{6,14},{7,15},{8,0},{9,1},... | collective-permute-start | bytes 1720328 | tf_op jit(solution)/shard_map/ppermute | solution.py:22
  8.9 0.5 collective-permute-start.6
  9.4 1.1 constant_dynamic-update-slice_fusion.7
  10.6 1.6 %collective-permute-start.1 = (bf16[80,3584]{1,0:T(8,128)(2,1)S(1)}, bf16[80,3584]{1,0:T(8,128)(2,1)S(1)}, u32[]{:S(2)}, u32[]{:S(2)}) collective-permute-start(bf16[80,3584]{1,0:T(8,128)(2,1)S(1)} %get-tuple-element.94), channel_id=1, source_target_pairs={{0,4},{1,5},{2,6},{3,7},{4,0},{5,1},{6,2},{7,3},{8,12},{9,13},{10,... | collective-permute-start | bytes 1720328 | tf_op jit(solution)/shard_map/ppermute | solution.py:22
  12.4 1.6 %convolution_convert_fusion.1 = bf16[80,3584]{1,0:T(8,128)(2,1)S(1)} fusion(bf16[128,3584]{1,0:T(8,128)(2,1)} %param.8, f32[128]{0:T(128)S(1)} %convert_reduce_fusion, pred[160,128]{1,0:T(8,128)(4,1)S(1)} %iota_compare_fusion.1), kind=kOutput, calls=%fused_computation.8 | convolution fusion | flops 75063296 | bytes 1501696 | tf_op jit(solution)/shard_map/dot_general | solution.py:17
  14.1 1.7 %convolution_convert_fusion.2 = bf16[80,3584]{1,0:T(8,128)(2,1)S(1)} fusion(bf16[128,3584]{1,0:T(8,128)(2,1)} %param.8, f32[128]{0:T(128)S(1)} %convert_reduce_fusion, pred[160,128]{1,0:T(8,128)(4,1)S(1)} %iota_compare_fusion.1), kind=kOutput, calls=%fused_computation.9 | convolution fusion | flops 75063296 | bytes 1501696 | tf_op jit(solution)/shard_map/dot_general | solution.py:17
  15.8 18.6 %collective-permute-done = bf16[80,3584]{1,0:T(8,128)(2,1)} collective-permute-done((bf16[80,3584]{1,0:T(8,128)(2,1)}, bf16[80,3584]{1,0:T(8,128)(2,1)}, u32[]{:S(2)}, u32[]{:S(2)}) %collective-permute-start) | collective-permute-done | bytes 573472 | tf_op jit(solution)/shard_map/ppermute | solution.py:22
  34.4 1.3 collective-permute-done.1
  35.8 0.6 collective-permute-start.8
  36.4 2.4 %collective-permute-start.4 = (bf16[80,3584]{1,0:T(8,128)(2,1)}, bf16[80,3584]{1,0:T(8,128)(2,1)S(1)}, u32[]{:S(2)}, u32[]{:S(2)}) collective-permute-start(bf16[80,3584]{1,0:T(8,128)(2,1)} %collective-permute-done), channel_id=1, source_target_pairs={{0,4},{1,5},{2,6},{3,7},{4,0},{5,1},{6,2},{7,3},{8,12},{9,13},{10,... | collective-permute-start | bytes 1720328 | tf_op jit(solution)/shard_map/ppermute | solution.py:22
  38.9 5.0 %collective-permute-done.6 = bf16[3584,128]{1,0:T(8,128)(2,1)S(1)} collective-permute-done((bf16[3584,128]{1,0:T(8,128)(2,1)}, bf16[3584,128]{1,0:T(8,128)(2,1)S(1)}, u32[]{:S(2)}, u32[]{:S(2)}) %collective-permute-start.6) | collective-permute-done | bytes 917536 | tf_op jit(solution)/shard_map/ppermute | solution.py:22
  43.9 1.7 %collective-permute-start.7 = (bf16[128,3584]{1,0:T(8,128)(2,1)S(1)}, bf16[128,3584]{1,0:T(8,128)(2,1)S(1)}, u32[]{:S(2)}, u32[]{:S(2)}) collective-permute-start(bf16[128,3584]{1,0:T(8,128)(2,1)S(1)} %bitcast.34), channel_id=1, source_target_pairs={{0,2},{1,3},{2,0},{3,1},{4,6},{5,7},{6,4},{7,5},{8,10},{9,11},{10,... | collective-permute-start | bytes 2752520 | tf_op jit(solution)/shard_map/ppermute | solution.py:22
  45.7 18.9 %collective-permute-done.4 = bf16[80,3584]{1,0:T(8,128)(2,1)S(1)} collective-permute-done((bf16[80,3584]{1,0:T(8,128)(2,1)}, bf16[80,3584]{1,0:T(8,128)(2,1)S(1)}, u32[]{:S(2)}, u32[]{:S(2)}) %collective-permute-start.4) | collective-permute-done | bytes 573472 | tf_op jit(solution)/shard_map/ppermute | solution.py:22
  64.6 1.4 collective-permute-start.10
  66.1 1.2 constant_dynamic-update-slice_fusion.10
  67.6 8.3 %collective-permute-done.10 = bf16[160,1536]{1,0:T(8,128)(2,1)S(1)} collective-permute-done((bf16[160,1536]{1,0:T(8,128)(2,1)S(1)}, bf16[160,1536]{1,0:T(8,128)(2,1)S(1)}, u32[]{:S(2)}, u32[]{:S(2)}) %collective-permute-start.10) | collective-permute-done | bytes 491552 | tf_op jit(solution)/shard_map/ppermute | solution.py:22
  76.0 3.2 %collective-permute-done.9 = bf16[80,3584]{1,0:T(8,128)(2,1)S(1)} collective-permute-done((bf16[80,3584]{1,0:T(8,128)(2,1)S(1)}, bf16[80,3584]{1,0:T(8,128)(2,1)S(1)}, u32[]{:S(2)}, u32[]{:S(2)}) %collective-permute-start.9) | collective-permute-done | bytes 573472 | tf_op jit(solution)/shard_map/ppermute | solution.py:22
  79.1 1.4 collective-permute-start.13
  80.6 0.3 collective-permute-start.12
  81.0 0.8 fusion.35
  81.8 0.3 copy-done.2
  82.1 0.8 fusion.36
  82.9 0.2 constant_dynamic-update-slice_fusion.8
  83.1 0.8 fusion.66
  83.8 0.8 fusion.8
  84.6 1.0 multiply_convert_fusion.6
  85.6 0.8 fusion.64
  86.4 0.9 fusion
  87.4 0.2 pad_maximum_fusion
  87.6 2.5 %collective-permute-done.13 = bf16[160,1536]{1,0:T(8,128)(2,1)S(1)} collective-permute-done((bf16[160,1536]{1,0:T(8,128)(2,1)S(1)}, bf16[160,1536]{1,0:T(8,128)(2,1)S(1)}, u32[]{:S(2)}, u32[]{:S(2)}) %collective-permute-start.13) | collective-permute-done | bytes 491552 | tf_op jit(solution)/shard_map/ppermute | solution.py:22
  90.0 3.2 %collective-permute-done.12 = bf16[80,3584]{1,0:T(8,128)(2,1)S(1)} collective-permute-done((bf16[80,3584]{1,0:T(8,128)(2,1)S(1)}, bf16[80,3584]{1,0:T(8,128)(2,1)S(1)}, u32[]{:S(2)}, u32[]{:S(2)}) %collective-permute-start.12) | collective-permute-done | bytes 573472 | tf_op jit(solution)/shard_map/ppermute | solution.py:22
  93.6 0.6 collective-permute-start.20
  94.2 2.0 %collective-permute-done.14 = bf16[160,3584]{1,0:T(8,128)(2,1)S(1)} collective-permute-done((bf16[160,3584]{1,0:T(8,128)(2,1)S(1)}, bf16[160,3584]{1,0:T(8,128)(2,1)S(1)}, u32[]{:S(2)}, u32[]{:S(2)}) %collective-permute-start.14) | collective-permute-done | bytes 1146912 | tf_op jit(solution)/shard_map/ppermute | solution.py:22
  96.2 1.0 multiply_reduce_fusion
  97.2 0.3 collective-permute-start.17
  97.8 0.9 convolution_convert_fusion
  98.8 1.0 convolution_convert_fusion.5
  99.9 0.8 fusion.63
  100.8 0.3 add_convert_fusion
  101.1 0.9 collective-permute-start.21
  102.0 0.9 fusion.1
  103.1 0.3 collective-permute-start.18
  103.4 1.7 %collective-permute-start.23 = (bf16[128,3584]{1,0:T(8,128)(2,1)S(1)}, bf16[128,3584]{1,0:T(8,128)(2,1)S(1)}, u32[]{:S(2)}, u32[]{:S(2)}) collective-permute-start(bf16[128,3584]{1,0:T(8,128)(2,1)S(1)} %convolution_convert_fusion), channel_id=1, source_target_pairs={{0,2},{1,3},{2,0},{3,1},{4,6},{5,7},{6,4},{7,5},{8,10},{9,11},{10,... | collective-permute-start | bytes 2752520 | tf_op jit(solution)/shard_map/ppermute | solution.py:22
  105.0 12.2 %collective-permute-done.21 = bf16[80,3712]{1,0:T(8,128)(2,1)S(1)} collective-permute-done((bf16[80,3712]{1,0:T(8,128)(2,1)S(1)}, bf16[80,3712]{1,0:T(8,128)(2,1)S(1)}, u32[]{:S(2)}, u32[]{:S(2)}) %collective-permute-start.21) | collective-permute-done | bytes 593952 | tf_op jit(solution)/shard_map/ppermute | solution.py:22
  117.2 1.7 %collective-permute-start.15 = (bf16[2048,256]{1,0:T(8,128)(2,1)S(1)}, bf16[2048,256]{1,0:T(8,128)(2,1)S(1)}, u32[]{:S(2)}, u32[]{:S(2)}) collective-permute-start(bf16[2048,256]{1,0:T(8,128)(2,1)S(1)} %convolution_convert_fusion.5), channel_id=1, source_target_pairs={{0,2},{1,3},{2,0},{3,1},{4,6},{5,7},{6,4},{7,5},{8,10},{9,11},{10,... | collective-permute-start | bytes 3145736 | tf_op jit(solution)/shard_map/ppermute | solution.py:22
  118.9 0.2 add_convert_fusion.2
  119.1 1.1 collective-permute-start.22
  120.2 0.3 add_convert_fusion.1
  120.6 1.4 collective-permute-start.19
  122.0 1.0 fusion.21
  123.1 0.9 fusion.5
  124.0 23.9 %collective-permute-done.19 = bf16[80,3712]{1,0:T(8,128)(2,1)S(1)} collective-permute-done((bf16[80,3712]{1,0:T(8,128)(2,1)S(1)}, bf16[80,3712]{1,0:T(8,128)(2,1)S(1)}, u32[]{:S(2)}, u32[]{:S(2)}) %collective-permute-start.19) | collective-permute-done | bytes 593952 | tf_op jit(solution)/shard_map/ppermute | solution.py:22
  148.0 0.5 fusion.30
  148.5 1.0 slice.202
  149.5 1.0 fusion.4
  150.7 1.0 maximum_bitcast_fusion.1
  151.7 1.0 maximum_bitcast_fusion
  152.7 1.8 %fusion.3 = bf16[1,128,3584]{2,1,0:T(8,128)(2,1)} fusion(bf16[640,3584]{1,0:T(8,128)(2,1)S(1)} %constant_dynamic-update-slice_fusion.11, bf16[128,3584]{1,0:T(8,128)(2,1)S(1)} %collective-permute-done.23, bf16[320,256]{1,0:T(8,128)(2,1)S(1)} %get-tuple-element.85, bf16[320,256]{1,0:T(8,128)(2,1)S(1)} %get-tuple-element.83), kind=kOutput, calls=%fused_computation.7 | convolution fusion | flops 588906496 | bytes 6750208 | tf_op jit(solution)/shard_map/dot_general | solution.py:17
  154.5 0.6 copy.15
  (64 shorter events, 2.5 us)
Async XLA Ops:
  0.6 4.5 %copy-start = (bf16[128,3584]{1,0:T(8,128)(2,1)S(1)}, bf16[128,3584]{1,0:T(8,128)(2,1)}, u32[]{:S(2)}) copy-start(bf16[128,3584]{1,0:T(8,128)(2,1)} %param.7) | copy-start | bytes 2752516
  0.6 11.5 %copy-start.5 = (bf16[128,1]{0,1:T(2,128)(2,1)S(1)}, bf16[128,1]{0,1:T(2,128)(2,1)}, u32[]{:S(2)}) copy-start(bf16[128,1]{0,1:T(2,128)(2,1)} %param.9) | copy-start | bytes 772
  0.7 35.0 %collective-permute-start.2 = (bf16[3584,128]{1,0:T(8,128)(2,1)}, bf16[3584,128]{1,0:T(8,128)(2,1)S(1)}, u32[]{:S(2)}, u32[]{:S(2)}) collective-permute-start(bf16[3584,128]{1,0:T(8,128)(2,1)} %bitcast.29), channel_id=1, source_target_pairs={{0,2},{1,3},{2,0},{3,1},{4,6},{5,7},{6,4},{7,5},{8,10},{9,11},{10,... | collective-permute-start | bytes 2752520 | tf_op jit(solution)/shard_map/ppermute | solution.py:22
  6.3 28.0 %collective-permute-start = (bf16[80,3584]{1,0:T(8,128)(2,1)}, bf16[80,3584]{1,0:T(8,128)(2,1)}, u32[]{:S(2)}, u32[]{:S(2)}) collective-permute-start(bf16[80,3584]{1,0:T(8,128)(2,1)} %convolution_convert_fusion.3), channel_id=1, source_target_pairs={{0,8},{1,9},{2,10},{3,11},{4,12},{5,13},{6,14},{7,15},{8,0},{9,1},... | collective-permute-start | bytes 1720328 | tf_op jit(solution)/shard_map/ppermute | solution.py:22
  8.9 35.0 %collective-permute-start.6 = (bf16[3584,128]{1,0:T(8,128)(2,1)}, bf16[3584,128]{1,0:T(8,128)(2,1)S(1)}, u32[]{:S(2)}, u32[]{:S(2)}) collective-permute-start(bf16[3584,128]{1,0:T(8,128)(2,1)} %bitcast.24), channel_id=1, source_target_pairs={{0,2},{1,3},{2,0},{3,1},{4,6},{5,7},{6,4},{7,5},{8,10},{9,11},{10,... | collective-permute-start | bytes 2752520 | tf_op jit(solution)/shard_map/ppermute | solution.py:22
  10.6 25.0 %collective-permute-start.1 = (bf16[80,3584]{1,0:T(8,128)(2,1)S(1)}, bf16[80,3584]{1,0:T(8,128)(2,1)S(1)}, u32[]{:S(2)}, u32[]{:S(2)}) collective-permute-start(bf16[80,3584]{1,0:T(8,128)(2,1)S(1)} %get-tuple-element.94), channel_id=1, source_target_pairs={{0,4},{1,5},{2,6},{3,7},{4,0},{5,1},{6,2},{7,3},{8,12},{9,13},{10,... | collective-permute-start | bytes 1720328 | tf_op jit(solution)/shard_map/ppermute | solution.py:22
  12.4 31.5 %copy-start.6 = (bf16[1,128,3584]{2,1,0:T(8,128)(2,1)S(1)}, bf16[1,128,3584]{2,1,0:T(8,128)(2,1)}, u32[]{:S(2)}) copy-start(bf16[1,128,3584]{2,1,0:T(8,128)(2,1)} %param.13) | copy-start | bytes 2752516
  14.1 31.6 %copy-start.4 = (bf16[640,3584]{1,0:T(8,128)(2,1)S(1)}, bf16[640,3584]{1,0:T(8,128)(2,1)}, u32[]{:S(2)}) copy-start(bf16[640,3584]{1,0:T(8,128)(2,1)} %get-tuple-element.93) | copy-start | bytes 13762564
  35.7 30.4 %collective-permute-start.3 = (bf16[160,3584]{1,0:T(8,128)(2,1)S(1)}, bf16[160,3584]{1,0:T(8,128)(2,1)S(1)}, u32[]{:S(2)}, u32[]{:S(2)}) collective-permute-start(bf16[160,3584]{1,0:T(8,128)(2,1)S(1)} %pad_maximum_fusion.5), channel_id=1, source_target_pairs={{0,1},{1,0},{2,3},{3,2},{4,5},{5,4},{6,7},{7,6},{8,9},{9,8},{10,11... | collective-permute-start | bytes 3440648 | tf_op jit(solution)/shard_map/ppermute | solution.py:22
  35.8 30.3 %collective-permute-start.8 = (bf16[80,3584]{1,0:T(8,128)(2,1)S(1)}, bf16[80,3584]{1,0:T(8,128)(2,1)S(1)}, u32[]{:S(2)}, u32[]{:S(2)}) collective-permute-start(bf16[80,3584]{1,0:T(8,128)(2,1)S(1)} %convolution_convert_fusion.1), channel_id=1, source_target_pairs={{0,8},{1,9},{2,10},{3,11},{4,12},{5,13},{6,14},{7,15},{8,0},{9,1},... | collective-permute-start | bytes 1720328 | tf_op jit(solution)/shard_map/ppermute | solution.py:22
  36.4 28.2 %collective-permute-start.4 = (bf16[80,3584]{1,0:T(8,128)(2,1)}, bf16[80,3584]{1,0:T(8,128)(2,1)S(1)}, u32[]{:S(2)}, u32[]{:S(2)}) collective-permute-start(bf16[80,3584]{1,0:T(8,128)(2,1)} %collective-permute-done), channel_id=1, source_target_pairs={{0,4},{1,5},{2,6},{3,7},{4,0},{5,1},{6,2},{7,3},{8,12},{9,13},{10,... | collective-permute-start | bytes 1720328 | tf_op jit(solution)/shard_map/ppermute | solution.py:22
  43.9 23.7 %collective-permute-start.7 = (bf16[128,3584]{1,0:T(8,128)(2,1)S(1)}, bf16[128,3584]{1,0:T(8,128)(2,1)S(1)}, u32[]{:S(2)}, u32[]{:S(2)}) collective-permute-start(bf16[128,3584]{1,0:T(8,128)(2,1)S(1)} %bitcast.34), channel_id=1, source_target_pairs={{0,2},{1,3},{2,0},{3,1},{4,6},{5,7},{6,4},{7,5},{8,10},{9,11},{10,... | collective-permute-start | bytes 2752520 | tf_op jit(solution)/shard_map/ppermute | solution.py:22
  64.6 11.3 %collective-permute-start.10 = (bf16[160,1536]{1,0:T(8,128)(2,1)S(1)}, bf16[160,1536]{1,0:T(8,128)(2,1)S(1)}, u32[]{:S(2)}, u32[]{:S(2)}) collective-permute-start(bf16[160,1536]{1,0:T(8,128)(2,1)S(1)} %fusion.39), channel_id=1, source_target_pairs={{0,2},{1,3},{2,0},{3,1},{4,6},{5,7},{6,4},{7,5},{8,10},{9,11},{10,... | collective-permute-start | bytes 1474568 | tf_op jit(solution)/shard_map/ppermute | solution.py:22
  66.0 13.1 %collective-permute-start.9 = (bf16[80,3584]{1,0:T(8,128)(2,1)S(1)}, bf16[80,3584]{1,0:T(8,128)(2,1)S(1)}, u32[]{:S(2)}, u32[]{:S(2)}) collective-permute-start(bf16[80,3584]{1,0:T(8,128)(2,1)S(1)} %collective-permute-done.8), channel_id=1, source_target_pairs={{0,4},{1,5},{2,6},{3,7},{4,0},{5,1},{6,2},{7,3},{8,12},{9,13},{10,... | collective-permute-start | bytes 1720328 | tf_op jit(solution)/shard_map/ppermute | solution.py:22
  67.3 13.7 %copy-start.3 = (bf16[1,3584,128]{2,1,0:T(8,128)(2,1)S(1)}, bf16[1,3584,128]{2,1,0:T(8,128)(2,1)}, u32[]{:S(2)}) copy-start(bf16[1,3584,128]{2,1,0:T(8,128)(2,1)} %param.11) | copy-start | bytes 2752516
  67.5 15.4 %collective-permute-start.5 = (bf16[160,3584]{1,0:T(8,128)(2,1)S(1)}, bf16[160,3584]{1,0:T(8,128)(2,1)S(1)}, u32[]{:S(2)}, u32[]{:S(2)}) collective-permute-start(bf16[160,3584]{1,0:T(8,128)(2,1)S(1)} %get-tuple-element.89), channel_id=1, source_target_pairs={{0,1},{1,0},{2,3},{3,2},{4,5},{5,4},{6,7},{7,6},{8,9},{9,8},{10,11... | collective-permute-start | bytes 3440648 | tf_op jit(solution)/shard_map/ppermute | solution.py:22
  79.1 10.9 %collective-permute-start.13 = (bf16[160,1536]{1,0:T(8,128)(2,1)S(1)}, bf16[160,1536]{1,0:T(8,128)(2,1)S(1)}, u32[]{:S(2)}, u32[]{:S(2)}) collective-permute-start(bf16[160,1536]{1,0:T(8,128)(2,1)S(1)} %slice.129), channel_id=1, source_target_pairs={{0,2},{1,3},{2,0},{3,1},{4,6},{5,7},{6,4},{7,5},{8,10},{9,11},{10,... | collective-permute-start | bytes 1474568 | tf_op jit(solution)/shard_map/ppermute | solution.py:22
  80.6 12.7 %collective-permute-start.12 = (bf16[80,3584]{1,0:T(8,128)(2,1)S(1)}, bf16[80,3584]{1,0:T(8,128)(2,1)S(1)}, u32[]{:S(2)}, u32[]{:S(2)}) collective-permute-start(bf16[80,3584]{1,0:T(8,128)(2,1)S(1)} %convolution_convert_fusion.2), channel_id=1, source_target_pairs={{0,4},{1,5},{2,6},{3,7},{4,0},{5,1},{6,2},{7,3},{8,12},{9,13},{10,... | collective-permute-start | bytes 1720328 | tf_op jit(solution)/shard_map/ppermute | solution.py:22
  80.9 1.2 copy-start.2
  80.9 2.9 %collective-permute-start.11 = (bf16[160,3584]{1,0:T(8,128)(2,1)S(1)}, bf16[160,3584]{1,0:T(8,128)(2,1)S(1)}, u32[]{:S(2)}, u32[]{:S(2)}) collective-permute-start(bf16[160,3584]{1,0:T(8,128)(2,1)S(1)} %pad_maximum_fusion.9), channel_id=1, source_target_pairs={{0,1},{1,0},{2,3},{3,2},{4,5},{5,4},{6,7},{7,6},{8,9},{9,8},{10,11... | collective-permute-start | bytes 3440648 | tf_op jit(solution)/shard_map/ppermute | solution.py:22
  93.3 2.9 %collective-permute-start.14 = (bf16[160,3584]{1,0:T(8,128)(2,1)S(1)}, bf16[160,3584]{1,0:T(8,128)(2,1)S(1)}, u32[]{:S(2)}, u32[]{:S(2)}) collective-permute-start(bf16[160,3584]{1,0:T(8,128)(2,1)S(1)} %pad_maximum_fusion.10), channel_id=1, source_target_pairs={{0,1},{1,0},{2,3},{3,2},{4,5},{5,4},{6,7},{7,6},{8,9},{9,8},{10,11... | collective-permute-start | bytes 3440648 | tf_op jit(solution)/shard_map/ppermute | solution.py:22
  93.6 7.2 %collective-permute-start.20 = (bf16[160,3712]{1,0:T(8,128)(2,1)S(1)}, bf16[160,3712]{1,0:T(8,128)(2,1)S(1)}, u32[]{:S(2)}, u32[]{:S(2)}) collective-permute-start(bf16[160,3712]{1,0:T(8,128)(2,1)S(1)} %slice.114), channel_id=1, source_target_pairs={{0,1},{1,0},{2,3},{3,2},{4,5},{5,4},{6,7},{7,6},{8,9},{9,8},{10,11... | collective-permute-start | bytes 3563528 | tf_op jit(solution)/shard_map/ppermute | solution.py:22
  97.2 24.8 %collective-permute-start.17 = (bf16[640,256]{1,0:T(8,128)(2,1)S(1)}, bf16[640,256]{1,0:T(8,128)(2,1)S(1)}, u32[]{:S(2)}, u32[]{:S(2)}) collective-permute-start(bf16[640,256]{1,0:T(8,128)(2,1)S(1)} %pad_maximum_fusion.15), channel_id=1, source_target_pairs={{0,2},{1,3},{2,0},{3,1},{4,6},{5,7},{6,4},{7,5},{8,10},{9,11},{10,... | collective-permute-start | bytes 983048 | tf_op jit(solution)/shard_map/ppermute | solution.py:22
  99.8 19.3 %collective-permute-start.16 = (bf16[320,1536]{1,0:T(8,128)(2,1)S(1)}, bf16[320,1536]{1,0:T(8,128)(2,1)S(1)}, u32[]{:S(2)}, u32[]{:S(2)}) collective-permute-start(bf16[320,1536]{1,0:T(8,128)(2,1)S(1)} %pad_maximum_fusion.11), channel_id=1, source_target_pairs={{0,1},{1,0},{2,3},{3,2},{4,5},{5,4},{6,7},{7,6},{8,9},{9,8},{10,11... | collective-permute-start | bytes 2949128 | tf_op jit(solution)/shard_map/ppermute | solution.py:22
  101.1 16.1 %collective-permute-start.21 = (bf16[80,3712]{1,0:T(8,128)(2,1)S(1)}, bf16[80,3712]{1,0:T(8,128)(2,1)S(1)}, u32[]{:S(2)}, u32[]{:S(2)}) collective-permute-start(bf16[80,3712]{1,0:T(8,128)(2,1)S(1)} %slice.144), channel_id=1, source_target_pairs={{0,4},{1,5},{2,6},{3,7},{4,0},{5,1},{6,2},{7,3},{8,12},{9,13},{10,... | collective-permute-start | bytes 1781768 | tf_op jit(solution)/shard_map/ppermute | solution.py:22
  103.1 17.2 %collective-permute-start.18 = (bf16[160,3712]{1,0:T(8,128)(2,1)S(1)}, bf16[160,3712]{1,0:T(8,128)(2,1)S(1)}, u32[]{:S(2)}, u32[]{:S(2)}) collective-permute-start(bf16[160,3712]{1,0:T(8,128)(2,1)S(1)} %pad_maximum_fusion.6), channel_id=1, source_target_pairs={{0,1},{1,0},{2,3},{3,2},{4,5},{5,4},{6,7},{7,6},{8,9},{9,8},{10,11... | collective-permute-start | bytes 3563528 | tf_op jit(solution)/shard_map/ppermute | solution.py:22
  103.4 49.3 %collective-permute-start.23 = (bf16[128,3584]{1,0:T(8,128)(2,1)S(1)}, bf16[128,3584]{1,0:T(8,128)(2,1)S(1)}, u32[]{:S(2)}, u32[]{:S(2)}) collective-permute-start(bf16[128,3584]{1,0:T(8,128)(2,1)S(1)} %convolution_convert_fusion), channel_id=1, source_target_pairs={{0,2},{1,3},{2,0},{3,1},{4,6},{5,7},{6,4},{7,5},{8,10},{9,11},{10,... | collective-permute-start | bytes 2752520 | tf_op jit(solution)/shard_map/ppermute | solution.py:22
  117.2 32.4 %collective-permute-start.15 = (bf16[2048,256]{1,0:T(8,128)(2,1)S(1)}, bf16[2048,256]{1,0:T(8,128)(2,1)S(1)}, u32[]{:S(2)}, u32[]{:S(2)}) collective-permute-start(bf16[2048,256]{1,0:T(8,128)(2,1)S(1)} %convolution_convert_fusion.5), channel_id=1, source_target_pairs={{0,2},{1,3},{2,0},{3,1},{4,6},{5,7},{6,4},{7,5},{8,10},{9,11},{10,... | collective-permute-start | bytes 3145736 | tf_op jit(solution)/shard_map/ppermute | solution.py:22
  119.1 28.9 %collective-permute-start.22 = (bf16[80,3712]{1,0:T(8,128)(2,1)S(1)}, bf16[80,3712]{1,0:T(8,128)(2,1)S(1)}, u32[]{:S(2)}, u32[]{:S(2)}) collective-permute-start(bf16[80,3712]{1,0:T(8,128)(2,1)S(1)} %add_convert_fusion.2), channel_id=1, source_target_pairs={{0,8},{1,9},{2,10},{3,11},{4,12},{5,13},{6,14},{7,15},{8,0},{9,1},... | collective-permute-start | bytes 1781768 | tf_op jit(solution)/shard_map/ppermute | solution.py:22
  120.6 27.2 %collective-permute-start.19 = (bf16[80,3712]{1,0:T(8,128)(2,1)S(1)}, bf16[80,3712]{1,0:T(8,128)(2,1)S(1)}, u32[]{:S(2)}, u32[]{:S(2)}) collective-permute-start(bf16[80,3712]{1,0:T(8,128)(2,1)S(1)} %slice.142), channel_id=1, source_target_pairs={{0,4},{1,5},{2,6},{3,7},{4,0},{5,1},{6,2},{7,3},{8,12},{9,13},{10,... | collective-permute-start | bytes 1781768 | tf_op jit(solution)/shard_map/ppermute | solution.py:22
  151.7 3.4 %copy-start.1 = (bf16[128,3584]{1,0:T(8,128)(2,1)S(1)}, bf16[128,3584]{1,0:T(8,128)(2,1)}, u32[]{:S(2)}) copy-start(bf16[128,3584]{1,0:T(8,128)(2,1)} %param.7) | copy-start | bytes 2752516

commit v6 on v5

--- a/solution.py
+++ b/solution.py
@@ -153,16 +153,16 @@
     grad_combine = out[:, features : features + 1] / weight
 
     first = (dot(x[:, :shared], both, 0, 0) + dot(x_p, got_both, 0, 0)).astype(BF16)
-    got_rest, first, grad_tokens = lax.optimization_barrier((got_rest, first, grad_tokens))
+    got_down, first = lax.optimization_barrier((got_down, first))
+    grad_down = (dot(hidden[:, :hid], u, 0, 0) + got_down.astype(F32)).astype(BF16)[None]
+    got_rest, first, grad_tokens, grad_combine, grad_down = lax.optimization_barrier(
+        (got_rest, first, grad_tokens, grad_combine, grad_down)
+    )
     rest = (dot(x[:, shared:], both, 0, 0) + got_rest.astype(F32)).astype(BF16)
     grad_gate, grad_up = (
         jnp.concatenate([first[:, at], rest[:, at]], axis=0)[None]
         for at in (slice(0, hid), slice(hid, None))
     )
-    got_down, grad_gate, grad_up, grad_combine = lax.optimization_barrier(
-        (got_down, grad_gate, grad_up, grad_combine)
-    )
-    grad_down = (dot(hidden[:, :hid], u, 0, 0) + got_down.astype(F32)).astype(BF16)[None]
     return (grad_tokens, grad_combine, grad_gate, grad_up, grad_down)
 
 

time: 155 us -> 155 us (level)
  transfers between devices with their start and end apart: 24 -> 24, of which waited for: 11 -> 12; matrix products, arithmetic and copies ran while one was open for 18% -> 17% of each run, Pallas kernels for 0% -> 0%
where the time goes in v6:
time: 155 us; the launch traced here: 154 us
  waiting for transfers between devices  98.2 us (63%)
  starting transfers between devices  24 us (15%)
  matrix products  21.3 us (14%)
  other arithmetic  5.02 us (3%)
  local copies, waits for them, and re-layouts  4.67 us (3%)
    ppermute x24, waiting for transfers between devices, flip(): return lax.ppermute(x, 'expert', [(i, i ^ mask) for i in range(n)])  98.2 us
    ppermute x24, starting transfers between devices, flip(): return lax.ppermute(x, 'expert', [(i, i ^ mask) for i in range(n)])  24 us
    dot_general x22, matrix products, dot(): lax.dot_general(a, b, (((ca,), (cb,)), ((), ())), preferred_element_type=...  21.3 us
  transfers between devices with their start and end apart: 24, of which 12 were waited for; matrix products, arithmetic and copies ran while one was open for 17% of the time, Pallas kernels for 0%

profile of v6, /device:TPU:0, one launch (start us, length us, event | category | flops | bytes accessed | tf_op | source)
XLA Modules:
  0.0 154.3 jit_solution(12013630100566453710)
XLA Ops:
  0.7 3.0 %collective-permute-start.2 = (bf16[3584,128]{1,0:T(8,128)(2,1)}, bf16[3584,128]{1,0:T(8,128)(2,1)S(1)}, u32[]{:S(2)}, u32[]{:S(2)}) collective-permute-start(bf16[3584,128]{1,0:T(8,128)(2,1)} %bitcast.29), channel_id=1, source_target_pairs={{0,2},{1,3},{2,0},{3,1},{4,6},{5,7},{6,4},{7,5},{8,10},{9,11},{10,... | collective-permute-start | bytes 2752520 | tf_op jit(solution)/shard_map/ppermute | solution.py:22
  3.7 0.7 xor_bitcast_fusion
  4.5 0.7 bitcast_add_fusion
  5.2 1.1 convolution_convert_fusion.3
  6.3 2.6 %collective-permute-start = (bf16[80,3584]{1,0:T(8,128)(2,1)}, bf16[80,3584]{1,0:T(8,128)(2,1)}, u32[]{:S(2)}, u32[]{:S(2)}) collective-permute-start(bf16[80,3584]{1,0:T(8,128)(2,1)} %convolution_convert_fusion.3), channel_id=1, source_target_pairs={{0,8},{1,9},{2,10},{3,11},{4,12},{5,13},{6,14},{7,15},{8,0},{9,1},... | collective-permute-start | bytes 1720328 | tf_op jit(solution)/shard_map/ppermute | solution.py:22
  8.9 0.5 collective-permute-start.6
  9.4 1.1 constant_dynamic-update-slice_fusion.7
  10.6 1.6 %collective-permute-start.1 = (bf16[80,3584]{1,0:T(8,128)(2,1)S(1)}, bf16[80,3584]{1,0:T(8,128)(2,1)S(1)}, u32[]{:S(2)}, u32[]{:S(2)}) collective-permute-start(bf16[80,3584]{1,0:T(8,128)(2,1)S(1)} %get-tuple-element.94), channel_id=1, source_target_pairs={{0,4},{1,5},{2,6},{3,7},{4,0},{5,1},{6,2},{7,3},{8,12},{9,13},{10,... | collective-permute-start | bytes 1720328 | tf_op jit(solution)/shard_map/ppermute | solution.py:22
  12.4 1.6 %convolution_convert_fusion.1 = bf16[80,3584]{1,0:T(8,128)(2,1)S(1)} fusion(bf16[128,3584]{1,0:T(8,128)(2,1)} %param.8, f32[128]{0:T(128)S(1)} %convert_reduce_fusion, pred[160,128]{1,0:T(8,128)(4,1)S(1)} %iota_compare_fusion.1), kind=kOutput, calls=%fused_computation.8 | convolution fusion | flops 75063296 | bytes 1501696 | tf_op jit(solution)/shard_map/dot_general | solution.py:17
  14.1 1.7 %convolution_convert_fusion.2 = bf16[80,3584]{1,0:T(8,128)(2,1)S(1)} fusion(bf16[128,3584]{1,0:T(8,128)(2,1)} %param.8, f32[128]{0:T(128)S(1)} %convert_reduce_fusion, pred[160,128]{1,0:T(8,128)(4,1)S(1)} %iota_compare_fusion.1), kind=kOutput, calls=%fused_computation.9 | convolution fusion | flops 75063296 | bytes 1501696 | tf_op jit(solution)/shard_map/dot_general | solution.py:17
  15.8 18.6 %collective-permute-done = bf16[80,3584]{1,0:T(8,128)(2,1)} collective-permute-done((bf16[80,3584]{1,0:T(8,128)(2,1)}, bf16[80,3584]{1,0:T(8,128)(2,1)}, u32[]{:S(2)}, u32[]{:S(2)}) %collective-permute-start) | collective-permute-done | bytes 573472 | tf_op jit(solution)/shard_map/ppermute | solution.py:22
  34.4 1.3 collective-permute-done.1
  35.8 0.6 collective-permute-start.8
  36.4 2.4 %collective-permute-start.4 = (bf16[80,3584]{1,0:T(8,128)(2,1)}, bf16[80,3584]{1,0:T(8,128)(2,1)S(1)}, u32[]{:S(2)}, u32[]{:S(2)}) collective-permute-start(bf16[80,3584]{1,0:T(8,128)(2,1)} %collective-permute-done), channel_id=1, source_target_pairs={{0,4},{1,5},{2,6},{3,7},{4,0},{5,1},{6,2},{7,3},{8,12},{9,13},{10,... | collective-permute-start | bytes 1720328 | tf_op jit(solution)/shard_map/ppermute | solution.py:22
  38.9 5.0 %collective-permute-done.6 = bf16[3584,128]{1,0:T(8,128)(2,1)S(1)} collective-permute-done((bf16[3584,128]{1,0:T(8,128)(2,1)}, bf16[3584,128]{1,0:T(8,128)(2,1)S(1)}, u32[]{:S(2)}, u32[]{:S(2)}) %collective-permute-start.6) | collective-permute-done | bytes 917536 | tf_op jit(solution)/shard_map/ppermute | solution.py:22
  43.9 1.7 %collective-permute-start.7 = (bf16[128,3584]{1,0:T(8,128)(2,1)S(1)}, bf16[128,3584]{1,0:T(8,128)(2,1)S(1)}, u32[]{:S(2)}, u32[]{:S(2)}) collective-permute-start(bf16[128,3584]{1,0:T(8,128)(2,1)S(1)} %bitcast.34), channel_id=1, source_target_pairs={{0,2},{1,3},{2,0},{3,1},{4,6},{5,7},{6,4},{7,5},{8,10},{9,11},{10,... | collective-permute-start | bytes 2752520 | tf_op jit(solution)/shard_map/ppermute | solution.py:22
  45.7 18.9 %collective-permute-done.4 = bf16[80,3584]{1,0:T(8,128)(2,1)S(1)} collective-permute-done((bf16[80,3584]{1,0:T(8,128)(2,1)}, bf16[80,3584]{1,0:T(8,128)(2,1)S(1)}, u32[]{:S(2)}, u32[]{:S(2)}) %collective-permute-start.4) | collective-permute-done | bytes 573472 | tf_op jit(solution)/shard_map/ppermute | solution.py:22
  64.6 1.4 collective-permute-start.10
  66.1 1.2 constant_dynamic-update-slice_fusion.10
  67.6 8.3 %collective-permute-done.10 = bf16[160,1536]{1,0:T(8,128)(2,1)S(1)} collective-permute-done((bf16[160,1536]{1,0:T(8,128)(2,1)S(1)}, bf16[160,1536]{1,0:T(8,128)(2,1)S(1)}, u32[]{:S(2)}, u32[]{:S(2)}) %collective-permute-start.10) | collective-permute-done | bytes 491552 | tf_op jit(solution)/shard_map/ppermute | solution.py:22
  76.0 3.2 %collective-permute-done.9 = bf16[80,3584]{1,0:T(8,128)(2,1)S(1)} collective-permute-done((bf16[80,3584]{1,0:T(8,128)(2,1)S(1)}, bf16[80,3584]{1,0:T(8,128)(2,1)S(1)}, u32[]{:S(2)}, u32[]{:S(2)}) %collective-permute-start.9) | collective-permute-done | bytes 573472 | tf_op jit(solution)/shard_map/ppermute | solution.py:22
  79.1 1.4 collective-permute-start.13
  80.6 0.3 collective-permute-start.12
  81.0 0.8 fusion.35
  81.8 0.3 copy-done.2
  82.1 0.8 fusion.36
  82.9 0.2 constant_dynamic-update-slice_fusion.8
  83.1 0.8 fusion.66
  83.8 0.8 fusion.8
  84.6 1.0 multiply_convert_fusion.6
  85.6 0.8 fusion.64
  86.4 0.9 fusion
  87.4 0.2 pad_maximum_fusion
  87.6 2.5 %collective-permute-done.13 = bf16[160,1536]{1,0:T(8,128)(2,1)S(1)} collective-permute-done((bf16[160,1536]{1,0:T(8,128)(2,1)S(1)}, bf16[160,1536]{1,0:T(8,128)(2,1)S(1)}, u32[]{:S(2)}, u32[]{:S(2)}) %collective-permute-start.13) | collective-permute-done | bytes 491552 | tf_op jit(solution)/shard_map/ppermute | solution.py:22
  90.0 3.2 %collective-permute-done.12 = bf16[80,3584]{1,0:T(8,128)(2,1)S(1)} collective-permute-done((bf16[80,3584]{1,0:T(8,128)(2,1)S(1)}, bf16[80,3584]{1,0:T(8,128)(2,1)S(1)}, u32[]{:S(2)}, u32[]{:S(2)}) %collective-permute-start.12) | collective-permute-done | bytes 573472 | tf_op jit(solution)/shard_map/ppermute | solution.py:22
  93.6 0.6 collective-permute-start.21
  94.2 2.0 %collective-permute-done.14 = bf16[160,3584]{1,0:T(8,128)(2,1)S(1)} collective-permute-done((bf16[160,3584]{1,0:T(8,128)(2,1)S(1)}, bf16[160,3584]{1,0:T(8,128)(2,1)S(1)}, u32[]{:S(2)}, u32[]{:S(2)}) %collective-permute-start.14) | collective-permute-done | bytes 1146912 | tf_op jit(solution)/shard_map/ppermute | solution.py:22
  96.2 1.0 multiply_reduce_fusion
  97.2 0.3 collective-permute-start.18
  97.8 0.9 convolution_convert_fusion
  98.8 1.0 convolution_convert_fusion.5
  99.9 0.8 fusion.63
  100.8 0.3 add_convert_fusion
  101.1 0.9 collective-permute-start.22
  102.0 0.9 fusion.1
  103.1 0.3 collective-permute-start.19
  103.4 1.7 %collective-permute-start.16 = (bf16[128,3584]{1,0:T(8,128)(2,1)S(1)}, bf16[128,3584]{1,0:T(8,128)(2,1)S(1)}, u32[]{:S(2)}, u32[]{:S(2)}) collective-permute-start(bf16[128,3584]{1,0:T(8,128)(2,1)S(1)} %convolution_convert_fusion), channel_id=1, source_target_pairs={{0,2},{1,3},{2,0},{3,1},{4,6},{5,7},{6,4},{7,5},{8,10},{9,11},{10,... | collective-permute-start | bytes 2752520 | tf_op jit(solution)/shard_map/ppermute | solution.py:22
  105.0 12.2 %collective-permute-done.22 = bf16[80,3712]{1,0:T(8,128)(2,1)S(1)} collective-permute-done((bf16[80,3712]{1,0:T(8,128)(2,1)S(1)}, bf16[80,3712]{1,0:T(8,128)(2,1)S(1)}, u32[]{:S(2)}, u32[]{:S(2)}) %collective-permute-start.22) | collective-permute-done | bytes 593952 | tf_op jit(solution)/shard_map/ppermute | solution.py:22
  117.2 1.7 %collective-permute-start.15 = (bf16[2048,256]{1,0:T(8,128)(2,1)S(1)}, bf16[2048,256]{1,0:T(8,128)(2,1)S(1)}, u32[]{:S(2)}, u32[]{:S(2)}) collective-permute-start(bf16[2048,256]{1,0:T(8,128)(2,1)S(1)} %convolution_convert_fusion.5), channel_id=1, source_target_pairs={{0,2},{1,3},{2,0},{3,1},{4,6},{5,7},{6,4},{7,5},{8,10},{9,11},{10,... | collective-permute-start | bytes 3145736 | tf_op jit(solution)/shard_map/ppermute | solution.py:22
  118.9 0.2 add_convert_fusion.2
  119.1 1.1 collective-permute-start.23
  120.2 1.1 fusion.21
  121.3 0.3 add_convert_fusion.1
  121.7 1.4 collective-permute-start.20
  123.1 0.9 fusion.5
  124.0 3.5 %collective-permute-done.16 = bf16[128,3584]{1,0:T(8,128)(2,1)S(1)} collective-permute-done((bf16[128,3584]{1,0:T(8,128)(2,1)S(1)}, bf16[128,3584]{1,0:T(8,128)(2,1)S(1)}, u32[]{:S(2)}, u32[]{:S(2)}) %collective-permute-start.16) | collective-permute-done | bytes 917536 | tf_op jit(solution)/shard_map/ppermute | solution.py:22
  127.4 1.8 %fusion.3 = bf16[1,128,3584]{2,1,0:T(8,128)(2,1)} fusion(bf16[640,3584]{1,0:T(8,128)(2,1)S(1)} %constant_dynamic-update-slice_fusion.11, bf16[128,3584]{1,0:T(8,128)(2,1)S(1)} %collective-permute-done.16, bf16[320,256]{1,0:T(8,128)(2,1)S(1)} %get-tuple-element.85, bf16[320,256]{1,0:T(8,128)(2,1)S(1)} %get-tuple-element.83), kind=kOutput, calls=%fused_computation.7 | convolution fusion | flops 588906496 | bytes 6750208 | tf_op jit(solution)/shard_map/dot_general | solution.py:17
  129.3 19.6 %collective-permute-done.20 = bf16[80,3712]{1,0:T(8,128)(2,1)S(1)} collective-permute-done((bf16[80,3712]{1,0:T(8,128)(2,1)S(1)}, bf16[80,3712]{1,0:T(8,128)(2,1)S(1)}, u32[]{:S(2)}, u32[]{:S(2)}) %collective-permute-start.20) | collective-permute-done | bytes 593952 | tf_op jit(solution)/shard_map/ppermute | solution.py:22
  149.1 0.5 fusion.30
  149.5 1.0 slice.202
  150.6 1.0 fusion.4
  151.7 0.6 copy.15
  152.3 1.0 maximum_bitcast_fusion.1
  153.3 1.0 maximum_bitcast_fusion
  (64 shorter events, 2.7 us)
Async XLA Ops:
  0.6 4.5 %copy-start = (bf16[128,3584]{1,0:T(8,128)(2,1)S(1)}, bf16[128,3584]{1,0:T(8,128)(2,1)}, u32[]{:S(2)}) copy-start(bf16[128,3584]{1,0:T(8,128)(2,1)} %param.7) | copy-start | bytes 2752516
  0.6 11.5 %copy-start.5 = (bf16[128,1]{0,1:T(2,128)(2,1)S(1)}, bf16[128,1]{0,1:T(2,128)(2,1)}, u32[]{:S(2)}) copy-start(bf16[128,1]{0,1:T(2,128)(2,1)} %param.9) | copy-start | bytes 772
  0.7 35.0 %collective-permute-start.2 = (bf16[3584,128]{1,0:T(8,128)(2,1)}, bf16[3584,128]{1,0:T(8,128)(2,1)S(1)}, u32[]{:S(2)}, u32[]{:S(2)}) collective-permute-start(bf16[3584,128]{1,0:T(8,128)(2,1)} %bitcast.29), channel_id=1, source_target_pairs={{0,2},{1,3},{2,0},{3,1},{4,6},{5,7},{6,4},{7,5},{8,10},{9,11},{10,... | collective-permute-start | bytes 2752520 | tf_op jit(solution)/shard_map/ppermute | solution.py:22
  6.3 28.0 %collective-permute-start = (bf16[80,3584]{1,0:T(8,128)(2,1)}, bf16[80,3584]{1,0:T(8,128)(2,1)}, u32[]{:S(2)}, u32[]{:S(2)}) collective-permute-start(bf16[80,3584]{1,0:T(8,128)(2,1)} %convolution_convert_fusion.3), channel_id=1, source_target_pairs={{0,8},{1,9},{2,10},{3,11},{4,12},{5,13},{6,14},{7,15},{8,0},{9,1},... | collective-permute-start | bytes 1720328 | tf_op jit(solution)/shard_map/ppermute | solution.py:22
  8.9 35.0 %collective-permute-start.6 = (bf16[3584,128]{1,0:T(8,128)(2,1)}, bf16[3584,128]{1,0:T(8,128)(2,1)S(1)}, u32[]{:S(2)}, u32[]{:S(2)}) collective-permute-start(bf16[3584,128]{1,0:T(8,128)(2,1)} %bitcast.24), channel_id=1, source_target_pairs={{0,2},{1,3},{2,0},{3,1},{4,6},{5,7},{6,4},{7,5},{8,10},{9,11},{10,... | collective-permute-start | bytes 2752520 | tf_op jit(solution)/shard_map/ppermute | solution.py:22
  10.6 25.0 %collective-permute-start.1 = (bf16[80,3584]{1,0:T(8,128)(2,1)S(1)}, bf16[80,3584]{1,0:T(8,128)(2,1)S(1)}, u32[]{:S(2)}, u32[]{:S(2)}) collective-permute-start(bf16[80,3584]{1,0:T(8,128)(2,1)S(1)} %get-tuple-element.94), channel_id=1, source_target_pairs={{0,4},{1,5},{2,6},{3,7},{4,0},{5,1},{6,2},{7,3},{8,12},{9,13},{10,... | collective-permute-start | bytes 1720328 | tf_op jit(solution)/shard_map/ppermute | solution.py:22
  12.4 31.5 %copy-start.6 = (bf16[1,128,3584]{2,1,0:T(8,128)(2,1)S(1)}, bf16[1,128,3584]{2,1,0:T(8,128)(2,1)}, u32[]{:S(2)}) copy-start(bf16[1,128,3584]{2,1,0:T(8,128)(2,1)} %param.13) | copy-start | bytes 2752516
  14.1 31.6 %copy-start.4 = (bf16[640,3584]{1,0:T(8,128)(2,1)S(1)}, bf16[640,3584]{1,0:T(8,128)(2,1)}, u32[]{:S(2)}) copy-start(bf16[640,3584]{1,0:T(8,128)(2,1)} %get-tuple-element.93) | copy-start | bytes 13762564
  35.7 30.4 %collective-permute-start.3 = (bf16[160,3584]{1,0:T(8,128)(2,1)S(1)}, bf16[160,3584]{1,0:T(8,128)(2,1)S(1)}, u32[]{:S(2)}, u32[]{:S(2)}) collective-permute-start(bf16[160,3584]{1,0:T(8,128)(2,1)S(1)} %pad_maximum_fusion.5), channel_id=1, source_target_pairs={{0,1},{1,0},{2,3},{3,2},{4,5},{5,4},{6,7},{7,6},{8,9},{9,8},{10,11... | collective-permute-start | bytes 3440648 | tf_op jit(solution)/shard_map/ppermute | solution.py:22
  35.8 30.3 %collective-permute-start.8 = (bf16[80,3584]{1,0:T(8,128)(2,1)S(1)}, bf16[80,3584]{1,0:T(8,128)(2,1)S(1)}, u32[]{:S(2)}, u32[]{:S(2)}) collective-permute-start(bf16[80,3584]{1,0:T(8,128)(2,1)S(1)} %convolution_convert_fusion.1), channel_id=1, source_target_pairs={{0,8},{1,9},{2,10},{3,11},{4,12},{5,13},{6,14},{7,15},{8,0},{9,1},... | collective-permute-start | bytes 1720328 | tf_op jit(solution)/shard_map/ppermute | solution.py:22
  36.4 28.2 %collective-permute-start.4 = (bf16[80,3584]{1,0:T(8,128)(2,1)}, bf16[80,3584]{1,0:T(8,128)(2,1)S(1)}, u32[]{:S(2)}, u32[]{:S(2)}) collective-permute-start(bf16[80,3584]{1,0:T(8,128)(2,1)} %collective-permute-done), channel_id=1, source_target_pairs={{0,4},{1,5},{2,6},{3,7},{4,0},{5,1},{6,2},{7,3},{8,12},{9,13},{10,... | collective-permute-start | bytes 1720328 | tf_op jit(solution)/shard_map/ppermute | solution.py:22
  43.9 23.7 %collective-permute-start.7 = (bf16[128,3584]{1,0:T(8,128)(2,1)S(1)}, bf16[128,3584]{1,0:T(8,128)(2,1)S(1)}, u32[]{:S(2)}, u32[]{:S(2)}) collective-permute-start(bf16[128,3584]{1,0:T(8,128)(2,1)S(1)} %bitcast.34), channel_id=1, source_target_pairs={{0,2},{1,3},{2,0},{3,1},{4,6},{5,7},{6,4},{7,5},{8,10},{9,11},{10,... | collective-permute-start | bytes 2752520 | tf_op jit(solution)/shard_map/ppermute | solution.py:22
  64.6 11.3 %collective-permute-start.10 = (bf16[160,1536]{1,0:T(8,128)(2,1)S(1)}, bf16[160,1536]{1,0:T(8,128)(2,1)S(1)}, u32[]{:S(2)}, u32[]{:S(2)}) collective-permute-start(bf16[160,1536]{1,0:T(8,128)(2,1)S(1)} %fusion.39), channel_id=1, source_target_pairs={{0,2},{1,3},{2,0},{3,1},{4,6},{5,7},{6,4},{7,5},{8,10},{9,11},{10,... | collective-permute-start | bytes 1474568 | tf_op jit(solution)/shard_map/ppermute | solution.py:22
  66.0 13.1 %collective-permute-start.9 = (bf16[80,3584]{1,0:T(8,128)(2,1)S(1)}, bf16[80,3584]{1,0:T(8,128)(2,1)S(1)}, u32[]{:S(2)}, u32[]{:S(2)}) collective-permute-start(bf16[80,3584]{1,0:T(8,128)(2,1)S(1)} %collective-permute-done.8), channel_id=1, source_target_pairs={{0,4},{1,5},{2,6},{3,7},{4,0},{5,1},{6,2},{7,3},{8,12},{9,13},{10,... | collective-permute-start | bytes 1720328 | tf_op jit(solution)/shard_map/ppermute | solution.py:22
  67.3 13.7 %copy-start.3 = (bf16[1,3584,128]{2,1,0:T(8,128)(2,1)S(1)}, bf16[1,3584,128]{2,1,0:T(8,128)(2,1)}, u32[]{:S(2)}) copy-start(bf16[1,3584,128]{2,1,0:T(8,128)(2,1)} %param.11) | copy-start | bytes 2752516
  67.5 15.4 %collective-permute-start.5 = (bf16[160,3584]{1,0:T(8,128)(2,1)S(1)}, bf16[160,3584]{1,0:T(8,128)(2,1)S(1)}, u32[]{:S(2)}, u32[]{:S(2)}) collective-permute-start(bf16[160,3584]{1,0:T(8,128)(2,1)S(1)} %get-tuple-element.89), channel_id=1, source_target_pairs={{0,1},{1,0},{2,3},{3,2},{4,5},{5,4},{6,7},{7,6},{8,9},{9,8},{10,11... | collective-permute-start | bytes 3440648 | tf_op jit(solution)/shard_map/ppermute | solution.py:22
  79.1 10.9 %collective-permute-start.13 = (bf16[160,1536]{1,0:T(8,128)(2,1)S(1)}, bf16[160,1536]{1,0:T(8,128)(2,1)S(1)}, u32[]{:S(2)}, u32[]{:S(2)}) collective-permute-start(bf16[160,1536]{1,0:T(8,128)(2,1)S(1)} %slice.129), channel_id=1, source_target_pairs={{0,2},{1,3},{2,0},{3,1},{4,6},{5,7},{6,4},{7,5},{8,10},{9,11},{10,... | collective-permute-start | bytes 1474568 | tf_op jit(solution)/shard_map/ppermute | solution.py:22
  80.6 12.7 %collective-permute-start.12 = (bf16[80,3584]{1,0:T(8,128)(2,1)S(1)}, bf16[80,3584]{1,0:T(8,128)(2,1)S(1)}, u32[]{:S(2)}, u32[]{:S(2)}) collective-permute-start(bf16[80,3584]{1,0:T(8,128)(2,1)S(1)} %convolution_convert_fusion.2), channel_id=1, source_target_pairs={{0,4},{1,5},{2,6},{3,7},{4,0},{5,1},{6,2},{7,3},{8,12},{9,13},{10,... | collective-permute-start | bytes 1720328 | tf_op jit(solution)/shard_map/ppermute | solution.py:22
  80.9 1.2 copy-start.2
  80.9 2.9 %collective-permute-start.11 = (bf16[160,3584]{1,0:T(8,128)(2,1)S(1)}, bf16[160,3584]{1,0:T(8,128)(2,1)S(1)}, u32[]{:S(2)}, u32[]{:S(2)}) collective-permute-start(bf16[160,3584]{1,0:T(8,128)(2,1)S(1)} %pad_maximum_fusion.9), channel_id=1, source_target_pairs={{0,1},{1,0},{2,3},{3,2},{4,5},{5,4},{6,7},{7,6},{8,9},{9,8},{10,11... | collective-permute-start | bytes 3440648 | tf_op jit(solution)/shard_map/ppermute | solution.py:22
  93.3 2.9 %collective-permute-start.14 = (bf16[160,3584]{1,0:T(8,128)(2,1)S(1)}, bf16[160,3584]{1,0:T(8,128)(2,1)S(1)}, u32[]{:S(2)}, u32[]{:S(2)}) collective-permute-start(bf16[160,3584]{1,0:T(8,128)(2,1)S(1)} %pad_maximum_fusion.10), channel_id=1, source_target_pairs={{0,1},{1,0},{2,3},{3,2},{4,5},{5,4},{6,7},{7,6},{8,9},{9,8},{10,11... | collective-permute-start | bytes 3440648 | tf_op jit(solution)/shard_map/ppermute | solution.py:22
  93.6 7.2 %collective-permute-start.21 = (bf16[160,3712]{1,0:T(8,128)(2,1)S(1)}, bf16[160,3712]{1,0:T(8,128)(2,1)S(1)}, u32[]{:S(2)}, u32[]{:S(2)}) collective-permute-start(bf16[160,3712]{1,0:T(8,128)(2,1)S(1)} %slice.114), channel_id=1, source_target_pairs={{0,1},{1,0},{2,3},{3,2},{4,5},{5,4},{6,7},{7,6},{8,9},{9,8},{10,11... | collective-permute-start | bytes 3563528 | tf_op jit(solution)/shard_map/ppermute | solution.py:22
  97.2 23.0 %collective-permute-start.18 = (bf16[640,256]{1,0:T(8,128)(2,1)S(1)}, bf16[640,256]{1,0:T(8,128)(2,1)S(1)}, u32[]{:S(2)}, u32[]{:S(2)}) collective-permute-start(bf16[640,256]{1,0:T(8,128)(2,1)S(1)} %pad_maximum_fusion.15), channel_id=1, source_target_pairs={{0,2},{1,3},{2,0},{3,1},{4,6},{5,7},{6,4},{7,5},{8,10},{9,11},{10,... | collective-permute-start | bytes 983048 | tf_op jit(solution)/shard_map/ppermute | solution.py:22
  99.8 19.3 %collective-permute-start.17 = (bf16[320,1536]{1,0:T(8,128)(2,1)S(1)}, bf16[320,1536]{1,0:T(8,128)(2,1)S(1)}, u32[]{:S(2)}, u32[]{:S(2)}) collective-permute-start(bf16[320,1536]{1,0:T(8,128)(2,1)S(1)} %pad_maximum_fusion.11), channel_id=1, source_target_pairs={{0,1},{1,0},{2,3},{3,2},{4,5},{5,4},{6,7},{7,6},{8,9},{9,8},{10,11... | collective-permute-start | bytes 2949128 | tf_op jit(solution)/shard_map/ppermute | solution.py:22
  101.1 16.1 %collective-permute-start.22 = (bf16[80,3712]{1,0:T(8,128)(2,1)S(1)}, bf16[80,3712]{1,0:T(8,128)(2,1)S(1)}, u32[]{:S(2)}, u32[]{:S(2)}) collective-permute-start(bf16[80,3712]{1,0:T(8,128)(2,1)S(1)} %slice.144), channel_id=1, source_target_pairs={{0,4},{1,5},{2,6},{3,7},{4,0},{5,1},{6,2},{7,3},{8,12},{9,13},{10,... | collective-permute-start | bytes 1781768 | tf_op jit(solution)/shard_map/ppermute | solution.py:22
  103.1 18.2 %collective-permute-start.19 = (bf16[160,3712]{1,0:T(8,128)(2,1)S(1)}, bf16[160,3712]{1,0:T(8,128)(2,1)S(1)}, u32[]{:S(2)}, u32[]{:S(2)}) collective-permute-start(bf16[160,3712]{1,0:T(8,128)(2,1)S(1)} %pad_maximum_fusion.6), channel_id=1, source_target_pairs={{0,1},{1,0},{2,3},{3,2},{4,5},{5,4},{6,7},{7,6},{8,9},{9,8},{10,11... | collective-permute-start | bytes 3563528 | tf_op jit(solution)/shard_map/ppermute | solution.py:22
  103.4 24.1 %collective-permute-start.16 = (bf16[128,3584]{1,0:T(8,128)(2,1)S(1)}, bf16[128,3584]{1,0:T(8,128)(2,1)S(1)}, u32[]{:S(2)}, u32[]{:S(2)}) collective-permute-start(bf16[128,3584]{1,0:T(8,128)(2,1)S(1)} %convolution_convert_fusion), channel_id=1, source_target_pairs={{0,2},{1,3},{2,0},{3,1},{4,6},{5,7},{6,4},{7,5},{8,10},{9,11},{10,... | collective-permute-start | bytes 2752520 | tf_op jit(solution)/shard_map/ppermute | solution.py:22
  117.2 33.4 %collective-permute-start.15 = (bf16[2048,256]{1,0:T(8,128)(2,1)S(1)}, bf16[2048,256]{1,0:T(8,128)(2,1)S(1)}, u32[]{:S(2)}, u32[]{:S(2)}) collective-permute-start(bf16[2048,256]{1,0:T(8,128)(2,1)S(1)} %convolution_convert_fusion.5), channel_id=1, source_target_pairs={{0,2},{1,3},{2,0},{3,1},{4,6},{5,7},{6,4},{7,5},{8,10},{9,11},{10,... | collective-permute-start | bytes 3145736 | tf_op jit(solution)/shard_map/ppermute | solution.py:22
  119.1 30.0 %collective-permute-start.23 = (bf16[80,3712]{1,0:T(8,128)(2,1)S(1)}, bf16[80,3712]{1,0:T(8,128)(2,1)S(1)}, u32[]{:S(2)}, u32[]{:S(2)}) collective-permute-start(bf16[80,3712]{1,0:T(8,128)(2,1)S(1)} %add_convert_fusion.2), channel_id=1, source_target_pairs={{0,8},{1,9},{2,10},{3,11},{4,12},{5,13},{6,14},{7,15},{8,0},{9,1},... | collective-permute-start | bytes 1781768 | tf_op jit(solution)/shard_map/ppermute | solution.py:22
  121.7 27.2 %collective-permute-start.20 = (bf16[80,3712]{1,0:T(8,128)(2,1)S(1)}, bf16[80,3712]{1,0:T(8,128)(2,1)S(1)}, u32[]{:S(2)}, u32[]{:S(2)}) collective-permute-start(bf16[80,3712]{1,0:T(8,128)(2,1)S(1)} %slice.142), channel_id=1, source_target_pairs={{0,4},{1,5},{2,6},{3,7},{4,0},{5,1},{6,2},{7,3},{8,12},{9,13},{10,... | collective-permute-start | bytes 1781768 | tf_op jit(solution)/shard_map/ppermute | solution.py:22
  151.7 2.6 %copy-start.1 = (bf16[128,3584]{1,0:T(8,128)(2,1)S(1)}, bf16[128,3584]{1,0:T(8,128)(2,1)}, u32[]{:S(2)}) copy-start(bf16[128,3584]{1,0:T(8,128)(2,1)} %param.7) | copy-start | bytes 2752516

commit v7 on v6

--- a/solution.py
+++ b/solution.py
@@ -7,7 +7,7 @@
 CORE = 1
 WEIGHT_BIT = 2
 ROW_BIT = 4
-SHARED_PART = 3
+SHARED_PART = 13
 
 F32 = jnp.float32
 BF16 = jnp.bfloat16
@@ -46,7 +46,7 @@
     experts = axis_count // SPLIT
     tok_rows, features = tokens.shape
     hid = w_gate.shape[2]
-    shared = features * SHARED_PART // 7 // 128 * 128
+    shared = features * SHARED_PART // 28 // 128 * 128
     capacity = min(tok_rows, 5 * tok_rows // (4 * experts))
     capacity = -(-capacity // 16) * 16
     mine = lax.axis_index("expert") // SPLIT

time: 155 us -> 155 us (level)
  no operation moved by 1% of the time
where the time goes in v7:
time: 155 us
  waiting for transfers between devices  98.7 us (64%)
  starting transfers between devices  23.9 us (15%)
  matrix products  21.1 us (14%)
  other arithmetic  5.04 us (3%)
  local copies, waits for them, and re-layouts  4.71 us (3%)
    ppermute x24, waiting for transfers between devices, flip(): return lax.ppermute(x, 'expert', [(i, i ^ mask) for i in range(n)])  98.7 us
    ppermute x24, starting transfers between devices, flip(): return lax.ppermute(x, 'expert', [(i, i ^ mask) for i in range(n)])  23.9 us
    dot_general x22, matrix products, dot(): lax.dot_general(a, b, (((ca,), (cb,)), ((), ())), preferred_element_type=...  21.1 us
  transfers between devices with their start and end apart: 24, of which 12 were waited for; matrix products, arithmetic and copies ran while one was open for 17% of the time, Pallas kernels for 0%

profile of v7, /device:TPU:0, one launch (start us, length us, event | category | flops | bytes accessed | tf_op | source)
XLA Modules:
  0.0 154.6 jit_solution(7287394323999119971)
XLA Ops:
  0.7 3.0 %collective-permute-start.2 = (bf16[3584,128]{1,0:T(8,128)(2,1)}, bf16[3584,128]{1,0:T(8,128)(2,1)S(1)}, u32[]{:S(2)}, u32[]{:S(2)}) collective-permute-start(bf16[3584,128]{1,0:T(8,128)(2,1)} %bitcast.29), channel_id=1, source_target_pairs={{0,2},{1,3},{2,0},{3,1},{4,6},{5,7},{6,4},{7,5},{8,10},{9,11},{10,... | collective-permute-start | bytes 2752520 | tf_op jit(solution)/shard_map/ppermute | solution.py:22
  3.7 0.7 xor_bitcast_fusion
  4.5 0.7 bitcast_add_fusion
  5.2 1.1 convolution_convert_fusion.3
  6.3 2.6 %collective-permute-start = (bf16[80,3584]{1,0:T(8,128)(2,1)}, bf16[80,3584]{1,0:T(8,128)(2,1)}, u32[]{:S(2)}, u32[]{:S(2)}) collective-permute-start(bf16[80,3584]{1,0:T(8,128)(2,1)} %convolution_convert_fusion.3), channel_id=1, source_target_pairs={{0,8},{1,9},{2,10},{3,11},{4,12},{5,13},{6,14},{7,15},{8,0},{9,1},... | collective-permute-start | bytes 1720328 | tf_op jit(solution)/shard_map/ppermute | solution.py:22
  8.9 0.5 collective-permute-start.6
  9.4 1.1 constant_dynamic-update-slice_fusion.7
  10.6 1.6 %collective-permute-start.1 = (bf16[80,3584]{1,0:T(8,128)(2,1)S(1)}, bf16[80,3584]{1,0:T(8,128)(2,1)S(1)}, u32[]{:S(2)}, u32[]{:S(2)}) collective-permute-start(bf16[80,3584]{1,0:T(8,128)(2,1)S(1)} %get-tuple-element.94), channel_id=1, source_target_pairs={{0,4},{1,5},{2,6},{3,7},{4,0},{5,1},{6,2},{7,3},{8,12},{9,13},{10,... | collective-permute-start | bytes 1720328 | tf_op jit(solution)/shard_map/ppermute | solution.py:22
  12.4 1.6 %convolution_convert_fusion.1 = bf16[80,3584]{1,0:T(8,128)(2,1)S(1)} fusion(bf16[128,3584]{1,0:T(8,128)(2,1)} %param.8, f32[128]{0:T(128)S(1)} %convert_reduce_fusion, pred[160,128]{1,0:T(8,128)(4,1)S(1)} %iota_compare_fusion.1), kind=kOutput, calls=%fused_computation.8 | convolution fusion | flops 75063296 | bytes 1501696 | tf_op jit(solution)/shard_map/dot_general | solution.py:17
  14.1 1.7 %convolution_convert_fusion.2 = bf16[80,3584]{1,0:T(8,128)(2,1)S(1)} fusion(bf16[128,3584]{1,0:T(8,128)(2,1)} %param.8, f32[128]{0:T(128)S(1)} %convert_reduce_fusion, pred[160,128]{1,0:T(8,128)(4,1)S(1)} %iota_compare_fusion.1), kind=kOutput, calls=%fused_computation.9 | convolution fusion | flops 75063296 | bytes 1501696 | tf_op jit(solution)/shard_map/dot_general | solution.py:17
  15.8 18.6 %collective-permute-done = bf16[80,3584]{1,0:T(8,128)(2,1)} collective-permute-done((bf16[80,3584]{1,0:T(8,128)(2,1)}, bf16[80,3584]{1,0:T(8,128)(2,1)}, u32[]{:S(2)}, u32[]{:S(2)}) %collective-permute-start) | collective-permute-done | bytes 573472 | tf_op jit(solution)/shard_map/ppermute | solution.py:22
  34.4 1.3 collective-permute-done.1
  35.8 0.6 collective-permute-start.8
  36.4 2.4 %collective-permute-start.4 = (bf16[80,3584]{1,0:T(8,128)(2,1)}, bf16[80,3584]{1,0:T(8,128)(2,1)S(1)}, u32[]{:S(2)}, u32[]{:S(2)}) collective-permute-start(bf16[80,3584]{1,0:T(8,128)(2,1)} %collective-permute-done), channel_id=1, source_target_pairs={{0,4},{1,5},{2,6},{3,7},{4,0},{5,1},{6,2},{7,3},{8,12},{9,13},{10,... | collective-permute-start | bytes 1720328 | tf_op jit(solution)/shard_map/ppermute | solution.py:22
  38.9 5.0 %collective-permute-done.6 = bf16[3584,128]{1,0:T(8,128)(2,1)S(1)} collective-permute-done((bf16[3584,128]{1,0:T(8,128)(2,1)}, bf16[3584,128]{1,0:T(8,128)(2,1)S(1)}, u32[]{:S(2)}, u32[]{:S(2)}) %collective-permute-start.6) | collective-permute-done | bytes 917536 | tf_op jit(solution)/shard_map/ppermute | solution.py:22
  43.9 1.7 %collective-permute-start.7 = (bf16[128,3584]{1,0:T(8,128)(2,1)S(1)}, bf16[128,3584]{1,0:T(8,128)(2,1)S(1)}, u32[]{:S(2)}, u32[]{:S(2)}) collective-permute-start(bf16[128,3584]{1,0:T(8,128)(2,1)S(1)} %bitcast.34), channel_id=1, source_target_pairs={{0,2},{1,3},{2,0},{3,1},{4,6},{5,7},{6,4},{7,5},{8,10},{9,11},{10,... | collective-permute-start | bytes 2752520 | tf_op jit(solution)/shard_map/ppermute | solution.py:22
  45.7 18.9 %collective-permute-done.4 = bf16[80,3584]{1,0:T(8,128)(2,1)S(1)} collective-permute-done((bf16[80,3584]{1,0:T(8,128)(2,1)}, bf16[80,3584]{1,0:T(8,128)(2,1)S(1)}, u32[]{:S(2)}, u32[]{:S(2)}) %collective-permute-start.4) | collective-permute-done | bytes 573472 | tf_op jit(solution)/shard_map/ppermute | solution.py:22
  64.6 1.4 collective-permute-start.10
  66.1 1.2 constant_dynamic-update-slice_fusion.10
  67.6 9.2 %collective-permute-done.10 = bf16[160,1664]{1,0:T(8,128)(2,1)S(1)} collective-permute-done((bf16[160,1664]{1,0:T(8,128)(2,1)S(1)}, bf16[160,1664]{1,0:T(8,128)(2,1)S(1)}, u32[]{:S(2)}, u32[]{:S(2)}) %collective-permute-start.10) | collective-permute-done | bytes 532512 | tf_op jit(solution)/shard_map/ppermute | solution.py:22
  76.8 2.3 %collective-permute-done.9 = bf16[80,3584]{1,0:T(8,128)(2,1)S(1)} collective-permute-done((bf16[80,3584]{1,0:T(8,128)(2,1)S(1)}, bf16[80,3584]{1,0:T(8,128)(2,1)S(1)}, u32[]{:S(2)}, u32[]{:S(2)}) %collective-permute-start.9) | collective-permute-done | bytes 573472 | tf_op jit(solution)/shard_map/ppermute | solution.py:22
  79.1 1.4 collective-permute-start.13
  80.6 0.3 collective-permute-start.12
  81.0 0.8 fusion.35
  81.8 0.3 copy-done.2
  82.1 0.8 fusion.36
  82.9 0.2 constant_dynamic-update-slice_fusion.8
  83.1 0.8 fusion.66
  83.8 0.8 fusion.6
  84.6 1.0 multiply_convert_fusion.6
  85.6 0.8 fusion.64
  86.4 0.9 fusion
  87.4 0.2 pad_maximum_fusion
  87.6 3.3 %collective-permute-done.13 = bf16[160,1664]{1,0:T(8,128)(2,1)S(1)} collective-permute-done((bf16[160,1664]{1,0:T(8,128)(2,1)S(1)}, bf16[160,1664]{1,0:T(8,128)(2,1)S(1)}, u32[]{:S(2)}, u32[]{:S(2)}) %collective-permute-start.13) | collective-permute-done | bytes 532512 | tf_op jit(solution)/shard_map/ppermute | solution.py:22
  90.9 2.3 %collective-permute-done.12 = bf16[80,3584]{1,0:T(8,128)(2,1)S(1)} collective-permute-done((bf16[80,3584]{1,0:T(8,128)(2,1)S(1)}, bf16[80,3584]{1,0:T(8,128)(2,1)S(1)}, u32[]{:S(2)}, u32[]{:S(2)}) %collective-permute-start.12) | collective-permute-done | bytes 573472 | tf_op jit(solution)/shard_map/ppermute | solution.py:22
  93.6 0.6 collective-permute-start.21
  94.2 2.0 %collective-permute-done.14 = bf16[160,3584]{1,0:T(8,128)(2,1)S(1)} collective-permute-done((bf16[160,3584]{1,0:T(8,128)(2,1)S(1)}, bf16[160,3584]{1,0:T(8,128)(2,1)S(1)}, u32[]{:S(2)}, u32[]{:S(2)}) %collective-permute-start.14) | collective-permute-done | bytes 1146912 | tf_op jit(solution)/shard_map/ppermute | solution.py:22
  96.2 1.0 multiply_reduce_fusion
  97.2 0.3 collective-permute-start.18
  97.8 0.9 convolution_convert_fusion
  98.8 1.0 convolution_convert_fusion.5
  99.8 0.8 fusion.63
  100.7 0.3 add_convert_fusion
  101.1 0.9 collective-permute-start.22
  102.0 0.9 fusion.1
  103.0 0.3 collective-permute-start.19
  103.3 1.7 %collective-permute-start.16 = (bf16[128,3584]{1,0:T(8,128)(2,1)S(1)}, bf16[128,3584]{1,0:T(8,128)(2,1)S(1)}, u32[]{:S(2)}, u32[]{:S(2)}) collective-permute-start(bf16[128,3584]{1,0:T(8,128)(2,1)S(1)} %convolution_convert_fusion), channel_id=1, source_target_pairs={{0,2},{1,3},{2,0},{3,1},{4,6},{5,7},{6,4},{7,5},{8,10},{9,11},{10,... | collective-permute-start | bytes 2752520 | tf_op jit(solution)/shard_map/ppermute | solution.py:22
  105.0 12.2 %collective-permute-done.22 = bf16[80,3712]{1,0:T(8,128)(2,1)S(1)} collective-permute-done((bf16[80,3712]{1,0:T(8,128)(2,1)S(1)}, bf16[80,3712]{1,0:T(8,128)(2,1)S(1)}, u32[]{:S(2)}, u32[]{:S(2)}) %collective-permute-start.22) | collective-permute-done | bytes 593952 | tf_op jit(solution)/shard_map/ppermute | solution.py:22
  117.1 1.7 %collective-permute-start.15 = (bf16[1920,256]{1,0:T(8,128)(2,1)S(1)}, bf16[1920,256]{1,0:T(8,128)(2,1)S(1)}, u32[]{:S(2)}, u32[]{:S(2)}) collective-permute-start(bf16[1920,256]{1,0:T(8,128)(2,1)S(1)} %convolution_convert_fusion.5), channel_id=1, source_target_pairs={{0,2},{1,3},{2,0},{3,1},{4,6},{5,7},{6,4},{7,5},{8,10},{9,11},{10,... | collective-permute-start | bytes 2949128 | tf_op jit(solution)/shard_map/ppermute | solution.py:22
  118.9 0.2 add_convert_fusion.2
  119.0 1.6 %collective-permute-start.23 = (bf16[80,3712]{1,0:T(8,128)(2,1)S(1)}, bf16[80,3712]{1,0:T(8,128)(2,1)S(1)}, u32[]{:S(2)}, u32[]{:S(2)}) collective-permute-start(bf16[80,3712]{1,0:T(8,128)(2,1)S(1)} %add_convert_fusion.2), channel_id=1, source_target_pairs={{0,8},{1,9},{2,10},{3,11},{4,12},{5,13},{6,14},{7,15},{8,0},{9,1},... | collective-permute-start | bytes 1781768 | tf_op jit(solution)/shard_map/ppermute | solution.py:22
  120.7 0.9 fusion.21
  121.6 0.3 add_convert_fusion.1
  122.0 0.9 collective-permute-start.20
  122.9 0.9 fusion.5
  123.8 3.7 %collective-permute-done.16 = bf16[128,3584]{1,0:T(8,128)(2,1)S(1)} collective-permute-done((bf16[128,3584]{1,0:T(8,128)(2,1)S(1)}, bf16[128,3584]{1,0:T(8,128)(2,1)S(1)}, u32[]{:S(2)}, u32[]{:S(2)}) %collective-permute-start.16) | collective-permute-done | bytes 917536 | tf_op jit(solution)/shard_map/ppermute | solution.py:22
  127.5 1.8 %fusion.3 = bf16[1,128,3584]{2,1,0:T(8,128)(2,1)} fusion(bf16[640,3584]{1,0:T(8,128)(2,1)S(1)} %constant_dynamic-update-slice_fusion.11, bf16[128,3584]{1,0:T(8,128)(2,1)S(1)} %collective-permute-done.16, bf16[320,256]{1,0:T(8,128)(2,1)S(1)} %get-tuple-element.85, bf16[320,256]{1,0:T(8,128)(2,1)S(1)} %get-tuple-element.83), kind=kOutput, calls=%fused_computation.7 | convolution fusion | flops 588906496 | bytes 6750208 | tf_op jit(solution)/shard_map/dot_general | solution.py:17
  129.4 19.8 %collective-permute-done.20 = bf16[80,3712]{1,0:T(8,128)(2,1)S(1)} collective-permute-done((bf16[80,3712]{1,0:T(8,128)(2,1)S(1)}, bf16[80,3712]{1,0:T(8,128)(2,1)S(1)}, u32[]{:S(2)}, u32[]{:S(2)}) %collective-permute-start.20) | collective-permute-done | bytes 593952 | tf_op jit(solution)/shard_map/ppermute | solution.py:22
  149.4 0.5 fusion.30
  149.8 1.0 slice.202
  150.9 1.0 fusion.4
  152.0 0.6 copy.15
  152.6 1.0 maximum_bitcast_fusion.1
  153.6 1.0 maximum_bitcast_fusion
  (64 shorter events, 2.8 us)
Async XLA Ops:
  0.6 4.5 %copy-start = (bf16[128,3584]{1,0:T(8,128)(2,1)S(1)}, bf16[128,3584]{1,0:T(8,128)(2,1)}, u32[]{:S(2)}) copy-start(bf16[128,3584]{1,0:T(8,128)(2,1)} %param.7) | copy-start | bytes 2752516
  0.6 11.5 %copy-start.5 = (bf16[128,1]{0,1:T(2,128)(2,1)S(1)}, bf16[128,1]{0,1:T(2,128)(2,1)}, u32[]{:S(2)}) copy-start(bf16[128,1]{0,1:T(2,128)(2,1)} %param.9) | copy-start | bytes 772
  0.7 35.0 %collective-permute-start.2 = (bf16[3584,128]{1,0:T(8,128)(2,1)}, bf16[3584,128]{1,0:T(8,128)(2,1)S(1)}, u32[]{:S(2)}, u32[]{:S(2)}) collective-permute-start(bf16[3584,128]{1,0:T(8,128)(2,1)} %bitcast.29), channel_id=1, source_target_pairs={{0,2},{1,3},{2,0},{3,1},{4,6},{5,7},{6,4},{7,5},{8,10},{9,11},{10,... | collective-permute-start | bytes 2752520 | tf_op jit(solution)/shard_map/ppermute | solution.py:22
  6.3 28.0 %collective-permute-start = (bf16[80,3584]{1,0:T(8,128)(2,1)}, bf16[80,3584]{1,0:T(8,128)(2,1)}, u32[]{:S(2)}, u32[]{:S(2)}) collective-permute-start(bf16[80,3584]{1,0:T(8,128)(2,1)} %convolution_convert_fusion.3), channel_id=1, source_target_pairs={{0,8},{1,9},{2,10},{3,11},{4,12},{5,13},{6,14},{7,15},{8,0},{9,1},... | collective-permute-start | bytes 1720328 | tf_op jit(solution)/shard_map/ppermute | solution.py:22
  8.9 35.0 %collective-permute-start.6 = (bf16[3584,128]{1,0:T(8,128)(2,1)}, bf16[3584,128]{1,0:T(8,128)(2,1)S(1)}, u32[]{:S(2)}, u32[]{:S(2)}) collective-permute-start(bf16[3584,128]{1,0:T(8,128)(2,1)} %bitcast.24), channel_id=1, source_target_pairs={{0,2},{1,3},{2,0},{3,1},{4,6},{5,7},{6,4},{7,5},{8,10},{9,11},{10,... | collective-permute-start | bytes 2752520 | tf_op jit(solution)/shard_map/ppermute | solution.py:22
  10.6 25.0 %collective-permute-start.1 = (bf16[80,3584]{1,0:T(8,128)(2,1)S(1)}, bf16[80,3584]{1,0:T(8,128)(2,1)S(1)}, u32[]{:S(2)}, u32[]{:S(2)}) collective-permute-start(bf16[80,3584]{1,0:T(8,128)(2,1)S(1)} %get-tuple-element.94), channel_id=1, source_target_pairs={{0,4},{1,5},{2,6},{3,7},{4,0},{5,1},{6,2},{7,3},{8,12},{9,13},{10,... | collective-permute-start | bytes 1720328 | tf_op jit(solution)/shard_map/ppermute | solution.py:22
  12.4 31.5 %copy-start.6 = (bf16[1,128,3584]{2,1,0:T(8,128)(2,1)S(1)}, bf16[1,128,3584]{2,1,0:T(8,128)(2,1)}, u32[]{:S(2)}) copy-start(bf16[1,128,3584]{2,1,0:T(8,128)(2,1)} %param.13) | copy-start | bytes 2752516
  14.1 31.6 %copy-start.4 = (bf16[640,3584]{1,0:T(8,128)(2,1)S(1)}, bf16[640,3584]{1,0:T(8,128)(2,1)}, u32[]{:S(2)}) copy-start(bf16[640,3584]{1,0:T(8,128)(2,1)} %get-tuple-element.93) | copy-start | bytes 13762564
  35.7 30.4 %collective-permute-start.3 = (bf16[160,3584]{1,0:T(8,128)(2,1)S(1)}, bf16[160,3584]{1,0:T(8,128)(2,1)S(1)}, u32[]{:S(2)}, u32[]{:S(2)}) collective-permute-start(bf16[160,3584]{1,0:T(8,128)(2,1)S(1)} %pad_maximum_fusion.5), channel_id=1, source_target_pairs={{0,1},{1,0},{2,3},{3,2},{4,5},{5,4},{6,7},{7,6},{8,9},{9,8},{10,11... | collective-permute-start | bytes 3440648 | tf_op jit(solution)/shard_map/ppermute | solution.py:22
  35.8 30.3 %collective-permute-start.8 = (bf16[80,3584]{1,0:T(8,128)(2,1)S(1)}, bf16[80,3584]{1,0:T(8,128)(2,1)S(1)}, u32[]{:S(2)}, u32[]{:S(2)}) collective-permute-start(bf16[80,3584]{1,0:T(8,128)(2,1)S(1)} %convolution_convert_fusion.1), channel_id=1, source_target_pairs={{0,8},{1,9},{2,10},{3,11},{4,12},{5,13},{6,14},{7,15},{8,0},{9,1},... | collective-permute-start | bytes 1720328 | tf_op jit(solution)/shard_map/ppermute | solution.py:22
  36.4 28.2 %collective-permute-start.4 = (bf16[80,3584]{1,0:T(8,128)(2,1)}, bf16[80,3584]{1,0:T(8,128)(2,1)S(1)}, u32[]{:S(2)}, u32[]{:S(2)}) collective-permute-start(bf16[80,3584]{1,0:T(8,128)(2,1)} %collective-permute-done), channel_id=1, source_target_pairs={{0,4},{1,5},{2,6},{3,7},{4,0},{5,1},{6,2},{7,3},{8,12},{9,13},{10,... | collective-permute-start | bytes 1720328 | tf_op jit(solution)/shard_map/ppermute | solution.py:22
  43.9 23.7 %collective-permute-start.7 = (bf16[128,3584]{1,0:T(8,128)(2,1)S(1)}, bf16[128,3584]{1,0:T(8,128)(2,1)S(1)}, u32[]{:S(2)}, u32[]{:S(2)}) collective-permute-start(bf16[128,3584]{1,0:T(8,128)(2,1)S(1)} %bitcast.34), channel_id=1, source_target_pairs={{0,2},{1,3},{2,0},{3,1},{4,6},{5,7},{6,4},{7,5},{8,10},{9,11},{10,... | collective-permute-start | bytes 2752520 | tf_op jit(solution)/shard_map/ppermute | solution.py:22
  64.6 12.2 %collective-permute-start.10 = (bf16[160,1664]{1,0:T(8,128)(2,1)S(1)}, bf16[160,1664]{1,0:T(8,128)(2,1)S(1)}, u32[]{:S(2)}, u32[]{:S(2)}) collective-permute-start(bf16[160,1664]{1,0:T(8,128)(2,1)S(1)} %fusion.39), channel_id=1, source_target_pairs={{0,2},{1,3},{2,0},{3,1},{4,6},{5,7},{6,4},{7,5},{8,10},{9,11},{10,... | collective-permute-start | bytes 1597448 | tf_op jit(solution)/shard_map/ppermute | solution.py:22
  66.0 13.1 %collective-permute-start.9 = (bf16[80,3584]{1,0:T(8,128)(2,1)S(1)}, bf16[80,3584]{1,0:T(8,128)(2,1)S(1)}, u32[]{:S(2)}, u32[]{:S(2)}) collective-permute-start(bf16[80,3584]{1,0:T(8,128)(2,1)S(1)} %collective-permute-done.8), channel_id=1, source_target_pairs={{0,4},{1,5},{2,6},{3,7},{4,0},{5,1},{6,2},{7,3},{8,12},{9,13},{10,... | collective-permute-start | bytes 1720328 | tf_op jit(solution)/shard_map/ppermute | solution.py:22
  67.3 13.7 %copy-start.3 = (bf16[1,3584,128]{2,1,0:T(8,128)(2,1)S(1)}, bf16[1,3584,128]{2,1,0:T(8,128)(2,1)}, u32[]{:S(2)}) copy-start(bf16[1,3584,128]{2,1,0:T(8,128)(2,1)} %param.11) | copy-start | bytes 2752516
  67.5 15.4 %collective-permute-start.5 = (bf16[160,3584]{1,0:T(8,128)(2,1)S(1)}, bf16[160,3584]{1,0:T(8,128)(2,1)S(1)}, u32[]{:S(2)}, u32[]{:S(2)}) collective-permute-start(bf16[160,3584]{1,0:T(8,128)(2,1)S(1)} %get-tuple-element.89), channel_id=1, source_target_pairs={{0,1},{1,0},{2,3},{3,2},{4,5},{5,4},{6,7},{7,6},{8,9},{9,8},{10,11... | collective-permute-start | bytes 3440648 | tf_op jit(solution)/shard_map/ppermute | solution.py:22
  79.1 11.8 %collective-permute-start.13 = (bf16[160,1664]{1,0:T(8,128)(2,1)S(1)}, bf16[160,1664]{1,0:T(8,128)(2,1)S(1)}, u32[]{:S(2)}, u32[]{:S(2)}) collective-permute-start(bf16[160,1664]{1,0:T(8,128)(2,1)S(1)} %slice.129), channel_id=1, source_target_pairs={{0,2},{1,3},{2,0},{3,1},{4,6},{5,7},{6,4},{7,5},{8,10},{9,11},{10,... | collective-permute-start | bytes 1597448 | tf_op jit(solution)/shard_map/ppermute | solution.py:22
  80.6 12.7 %collective-permute-start.12 = (bf16[80,3584]{1,0:T(8,128)(2,1)S(1)}, bf16[80,3584]{1,0:T(8,128)(2,1)S(1)}, u32[]{:S(2)}, u32[]{:S(2)}) collective-permute-start(bf16[80,3584]{1,0:T(8,128)(2,1)S(1)} %convolution_convert_fusion.2), channel_id=1, source_target_pairs={{0,4},{1,5},{2,6},{3,7},{4,0},{5,1},{6,2},{7,3},{8,12},{9,13},{10,... | collective-permute-start | bytes 1720328 | tf_op jit(solution)/shard_map/ppermute | solution.py:22
  80.9 1.2 copy-start.2
  80.9 2.9 %collective-permute-start.11 = (bf16[160,3584]{1,0:T(8,128)(2,1)S(1)}, bf16[160,3584]{1,0:T(8,128)(2,1)S(1)}, u32[]{:S(2)}, u32[]{:S(2)}) collective-permute-start(bf16[160,3584]{1,0:T(8,128)(2,1)S(1)} %pad_maximum_fusion.9), channel_id=1, source_target_pairs={{0,1},{1,0},{2,3},{3,2},{4,5},{5,4},{6,7},{7,6},{8,9},{9,8},{10,11... | collective-permute-start | bytes 3440648 | tf_op jit(solution)/shard_map/ppermute | solution.py:22
  93.3 2.9 %collective-permute-start.14 = (bf16[160,3584]{1,0:T(8,128)(2,1)S(1)}, bf16[160,3584]{1,0:T(8,128)(2,1)S(1)}, u32[]{:S(2)}, u32[]{:S(2)}) collective-permute-start(bf16[160,3584]{1,0:T(8,128)(2,1)S(1)} %pad_maximum_fusion.10), channel_id=1, source_target_pairs={{0,1},{1,0},{2,3},{3,2},{4,5},{5,4},{6,7},{7,6},{8,9},{9,8},{10,11... | collective-permute-start | bytes 3440648 | tf_op jit(solution)/shard_map/ppermute | solution.py:22
  93.6 7.2 %collective-permute-start.21 = (bf16[160,3712]{1,0:T(8,128)(2,1)S(1)}, bf16[160,3712]{1,0:T(8,128)(2,1)S(1)}, u32[]{:S(2)}, u32[]{:S(2)}) collective-permute-start(bf16[160,3712]{1,0:T(8,128)(2,1)S(1)} %slice.114), channel_id=1, source_target_pairs={{0,1},{1,0},{2,3},{3,2},{4,5},{5,4},{6,7},{7,6},{8,9},{9,8},{10,11... | collective-permute-start | bytes 3563528 | tf_op jit(solution)/shard_map/ppermute | solution.py:22
  97.2 23.5 %collective-permute-start.18 = (bf16[640,256]{1,0:T(8,128)(2,1)S(1)}, bf16[640,256]{1,0:T(8,128)(2,1)S(1)}, u32[]{:S(2)}, u32[]{:S(2)}) collective-permute-start(bf16[640,256]{1,0:T(8,128)(2,1)S(1)} %pad_maximum_fusion.15), channel_id=1, source_target_pairs={{0,2},{1,3},{2,0},{3,1},{4,6},{5,7},{6,4},{7,5},{8,10},{9,11},{10,... | collective-permute-start | bytes 983048 | tf_op jit(solution)/shard_map/ppermute | solution.py:22
  99.7 19.3 %collective-permute-start.17 = (bf16[320,1664]{1,0:T(8,128)(2,1)S(1)}, bf16[320,1664]{1,0:T(8,128)(2,1)S(1)}, u32[]{:S(2)}, u32[]{:S(2)}) collective-permute-start(bf16[320,1664]{1,0:T(8,128)(2,1)S(1)} %pad_maximum_fusion.11), channel_id=1, source_target_pairs={{0,1},{1,0},{2,3},{3,2},{4,5},{5,4},{6,7},{7,6},{8,9},{9,8},{10,11... | collective-permute-start | bytes 3194888 | tf_op jit(solution)/shard_map/ppermute | solution.py:22
  101.1 16.1 %collective-permute-start.22 = (bf16[80,3712]{1,0:T(8,128)(2,1)S(1)}, bf16[80,3712]{1,0:T(8,128)(2,1)S(1)}, u32[]{:S(2)}, u32[]{:S(2)}) collective-permute-start(bf16[80,3712]{1,0:T(8,128)(2,1)S(1)} %slice.144), channel_id=1, source_target_pairs={{0,4},{1,5},{2,6},{3,7},{4,0},{5,1},{6,2},{7,3},{8,12},{9,13},{10,... | collective-permute-start | bytes 1781768 | tf_op jit(solution)/shard_map/ppermute | solution.py:22
  103.0 18.6 %collective-permute-start.19 = (bf16[160,3712]{1,0:T(8,128)(2,1)S(1)}, bf16[160,3712]{1,0:T(8,128)(2,1)S(1)}, u32[]{:S(2)}, u32[]{:S(2)}) collective-permute-start(bf16[160,3712]{1,0:T(8,128)(2,1)S(1)} %pad_maximum_fusion.6), channel_id=1, source_target_pairs={{0,1},{1,0},{2,3},{3,2},{4,5},{5,4},{6,7},{7,6},{8,9},{9,8},{10,11... | collective-permute-start | bytes 3563528 | tf_op jit(solution)/shard_map/ppermute | solution.py:22
  103.3 24.2 %collective-permute-start.16 = (bf16[128,3584]{1,0:T(8,128)(2,1)S(1)}, bf16[128,3584]{1,0:T(8,128)(2,1)S(1)}, u32[]{:S(2)}, u32[]{:S(2)}) collective-permute-start(bf16[128,3584]{1,0:T(8,128)(2,1)S(1)} %convolution_convert_fusion), channel_id=1, source_target_pairs={{0,2},{1,3},{2,0},{3,1},{4,6},{5,7},{6,4},{7,5},{8,10},{9,11},{10,... | collective-permute-start | bytes 2752520 | tf_op jit(solution)/shard_map/ppermute | solution.py:22
  117.1 33.8 %collective-permute-start.15 = (bf16[1920,256]{1,0:T(8,128)(2,1)S(1)}, bf16[1920,256]{1,0:T(8,128)(2,1)S(1)}, u32[]{:S(2)}, u32[]{:S(2)}) collective-permute-start(bf16[1920,256]{1,0:T(8,128)(2,1)S(1)} %convolution_convert_fusion.5), channel_id=1, source_target_pairs={{0,2},{1,3},{2,0},{3,1},{4,6},{5,7},{6,4},{7,5},{8,10},{9,11},{10,... | collective-permute-start | bytes 2949128 | tf_op jit(solution)/shard_map/ppermute | solution.py:22
  119.0 30.3 %collective-permute-start.23 = (bf16[80,3712]{1,0:T(8,128)(2,1)S(1)}, bf16[80,3712]{1,0:T(8,128)(2,1)S(1)}, u32[]{:S(2)}, u32[]{:S(2)}) collective-permute-start(bf16[80,3712]{1,0:T(8,128)(2,1)S(1)} %add_convert_fusion.2), channel_id=1, source_target_pairs={{0,8},{1,9},{2,10},{3,11},{4,12},{5,13},{6,14},{7,15},{8,0},{9,1},... | collective-permute-start | bytes 1781768 | tf_op jit(solution)/shard_map/ppermute | solution.py:22
  122.0 27.2 %collective-permute-start.20 = (bf16[80,3712]{1,0:T(8,128)(2,1)S(1)}, bf16[80,3712]{1,0:T(8,128)(2,1)S(1)}, u32[]{:S(2)}, u32[]{:S(2)}) collective-permute-start(bf16[80,3712]{1,0:T(8,128)(2,1)S(1)} %slice.142), channel_id=1, source_target_pairs={{0,4},{1,5},{2,6},{3,7},{4,0},{5,1},{6,2},{7,3},{8,12},{9,13},{10,... | collective-permute-start | bytes 1781768 | tf_op jit(solution)/shard_map/ppermute | solution.py:22
  152.0 2.6 %copy-start.1 = (bf16[128,3584]{1,0:T(8,128)(2,1)S(1)}, bf16[128,3584]{1,0:T(8,128)(2,1)}, u32[]{:S(2)}) copy-start(bf16[128,3584]{1,0:T(8,128)(2,1)} %param.7) | copy-start | bytes 2752516

commit v8 on v6

--- a/solution.py
+++ b/solution.py
@@ -148,9 +148,9 @@
     got_down = flip(down_p, WEIGHT_BIT)
 
     slot_rows = jnp.concatenate([near_rows] + back, axis=0)
-    out = dot(select, slot_rows, 0, 0)
-    grad_tokens = out[:, :features].astype(BF16)
-    grad_combine = out[:, features : features + 1] / weight
+    grad_tokens = dot(select, slot_rows[:, :features], 0, 0).astype(BF16)
+    prob = dot(slot_rows[:, features:], select, 0, 0)[:1]
+    grad_combine = (prob / weight.reshape(1, tok_rows)).reshape(tok_rows, 1)
 
     first = (dot(x[:, :shared], both, 0, 0) + dot(x_p, got_both, 0, 0)).astype(BF16)
     got_down, first = lax.optimization_barrier((got_down, first))

time: 155 us -> 153 us (0.987)
  local copies, waits for them, and re-layouts: 4.67 us -> 1.87 us
  waiting for transfers between devices: 98.2 us -> 101 us
  matrix products: 21.3 us -> 18.7 us
  starting transfers between devices: 24 us -> 25.6 us
    ppermute x24, waiting for transfers between devices: 98.2 us -> 101 us  [flip(): return lax.ppermute(x, 'expert', [(i, i ^ mask) for i in range(n)])]
    dot_general x22 -> x23, matrix products: 21.3 us -> 18.7 us  [dot(): lax.dot_general(a, b, (((ca,), (cb,)), ((), ())), preferred_element_type=...]
    unnamed x25 -> x23, local copies, waits for them, and re-layouts: 2.73 us -> 0.95 us
    ppermute x24, starting transfers between devices: 24 us -> 25.6 us  [flip(): return lax.ppermute(x, 'expert', [(i, i ^ mask) for i in range(n)])]
  transfers between devices with their start and end apart: 24 -> 24, of which waited for: 12 -> 13; matrix products, arithmetic and copies ran while one was open for 17% -> 13% of each run, Pallas kernels for 0% -> 0%
where the time goes in v8:
time: 153 us
  waiting for transfers between devices  101 us (66%)
  starting transfers between devices  25.6 us (17%)
  matrix products  18.7 us (12%)
  other arithmetic  5.03 us (3%)
  local copies, waits for them, and re-layouts  1.87 us (1%)
    ppermute x24, waiting for transfers between devices, flip(): return lax.ppermute(x, 'expert', [(i, i ^ mask) for i in range(n)])  101 us
    ppermute x24, starting transfers between devices, flip(): return lax.ppermute(x, 'expert', [(i, i ^ mask) for i in range(n)])  25.6 us
    dot_general x23, matrix products, dot(): lax.dot_general(a, b, (((ca,), (cb,)), ((), ())), preferred_element_type=...  18.7 us
  transfers between devices with their start and end apart: 24, of which 13 were waited for; matrix products, arithmetic and copies ran while one was open for 13% of the time, Pallas kernels for 0%

profile of v8, /device:TPU:0, one launch (start us, length us, event | category | flops | bytes accessed | tf_op | source)
XLA Modules:
  0.0 153.2 jit_solution(3171935366154806865)
XLA Ops:
  0.7 0.8 xor_bitcast_fusion
  1.6 0.7 bitcast_add_fusion
  2.3 0.3 convolution_convert_fusion.4
  2.6 4.1 %collective-permute-start = (bf16[80,3584]{1,0:T(8,128)(2,1)S(1)}, bf16[80,3584]{1,0:T(8,128)(2,1)S(1)}, u32[]{:S(2)}, u32[]{:S(2)}) collective-permute-start(bf16[80,3584]{1,0:T(8,128)(2,1)S(1)} %convolution_convert_fusion.4), channel_id=1, source_target_pairs={{0,8},{1,9},{2,10},{3,11},{4,12},{5,13},{6,14},{7,15},{8,0},{9,1},... | collective-permute-start | bytes 1720328 | tf_op jit(solution)/shard_map/ppermute | solution.py:22
  6.7 1.5 collective-permute-start.2
  8.2 0.5 collective-permute-start.6
  8.8 0.3 constant_dynamic-update-slice_fusion.7
  9.1 1.6 %collective-permute-start.1 = (bf16[80,3584]{1,0:T(8,128)(2,1)S(1)}, bf16[80,3584]{1,0:T(8,128)(2,1)S(1)}, u32[]{:S(2)}, u32[]{:S(2)}) collective-permute-start(bf16[80,3584]{1,0:T(8,128)(2,1)S(1)} %get-tuple-element.84), channel_id=1, source_target_pairs={{0,4},{1,5},{2,6},{3,7},{4,0},{5,1},{6,2},{7,3},{8,12},{9,13},{10,... | collective-permute-start | bytes 1720328 | tf_op jit(solution)/shard_map/ppermute | solution.py:22
  10.7 0.4 convolution_convert_fusion.3
  11.1 0.4 convolution_convert_fusion.2
  11.5 20.6 %collective-permute-done = bf16[80,3584]{1,0:T(8,128)(2,1)S(1)} collective-permute-done((bf16[80,3584]{1,0:T(8,128)(2,1)S(1)}, bf16[80,3584]{1,0:T(8,128)(2,1)S(1)}, u32[]{:S(2)}, u32[]{:S(2)}) %collective-permute-start) | collective-permute-done | bytes 573472 | tf_op jit(solution)/shard_map/ppermute | solution.py:22
  32.1 2.0 %collective-permute-done.1 = bf16[80,3584]{1,0:T(8,128)(2,1)S(1)} collective-permute-done((bf16[80,3584]{1,0:T(8,128)(2,1)S(1)}, bf16[80,3584]{1,0:T(8,128)(2,1)S(1)}, u32[]{:S(2)}, u32[]{:S(2)}) %collective-permute-start.1) | collective-permute-done | bytes 573472 | tf_op jit(solution)/shard_map/ppermute | solution.py:22
  34.3 0.6 collective-permute-start.8
  34.9 2.5 %collective-permute-start.4 = (bf16[80,3584]{1,0:T(8,128)(2,1)S(1)}, bf16[80,3584]{1,0:T(8,128)(2,1)S(1)}, u32[]{:S(2)}, u32[]{:S(2)}) collective-permute-start(bf16[80,3584]{1,0:T(8,128)(2,1)S(1)} %collective-permute-done), channel_id=1, source_target_pairs={{0,4},{1,5},{2,6},{3,7},{4,0},{5,1},{6,2},{7,3},{8,12},{9,13},{10,... | collective-permute-start | bytes 1720328 | tf_op jit(solution)/shard_map/ppermute | solution.py:22
  37.4 11.0 %collective-permute-done.6 = bf16[3584,128]{1,0:T(8,128)(2,1)S(1)} collective-permute-done((bf16[3584,128]{1,0:T(8,128)(2,1)}, bf16[3584,128]{1,0:T(8,128)(2,1)S(1)}, u32[]{:S(2)}, u32[]{:S(2)}) %collective-permute-start.6) | collective-permute-done | bytes 917536 | tf_op jit(solution)/shard_map/ppermute | solution.py:22
  48.4 1.5 collective-permute-start.7
  50.0 13.0 %collective-permute-done.4 = bf16[80,3584]{1,0:T(8,128)(2,1)S(1)} collective-permute-done((bf16[80,3584]{1,0:T(8,128)(2,1)S(1)}, bf16[80,3584]{1,0:T(8,128)(2,1)S(1)}, u32[]{:S(2)}, u32[]{:S(2)}) %collective-permute-start.4) | collective-permute-done | bytes 573472 | tf_op jit(solution)/shard_map/ppermute | solution.py:22
  63.0 1.5 collective-permute-start.10
  65.0 6.8 %collective-permute-done.7 = bf16[128,3584]{1,0:T(8,128)(2,1)S(1)} collective-permute-done((bf16[128,3584]{1,0:T(8,128)(2,1)S(1)}, bf16[128,3584]{1,0:T(8,128)(2,1)S(1)}, u32[]{:S(2)}, u32[]{:S(2)}) %collective-permute-start.7) | collective-permute-done | bytes 917536 | tf_op jit(solution)/shard_map/ppermute | solution.py:22
  71.7 8.1 %collective-permute-done.10 = bf16[160,1536]{1,0:T(8,128)(2,1)S(1)} collective-permute-done((bf16[160,1536]{1,0:T(8,128)(2,1)S(1)}, bf16[160,1536]{1,0:T(8,128)(2,1)S(1)}, u32[]{:S(2)}, u32[]{:S(2)}) %collective-permute-start.10) | collective-permute-done | bytes 491552 | tf_op jit(solution)/shard_map/ppermute | solution.py:22
  79.9 1.5 collective-permute-start.13
  81.4 1.6 %collective-permute-start.12 = (bf16[80,3584]{1,0:T(8,128)(2,1)S(1)}, bf16[80,3584]{1,0:T(8,128)(2,1)S(1)}, u32[]{:S(2)}, u32[]{:S(2)}) collective-permute-start(bf16[80,3584]{1,0:T(8,128)(2,1)S(1)} %convolution_convert_fusion.3), channel_id=1, source_target_pairs={{0,4},{1,5},{2,6},{3,7},{4,0},{5,1},{6,2},{7,3},{8,12},{9,13},{10,... | collective-permute-start | bytes 1720328 | tf_op jit(solution)/shard_map/ppermute | solution.py:22
  83.1 0.8 fusion.34
  83.9 0.3 copy-done.2
  84.2 0.8 fusion.35
  85.0 0.2 constant_dynamic-update-slice_fusion.8
  85.2 0.8 fusion.69
  85.9 0.8 fusion.8
  86.7 1.0 multiply_convert_fusion.6
  87.7 0.8 fusion.67
  88.5 0.9 fusion
  89.5 0.2 pad_maximum_fusion
  89.7 1.0 collective-permute-done.13
  90.7 3.0 %collective-permute-done.12 = bf16[80,3584]{1,0:T(8,128)(2,1)S(1)} collective-permute-done((bf16[80,3584]{1,0:T(8,128)(2,1)S(1)}, bf16[80,3584]{1,0:T(8,128)(2,1)S(1)}, u32[]{:S(2)}, u32[]{:S(2)}) %collective-permute-start.12) | collective-permute-done | bytes 573472 | tf_op jit(solution)/shard_map/ppermute | solution.py:22
  94.0 0.6 collective-permute-start.21
  94.7 2.0 %collective-permute-done.14 = bf16[160,3584]{1,0:T(8,128)(2,1)S(1)} collective-permute-done((bf16[160,3584]{1,0:T(8,128)(2,1)S(1)}, bf16[160,3584]{1,0:T(8,128)(2,1)S(1)}, u32[]{:S(2)}, u32[]{:S(2)}) %collective-permute-start.14) | collective-permute-done | bytes 1146912 | tf_op jit(solution)/shard_map/ppermute | solution.py:22
  96.6 0.9 multiply_reduce_fusion
  97.7 0.6 collective-permute-start.18
  98.5 0.9 convolution_convert_fusion.1
  99.4 1.0 convolution_convert_fusion.6
  100.6 0.8 fusion.66
  101.4 0.3 add_convert_fusion
  101.8 1.8 %collective-permute-start.22 = (bf16[80,3712]{1,0:T(8,128)(2,1)S(1)}, bf16[80,3712]{1,0:T(8,128)(2,1)S(1)}, u32[]{:S(2)}, u32[]{:S(2)}) collective-permute-start(bf16[80,3712]{1,0:T(8,128)(2,1)S(1)} %slice.150), channel_id=1, source_target_pairs={{0,4},{1,5},{2,6},{3,7},{4,0},{5,1},{6,2},{7,3},{8,12},{9,13},{10,... | collective-permute-start | bytes 1781768 | tf_op jit(solution)/shard_map/ppermute | solution.py:22
  103.6 0.9 fusion.1
  104.7 0.3 collective-permute-start.19
  104.9 1.5 collective-permute-start.16
  106.5 11.4 %collective-permute-done.22 = bf16[80,3712]{1,0:T(8,128)(2,1)S(1)} collective-permute-done((bf16[80,3712]{1,0:T(8,128)(2,1)S(1)}, bf16[80,3712]{1,0:T(8,128)(2,1)S(1)}, u32[]{:S(2)}, u32[]{:S(2)}) %collective-permute-start.22) | collective-permute-done | bytes 593952 | tf_op jit(solution)/shard_map/ppermute | solution.py:22
  117.8 1.5 collective-permute-start.15
  119.3 0.2 add_convert_fusion.2
  119.5 0.5 collective-permute-start.23
  120.0 1.1 fusion.21
  121.1 0.3 add_convert_fusion.1
  121.5 1.7 %collective-permute-start.20 = (bf16[80,3712]{1,0:T(8,128)(2,1)S(1)}, bf16[80,3712]{1,0:T(8,128)(2,1)S(1)}, u32[]{:S(2)}, u32[]{:S(2)}) collective-permute-start(bf16[80,3712]{1,0:T(8,128)(2,1)S(1)} %slice.148), channel_id=1, source_target_pairs={{0,4},{1,5},{2,6},{3,7},{4,0},{5,1},{6,2},{7,3},{8,12},{9,13},{10,... | collective-permute-start | bytes 1781768 | tf_op jit(solution)/shard_map/ppermute | solution.py:22
  123.2 0.9 fusion.5
  124.0 4.1 %collective-permute-done.16 = bf16[128,3584]{1,0:T(8,128)(2,1)S(1)} collective-permute-done((bf16[128,3584]{1,0:T(8,128)(2,1)S(1)}, bf16[128,3584]{1,0:T(8,128)(2,1)S(1)}, u32[]{:S(2)}, u32[]{:S(2)}) %collective-permute-start.16) | collective-permute-done | bytes 917536 | tf_op jit(solution)/shard_map/ppermute | solution.py:22
  128.1 1.8 %fusion.3 = bf16[1,128,3584]{2,1,0:T(8,128)(2,1)} fusion(bf16[640,3584]{1,0:T(8,128)(2,1)S(1)} %constant_dynamic-update-slice_fusion.11, bf16[128,3584]{1,0:T(8,128)(2,1)S(1)} %collective-permute-done.16, bf16[320,256]{1,0:T(8,128)(2,1)S(1)} %get-tuple-element.75, bf16[320,256]{1,0:T(8,128)(2,1)S(1)} %get-tuple-element.73), kind=kOutput, calls=%fused_computation.8 | convolution fusion | flops 588906496 | bytes 6750208 | tf_op jit(solution)/shard_map/dot_general | solution.py:17
  129.9 15.0 %collective-permute-done.20 = bf16[80,3712]{1,0:T(8,128)(2,1)S(1)} collective-permute-done((bf16[80,3712]{1,0:T(8,128)(2,1)S(1)}, bf16[80,3712]{1,0:T(8,128)(2,1)S(1)}, u32[]{:S(2)}, u32[]{:S(2)}) %collective-permute-start.20) | collective-permute-done | bytes 593952 | tf_op jit(solution)/shard_map/ppermute | solution.py:22
  145.0 0.1 add_convert_fusion.3
  145.1 2.8 %collective-permute-done.23 = bf16[80,3712]{1,0:T(8,128)(2,1)S(1)} collective-permute-done((bf16[80,3712]{1,0:T(8,128)(2,1)S(1)}, bf16[80,3712]{1,0:T(8,128)(2,1)S(1)}, u32[]{:S(2)}, u32[]{:S(2)}) %collective-permute-start.23) | collective-permute-done | bytes 593952 | tf_op jit(solution)/shard_map/ppermute | solution.py:22
  147.9 0.7 fusion.33
  148.6 1.4 convolution_convert_fusion
  150.0 1.1 fusion.4
  151.2 1.0 maximum_bitcast_fusion.1
  152.2 1.0 maximum_bitcast_fusion
  (61 shorter events, 2.4 us)
Async XLA Ops:
  0.6 1.7 %copy-start = (bf16[128,3584]{1,0:T(8,128)(2,1)S(1)}, bf16[128,3584]{1,0:T(8,128)(2,1)}, u32[]{:S(2)}) copy-start(bf16[128,3584]{1,0:T(8,128)(2,1)} %param.7) | copy-start | bytes 2752516
  0.6 10.1 %copy-start.5 = (bf16[128,1]{0,1:T(2,128)(2,1)S(1)}, bf16[128,1]{0,1:T(2,128)(2,1)}, u32[]{:S(2)}) copy-start(bf16[128,1]{0,1:T(2,128)(2,1)} %param.9) | copy-start | bytes 772
  0.7 10.1 %copy-start.4 = (bf16[128,3584]{1,0:T(8,128)(2,1)S(1)}, bf16[128,3584]{1,0:T(8,128)(2,1)}, u32[]{:S(2)}) copy-start(bf16[128,3584]{1,0:T(8,128)(2,1)} %param.8) | copy-start | bytes 2752516
  2.6 29.5 %collective-permute-start = (bf16[80,3584]{1,0:T(8,128)(2,1)S(1)}, bf16[80,3584]{1,0:T(8,128)(2,1)S(1)}, u32[]{:S(2)}, u32[]{:S(2)}) collective-permute-start(bf16[80,3584]{1,0:T(8,128)(2,1)S(1)} %convolution_convert_fusion.4), channel_id=1, source_target_pairs={{0,8},{1,9},{2,10},{3,11},{4,12},{5,13},{6,14},{7,15},{8,0},{9,1},... | collective-permute-start | bytes 1720328 | tf_op jit(solution)/shard_map/ppermute | solution.py:22
  6.7 27.4 %collective-permute-start.2 = (bf16[3584,128]{1,0:T(8,128)(2,1)}, bf16[3584,128]{1,0:T(8,128)(2,1)S(1)}, u32[]{:S(2)}, u32[]{:S(2)}) collective-permute-start(bf16[3584,128]{1,0:T(8,128)(2,1)} %bitcast.35), channel_id=1, source_target_pairs={{0,2},{1,3},{2,0},{3,1},{4,6},{5,7},{6,4},{7,5},{8,10},{9,11},{10,... | collective-permute-start | bytes 2752520 | tf_op jit(solution)/shard_map/ppermute | solution.py:22
  8.2 40.2 %collective-permute-start.6 = (bf16[3584,128]{1,0:T(8,128)(2,1)}, bf16[3584,128]{1,0:T(8,128)(2,1)S(1)}, u32[]{:S(2)}, u32[]{:S(2)}) collective-permute-start(bf16[3584,128]{1,0:T(8,128)(2,1)} %bitcast.30), channel_id=1, source_target_pairs={{0,2},{1,3},{2,0},{3,1},{4,6},{5,7},{6,4},{7,5},{8,10},{9,11},{10,... | collective-permute-start | bytes 2752520 | tf_op jit(solution)/shard_map/ppermute | solution.py:22
  9.1 25.1 %collective-permute-start.1 = (bf16[80,3584]{1,0:T(8,128)(2,1)S(1)}, bf16[80,3584]{1,0:T(8,128)(2,1)S(1)}, u32[]{:S(2)}, u32[]{:S(2)}) collective-permute-start(bf16[80,3584]{1,0:T(8,128)(2,1)S(1)} %get-tuple-element.84), channel_id=1, source_target_pairs={{0,4},{1,5},{2,6},{3,7},{4,0},{5,1},{6,2},{7,3},{8,12},{9,13},{10,... | collective-permute-start | bytes 1720328 | tf_op jit(solution)/shard_map/ppermute | solution.py:22
  11.5 36.9 %copy-start.6 = (bf16[1,128,3584]{2,1,0:T(8,128)(2,1)S(1)}, bf16[1,128,3584]{2,1,0:T(8,128)(2,1)}, u32[]{:S(2)}) copy-start(bf16[1,128,3584]{2,1,0:T(8,128)(2,1)} %param.13) | copy-start | bytes 2752516
  34.2 30.2 %collective-permute-start.3 = (bf16[160,3584]{1,0:T(8,128)(2,1)S(1)}, bf16[160,3584]{1,0:T(8,128)(2,1)S(1)}, u32[]{:S(2)}, u32[]{:S(2)}) collective-permute-start(bf16[160,3584]{1,0:T(8,128)(2,1)S(1)} %pad_maximum_fusion.5), channel_id=1, source_target_pairs={{0,1},{1,0},{2,3},{3,2},{4,5},{5,4},{6,7},{7,6},{8,9},{9,8},{10,11... | collective-permute-start | bytes 3440648 | tf_op jit(solution)/shard_map/ppermute | solution.py:22
  34.3 30.2 %collective-permute-start.8 = (bf16[80,3584]{1,0:T(8,128)(2,1)S(1)}, bf16[80,3584]{1,0:T(8,128)(2,1)S(1)}, u32[]{:S(2)}, u32[]{:S(2)}) collective-permute-start(bf16[80,3584]{1,0:T(8,128)(2,1)S(1)} %convolution_convert_fusion.2), channel_id=1, source_target_pairs={{0,8},{1,9},{2,10},{3,11},{4,12},{5,13},{6,14},{7,15},{8,0},{9,1},... | collective-permute-start | bytes 1720328 | tf_op jit(solution)/shard_map/ppermute | solution.py:22
  34.9 28.1 %collective-permute-start.4 = (bf16[80,3584]{1,0:T(8,128)(2,1)S(1)}, bf16[80,3584]{1,0:T(8,128)(2,1)S(1)}, u32[]{:S(2)}, u32[]{:S(2)}) collective-permute-start(bf16[80,3584]{1,0:T(8,128)(2,1)S(1)} %collective-permute-done), channel_id=1, source_target_pairs={{0,4},{1,5},{2,6},{3,7},{4,0},{5,1},{6,2},{7,3},{8,12},{9,13},{10,... | collective-permute-start | bytes 1720328 | tf_op jit(solution)/shard_map/ppermute | solution.py:22
  48.4 23.3 %collective-permute-start.7 = (bf16[128,3584]{1,0:T(8,128)(2,1)S(1)}, bf16[128,3584]{1,0:T(8,128)(2,1)S(1)}, u32[]{:S(2)}, u32[]{:S(2)}) collective-permute-start(bf16[128,3584]{1,0:T(8,128)(2,1)S(1)} %bitcast.40), channel_id=1, source_target_pairs={{0,2},{1,3},{2,0},{3,1},{4,6},{5,7},{6,4},{7,5},{8,10},{9,11},{10,... | collective-permute-start | bytes 2752520 | tf_op jit(solution)/shard_map/ppermute | solution.py:22
  63.0 16.9 %collective-permute-start.10 = (bf16[160,1536]{1,0:T(8,128)(2,1)S(1)}, bf16[160,1536]{1,0:T(8,128)(2,1)S(1)}, u32[]{:S(2)}, u32[]{:S(2)}) collective-permute-start(bf16[160,1536]{1,0:T(8,128)(2,1)S(1)} %fusion.38), channel_id=1, source_target_pairs={{0,2},{1,3},{2,0},{3,1},{4,6},{5,7},{6,4},{7,5},{8,10},{9,11},{10,... | collective-permute-start | bytes 1474568 | tf_op jit(solution)/shard_map/ppermute | solution.py:22
  64.5 15.4 %collective-permute-start.9 = (bf16[80,3584]{1,0:T(8,128)(2,1)S(1)}, bf16[80,3584]{1,0:T(8,128)(2,1)S(1)}, u32[]{:S(2)}, u32[]{:S(2)}) collective-permute-start(bf16[80,3584]{1,0:T(8,128)(2,1)S(1)} %collective-permute-done.8), channel_id=1, source_target_pairs={{0,4},{1,5},{2,6},{3,7},{4,0},{5,1},{6,2},{7,3},{8,12},{9,13},{10,... | collective-permute-start | bytes 1720328 | tf_op jit(solution)/shard_map/ppermute | solution.py:22
  64.7 18.4 %copy-start.3 = (bf16[1,3584,128]{2,1,0:T(8,128)(2,1)S(1)}, bf16[1,3584,128]{2,1,0:T(8,128)(2,1)}, u32[]{:S(2)}) copy-start(bf16[1,3584,128]{2,1,0:T(8,128)(2,1)} %param.11) | copy-start | bytes 2752516
  64.8 20.1 %collective-permute-start.5 = (bf16[160,3584]{1,0:T(8,128)(2,1)S(1)}, bf16[160,3584]{1,0:T(8,128)(2,1)S(1)}, u32[]{:S(2)}, u32[]{:S(2)}) collective-permute-start(bf16[160,3584]{1,0:T(8,128)(2,1)S(1)} %get-tuple-element.79), channel_id=1, source_target_pairs={{0,1},{1,0},{2,3},{3,2},{4,5},{5,4},{6,7},{7,6},{8,9},{9,8},{10,11... | collective-permute-start | bytes 3440648 | tf_op jit(solution)/shard_map/ppermute | solution.py:22
  79.9 10.9 %collective-permute-start.13 = (bf16[160,1536]{1,0:T(8,128)(2,1)S(1)}, bf16[160,1536]{1,0:T(8,128)(2,1)S(1)}, u32[]{:S(2)}, u32[]{:S(2)}) collective-permute-start(bf16[160,1536]{1,0:T(8,128)(2,1)S(1)} %slice.135), channel_id=1, source_target_pairs={{0,2},{1,3},{2,0},{3,1},{4,6},{5,7},{6,4},{7,5},{8,10},{9,11},{10,... | collective-permute-start | bytes 1474568 | tf_op jit(solution)/shard_map/ppermute | solution.py:22
  81.4 12.3 %collective-permute-start.12 = (bf16[80,3584]{1,0:T(8,128)(2,1)S(1)}, bf16[80,3584]{1,0:T(8,128)(2,1)S(1)}, u32[]{:S(2)}, u32[]{:S(2)}) collective-permute-start(bf16[80,3584]{1,0:T(8,128)(2,1)S(1)} %convolution_convert_fusion.3), channel_id=1, source_target_pairs={{0,4},{1,5},{2,6},{3,7},{4,0},{5,1},{6,2},{7,3},{8,12},{9,13},{10,... | collective-permute-start | bytes 1720328 | tf_op jit(solution)/shard_map/ppermute | solution.py:22
  83.0 1.2 copy-start.2
  83.0 2.9 %collective-permute-start.11 = (bf16[160,3584]{1,0:T(8,128)(2,1)S(1)}, bf16[160,3584]{1,0:T(8,128)(2,1)S(1)}, u32[]{:S(2)}, u32[]{:S(2)}) collective-permute-start(bf16[160,3584]{1,0:T(8,128)(2,1)S(1)} %pad_maximum_fusion.9), channel_id=1, source_target_pairs={{0,1},{1,0},{2,3},{3,2},{4,5},{5,4},{6,7},{7,6},{8,9},{9,8},{10,11... | collective-permute-start | bytes 3440648 | tf_op jit(solution)/shard_map/ppermute | solution.py:22
  93.8 2.9 %collective-permute-start.14 = (bf16[160,3584]{1,0:T(8,128)(2,1)S(1)}, bf16[160,3584]{1,0:T(8,128)(2,1)S(1)}, u32[]{:S(2)}, u32[]{:S(2)}) collective-permute-start(bf16[160,3584]{1,0:T(8,128)(2,1)S(1)} %pad_maximum_fusion.10), channel_id=1, source_target_pairs={{0,1},{1,0},{2,3},{3,2},{4,5},{5,4},{6,7},{7,6},{8,9},{9,8},{10,11... | collective-permute-start | bytes 3440648 | tf_op jit(solution)/shard_map/ppermute | solution.py:22
  94.0 7.5 %collective-permute-start.21 = (bf16[160,3712]{1,0:T(8,128)(2,1)S(1)}, bf16[160,3712]{1,0:T(8,128)(2,1)S(1)}, u32[]{:S(2)}, u32[]{:S(2)}) collective-permute-start(bf16[160,3712]{1,0:T(8,128)(2,1)S(1)} %slice.116), channel_id=1, source_target_pairs={{0,1},{1,0},{2,3},{3,2},{4,5},{5,4},{6,7},{7,6},{8,9},{9,8},{10,11... | collective-permute-start | bytes 3563528 | tf_op jit(solution)/shard_map/ppermute | solution.py:22
  97.7 22.4 %collective-permute-start.18 = (bf16[640,256]{1,0:T(8,128)(2,1)S(1)}, bf16[640,256]{1,0:T(8,128)(2,1)S(1)}, u32[]{:S(2)}, u32[]{:S(2)}) collective-permute-start(bf16[640,256]{1,0:T(8,128)(2,1)S(1)} %pad_maximum_fusion.15), channel_id=1, source_target_pairs={{0,2},{1,3},{2,0},{3,1},{4,6},{5,7},{6,4},{7,5},{8,10},{9,11},{10,... | collective-permute-start | bytes 983048 | tf_op jit(solution)/shard_map/ppermute | solution.py:22
  100.5 19.0 %collective-permute-start.17 = (bf16[320,1536]{1,0:T(8,128)(2,1)S(1)}, bf16[320,1536]{1,0:T(8,128)(2,1)S(1)}, u32[]{:S(2)}, u32[]{:S(2)}) collective-permute-start(bf16[320,1536]{1,0:T(8,128)(2,1)S(1)} %pad_maximum_fusion.11), channel_id=1, source_target_pairs={{0,1},{1,0},{2,3},{3,2},{4,5},{5,4},{6,7},{7,6},{8,9},{9,8},{10,11... | collective-permute-start | bytes 2949128 | tf_op jit(solution)/shard_map/ppermute | solution.py:22
  101.8 16.1 %collective-permute-start.22 = (bf16[80,3712]{1,0:T(8,128)(2,1)S(1)}, bf16[80,3712]{1,0:T(8,128)(2,1)S(1)}, u32[]{:S(2)}, u32[]{:S(2)}) collective-permute-start(bf16[80,3712]{1,0:T(8,128)(2,1)S(1)} %slice.150), channel_id=1, source_target_pairs={{0,4},{1,5},{2,6},{3,7},{4,0},{5,1},{6,2},{7,3},{8,12},{9,13},{10,... | collective-permute-start | bytes 1781768 | tf_op jit(solution)/shard_map/ppermute | solution.py:22
  104.7 16.4 %collective-permute-start.19 = (bf16[160,3712]{1,0:T(8,128)(2,1)S(1)}, bf16[160,3712]{1,0:T(8,128)(2,1)S(1)}, u32[]{:S(2)}, u32[]{:S(2)}) collective-permute-start(bf16[160,3712]{1,0:T(8,128)(2,1)S(1)} %pad_maximum_fusion.6), channel_id=1, source_target_pairs={{0,1},{1,0},{2,3},{3,2},{4,5},{5,4},{6,7},{7,6},{8,9},{9,8},{10,11... | collective-permute-start | bytes 3563528 | tf_op jit(solution)/shard_map/ppermute | solution.py:22
  104.9 23.2 %collective-permute-start.16 = (bf16[128,3584]{1,0:T(8,128)(2,1)S(1)}, bf16[128,3584]{1,0:T(8,128)(2,1)S(1)}, u32[]{:S(2)}, u32[]{:S(2)}) collective-permute-start(bf16[128,3584]{1,0:T(8,128)(2,1)S(1)} %convolution_convert_fusion.1), channel_id=1, source_target_pairs={{0,2},{1,3},{2,0},{3,1},{4,6},{5,7},{6,4},{7,5},{8,10},{9,11},{10,... | collective-permute-start | bytes 2752520 | tf_op jit(solution)/shard_map/ppermute | solution.py:22
  117.8 32.2 %collective-permute-start.15 = (bf16[2048,256]{1,0:T(8,128)(2,1)S(1)}, bf16[2048,256]{1,0:T(8,128)(2,1)S(1)}, u32[]{:S(2)}, u32[]{:S(2)}) collective-permute-start(bf16[2048,256]{1,0:T(8,128)(2,1)S(1)} %convolution_convert_fusion.6), channel_id=1, source_target_pairs={{0,2},{1,3},{2,0},{3,1},{4,6},{5,7},{6,4},{7,5},{8,10},{9,11},{10,... | collective-permute-start | bytes 3145736 | tf_op jit(solution)/shard_map/ppermute | solution.py:22
  119.5 28.4 %collective-permute-start.23 = (bf16[80,3712]{1,0:T(8,128)(2,1)S(1)}, bf16[80,3712]{1,0:T(8,128)(2,1)S(1)}, u32[]{:S(2)}, u32[]{:S(2)}) collective-permute-start(bf16[80,3712]{1,0:T(8,128)(2,1)S(1)} %add_convert_fusion.2), channel_id=1, source_target_pairs={{0,8},{1,9},{2,10},{3,11},{4,12},{5,13},{6,14},{7,15},{8,0},{9,1},... | collective-permute-start | bytes 1781768 | tf_op jit(solution)/shard_map/ppermute | solution.py:22
  121.5 23.5 %collective-permute-start.20 = (bf16[80,3712]{1,0:T(8,128)(2,1)S(1)}, bf16[80,3712]{1,0:T(8,128)(2,1)S(1)}, u32[]{:S(2)}, u32[]{:S(2)}) collective-permute-start(bf16[80,3712]{1,0:T(8,128)(2,1)S(1)} %slice.148), channel_id=1, source_target_pairs={{0,4},{1,5},{2,6},{3,7},{4,0},{5,1},{6,2},{7,3},{8,12},{9,13},{10,... | collective-permute-start | bytes 1781768 | tf_op jit(solution)/shard_map/ppermute | solution.py:22
  151.1 2.1 %copy-start.1 = (bf16[128,3584]{1,0:T(8,128)(2,1)S(1)}, bf16[128,3584]{1,0:T(8,128)(2,1)}, u32[]{:S(2)}) copy-start(bf16[128,3584]{1,0:T(8,128)(2,1)} %param.7) | copy-start | bytes 2752516
